TPU v7x, 32 devices: a whole 2x2x4 slice. The times are simulated.
32 devices in a mesh: dp: 4 (over y, core), band: 8 (over z, x).
Axes of the slice: x: 2, y: 2, z: 4, core: 2. Of those that a mesh axis runs over, the one named last changes fastest.
Arguments:
- tokens: bfloat16 [8, 1024, 1152], P('dp', 'band'), may hold values from -6 to 6
- cotangent: bfloat16 [8, 1024, 1152], P('dp', 'band'), may hold values from -6 to 6
- lengths: int32 [8, 4], P('dp'), may hold values from 0 to 1024, as said below
- cond_index: int32 [8, 4], P('dp'), may hold values from 0 to 999
- cond_table: bfloat16 [1000, 1152], replicated, may hold values from -6 to 6
- w_mod: bfloat16 [1152, 6912], P(None, 'dp'), may hold values from -0.1875 to 0.1875
- b_mod: float32 [6912], replicated, may hold values from -3 to 3
- w_qkv: bfloat16 [1152, 3456], P(None, 'dp'), may hold values from -0.1875 to 0.1875
- b_query: float32 [1152], replicated, may hold values from -2 to 2
- b_value: float32 [1152], replicated, may hold values from -2 to 2
- w_out: bfloat16 [1152, 1152], P(None, 'dp'), may hold values from -1.5 to 1.5
- b_out: float32 [1152], replicated, may hold values from -2 to 2
- w_up: bfloat16 [1152, 4608], P(None, 'dp'), may hold values from -0.1875 to 0.1875
- b_up: float32 [4608], replicated, may hold values from -2 to 2
- w_down: bfloat16 [4608, 1152], P(None, 'dp'), may hold values from -0.09375 to 0.09375
- b_down: float32 [1152], replicated, may hold values from -2 to 2
Outputs:
- output: bfloat16 [8, 1024, 1152], P('dp', 'band')
- grad_tokens: bfloat16 [8, 1024, 1152], P('dp', 'band')
- grad_cond_table: float32 [1000, 1152], replicated
- grad_w_mod: float32 [1152, 6912], P('dp', 'band')
- grad_w_qkv: float32 [1152, 3456], P('dp', 'band')
- grad_w_out: float32 [1152, 1152], P('dp', 'band')
- grad_w_up: float32 [1152, 4608], P('dp', 'band')
- grad_w_down: float32 [4608, 1152], P('band', 'dp')
- grad_b_mod: float32 [6912], replicated
- grad_b_query: float32 [1152], replicated
- grad_b_value: float32 [1152], replicated
- grad_b_out: float32 [1152], replicated
- grad_b_up: float32 [4608], replicated
- grad_b_down: float32 [1152], replicated
Inputs may be any that keep to these rules, and one draw needn't show every extreme that they name: In each row the nonzero lengths come first and add up to 1024; each is 256, 1024 or 1024. In every aligned block of 2 rows one row, drawn from the seed, is a single image of 1024 patches; the other rows hold images of 256 and 1024 patches only.
All inputs are finite; a program needn't handle non-finite values.
Results may differ from a plain program's by a relative error of at most 0.023.
Values may be sent and summed in bfloat16 or wider, within the bound.
No kernel may reach another device: no remote copies, remote signals or barrier semaphores. Data moves between devices by JAX's collectives and lax.ppermute only.
A program may use at most 384 MiB of HBM per device.

v0:
```python
import math

import jax
import jax.numpy as jnp
from jax import lax
from jax.sharding import PartitionSpec as P

H = 16
HD = 72


EPSILON = 1e-06
HIGHEST = lax.Precision.HIGHEST
NEGATIVE = -1e30
GELU_COEF = 0.7978845608028654


def gelu_tanh(inputs):
    return (
        0.5 * inputs * (1.0 + jnp.tanh(GELU_COEF * (inputs + 0.044715 * inputs * inputs * inputs)))
    )


def layer_norm(inputs):
    average = jnp.mean(inputs, axis=-1, keepdims=True)
    centred = inputs - average
    spread = jnp.mean(centred * centred, axis=-1, keepdims=True)
    return centred * lax.rsqrt(spread + EPSILON)


def segment_of(image_ends, offset, span_len):
    places = offset + jnp.arange(span_len, dtype=jnp.int32)
    return jnp.sum((image_ends[:, None, :] <= places[None, :, None]).astype(jnp.int32), axis=-1)


def masked_scores(queries, keys_row, seg_query, seg_key):
    factor = 1.0 / math.sqrt(HD)
    scores = (
        jnp.einsum("qhd,khd->hqk", queries, keys_row, preferred_element_type=jnp.float32) * factor
    )
    allowed = seg_query[:, None] == seg_key[None, :]
    return jnp.where(allowed[None], scores, NEGATIVE)


def attend_row(inputs):
    queries, keys_row, values_row, seg_query, seg_key = inputs
    scores = masked_scores(queries, keys_row, seg_query, seg_key)
    row_top = jnp.max(scores, axis=-1, keepdims=True)
    exponent = jnp.exp(scores - row_top)
    row_total = jnp.sum(exponent, axis=-1, keepdims=True)
    attn_probs = (exponent / row_total).astype(jnp.bfloat16)
    attended = jnp.einsum(
        "hqk,khd->qhd", attn_probs, values_row, preferred_element_type=jnp.float32
    )
    return (attended, row_top[:, :, 0].T, row_total[:, :, 0].T)


def score_grads(
    queries, keys_row, values_row, grad_out, seg_query, seg_key, row_top, row_total, row_delta
):
    scores = masked_scores(queries, keys_row, seg_query, seg_key)
    attn_probs = jnp.exp(scores - row_top.T[:, :, None]) / row_total.T[:, :, None]
    grad_probs = jnp.einsum(
        "qhd,khd->hqk", grad_out, values_row, preferred_element_type=jnp.float32
    )
    grad_scores = (attn_probs * (grad_probs - row_delta.T[:, :, None])).astype(jnp.bfloat16)
    return (attn_probs.astype(jnp.bfloat16), grad_scores)


def full_back(inputs):
    queries, keys_row, values_row, grad_out, seg_query, seg_key, row_top, row_total, row_delta = (
        inputs
    )
    factor = 1.0 / math.sqrt(HD)
    prob_low, grad_scores = score_grads(
        queries, keys_row, values_row, grad_out, seg_query, seg_key, row_top, row_total, row_delta
    )
    grad_query = (
        jnp.einsum("hqk,khd->qhd", grad_scores, keys_row, preferred_element_type=jnp.float32)
        * factor
    )
    grad_key = (
        jnp.einsum("hqk,qhd->khd", grad_scores, queries, preferred_element_type=jnp.float32)
        * factor
    )
    grad_value = jnp.einsum("hqk,qhd->khd", prob_low, grad_out, preferred_element_type=jnp.float32)
    return (grad_query, grad_key, grad_value)


def pack_columns(matrices, pieces):
    parted = [
        member.reshape(member.shape[0], pieces, member.shape[1] // pieces) for member in matrices
    ]
    joined = jnp.concatenate(parted, axis=2)
    return joined.reshape(joined.shape[0], joined.shape[1] * joined.shape[2])


def unpack_columns(packed, widths, pieces):
    results = []
    start = 0
    for width in widths:
        share = width // pieces
        results.append(packed[:, start : start + share])
        start = start + share
    return results


def shards(
    tokens,
    cotangent,
    lengths,
    cond_index,
    cond_table,
    w_mod,
    b_mod,
    w_qkv,
    b_query,
    b_value,
    w_out,
    b_out,
    w_up,
    b_up,
    w_down,
    b_down,
):
    row_count, band_len, model_width = tokens.shape
    mod_full, qkv_full, out_full, up_full, down_full = (
        lax.all_gather(w_mod, "dp", axis=1, tiled=True),
        lax.all_gather(w_qkv, "dp", axis=1, tiled=True),
        lax.all_gather(w_out, "dp", axis=1, tiled=True),
        lax.all_gather(w_up, "dp", axis=1, tiled=True),
        lax.all_gather(w_down, "dp", axis=1, tiled=True),
    )
    band_count = lax.axis_size("band")
    row_len = band_len * band_count
    band_first_place = lax.axis_index("band") * band_len
    image_ends = jnp.cumsum(lengths, axis=-1)
    seg_local = segment_of(image_ends, band_first_place, band_len)
    seg_whole = segment_of(image_ends, 0, row_len)
    image_picks = (seg_local[..., None] == jnp.arange(lengths.shape[1], dtype=jnp.int32)).astype(
        jnp.float32
    )
    class_hot = (cond_index[..., None] == jnp.arange(cond_table.shape[0], dtype=jnp.int32)).astype(
        jnp.bfloat16
    )
    condition = jnp.einsum("ric,cd->rid", class_hot, cond_table, preferred_element_type=jnp.float32)
    silu_cond = jax.nn.silu(condition).astype(jnp.bfloat16)
    modulation = (
        jnp.einsum("rid,dm->rim", silu_cond, mod_full, preferred_element_type=jnp.float32) + b_mod
    )
    token_mod = jnp.einsum("rti,rim->rtm", image_picks, modulation, precision=HIGHEST)
    shift_a, scale_a, gate_a, shift_b, scale_b, gate_b = jnp.split(token_mod, 6, axis=-1)
    inputs = tokens.astype(jnp.float32)
    norm_a = layer_norm(inputs)
    hidden_a = (norm_a * (1.0 + scale_a) + shift_a).astype(jnp.bfloat16)
    projected = jnp.einsum("rtd,de->rte", hidden_a, qkv_full, preferred_element_type=jnp.float32)
    queries = (projected[..., :model_width] + b_query).astype(jnp.bfloat16)
    keys_local = projected[..., model_width : 2 * model_width].astype(jnp.bfloat16)
    values_local = (projected[..., 2 * model_width :] + b_value).astype(jnp.bfloat16)
    keys_whole, values_whole = (
        lax.all_gather(keys_local, "band", axis=1, tiled=True),
        lax.all_gather(values_local, "band", axis=1, tiled=True),
    )
    query_heads = queries.reshape(row_count, band_len, H, HD)
    key_heads = keys_whole.reshape(row_count, row_len, H, HD)
    value_heads = values_whole.reshape(row_count, row_len, H, HD)
    attended, row_top, row_total = lax.map(
        attend_row, (query_heads, key_heads, value_heads, seg_local, seg_whole)
    )
    attended_flat = attended.reshape(row_count, band_len, model_width)
    attended_low = attended_flat.astype(jnp.bfloat16)
    branch = (
        jnp.einsum("rtd,de->rte", attended_low, out_full, preferred_element_type=jnp.float32)
        + b_out
    )
    middle = inputs + gate_a * branch
    norm_b = layer_norm(middle)
    hidden_b = (norm_b * (1.0 + scale_b) + shift_b).astype(jnp.bfloat16)
    pre_act = (
        jnp.einsum("rtd,df->rtf", hidden_b, up_full, preferred_element_type=jnp.float32) + b_up
    )
    activated = gelu_tanh(pre_act).astype(jnp.bfloat16)
    mlp_out = (
        jnp.einsum("rtf,fd->rtd", activated, down_full, preferred_element_type=jnp.float32) + b_down
    )
    output = (middle + gate_b * mlp_out).astype(jnp.bfloat16)
    grad_output = cotangent.astype(jnp.float32)
    grad_mlp = (gate_b * grad_output).astype(jnp.bfloat16)
    grad_gate_b = grad_output * mlp_out
    grad_w_down = jnp.einsum("rtf,rtd->fd", activated, grad_mlp, preferred_element_type=jnp.float32)
    grad_b_down = jnp.sum(grad_mlp.astype(jnp.float32), axis=(0, 1))
    grad_act = jnp.einsum(
        "rtd,fd->rtf", grad_mlp, down_full, preferred_element_type=jnp.float32
    ).astype(jnp.bfloat16)
    gelu_unused, gelu_pull = jax.vjp(gelu_tanh, pre_act)
    grad_pre = gelu_pull(grad_act.astype(jnp.float32))[0].astype(jnp.bfloat16)
    grad_w_up = jnp.einsum("rtd,rtf->df", hidden_b, grad_pre, preferred_element_type=jnp.float32)
    grad_b_up = jnp.sum(grad_pre.astype(jnp.float32), axis=(0, 1))
    grad_hidden_b = jnp.einsum("rtf,df->rtd", grad_pre, up_full, preferred_element_type=jnp.float32)
    norm_unused_b, norm_pull_b = jax.vjp(layer_norm, middle)
    grad_middle = grad_output + norm_pull_b(grad_hidden_b * (1.0 + scale_b))[0]
    grad_scale_b = grad_hidden_b * norm_b
    grad_branch = (gate_a * grad_middle).astype(jnp.bfloat16)
    grad_gate_a = grad_middle * branch
    grad_w_out = jnp.einsum(
        "rtd,rte->de", attended_low, grad_branch, preferred_element_type=jnp.float32
    )
    grad_b_out = jnp.sum(grad_branch.astype(jnp.float32), axis=(0, 1))
    grad_attended = jnp.einsum(
        "rte,de->rtd", grad_branch, out_full, preferred_element_type=jnp.float32
    ).astype(jnp.bfloat16)
    row_delta = jnp.sum(
        (grad_attended.astype(jnp.float32) * attended_flat).reshape(row_count, band_len, H, HD),
        axis=-1,
    )
    grad_heads = grad_attended.reshape(row_count, band_len, H, HD)
    grad_query, grad_key_row, grad_value_row = lax.map(
        full_back,
        (
            query_heads,
            key_heads,
            value_heads,
            grad_heads,
            seg_local,
            seg_whole,
            row_top,
            row_total,
            row_delta,
        ),
    )
    joined_row = jnp.concatenate(
        [
            grad_key_row.reshape(row_count, row_len, model_width),
            grad_value_row.reshape(row_count, row_len, model_width),
        ],
        axis=-1,
    )
    summed = lax.psum_scatter(
        joined_row.astype(jnp.bfloat16), "band", scatter_dimension=1, tiled=True
    ).astype(jnp.float32)
    grad_key = summed[..., :model_width]
    grad_value = summed[..., model_width:]
    grad_q_low = grad_query.reshape(row_count, band_len, model_width).astype(jnp.bfloat16)
    grad_k_low = grad_key.astype(jnp.bfloat16)
    grad_v_low = grad_value.astype(jnp.bfloat16)
    grad_projected = jnp.concatenate([grad_q_low, grad_k_low, grad_v_low], axis=-1)
    grad_w_qkv = jnp.einsum(
        "rtd,rte->de", hidden_a, grad_projected, preferred_element_type=jnp.float32
    )
    grad_b_query = jnp.sum(grad_q_low.astype(jnp.float32), axis=(0, 1))
    grad_b_value = jnp.sum(grad_v_low.astype(jnp.float32), axis=(0, 1))
    grad_hidden_a = jnp.einsum(
        "rte,de->rtd", grad_projected, qkv_full, preferred_element_type=jnp.float32
    )
    norm_unused_a, norm_pull_a = jax.vjp(layer_norm, inputs)
    grad_tokens = (grad_middle + norm_pull_a(grad_hidden_a * (1.0 + scale_a))[0]).astype(
        jnp.bfloat16
    )
    grad_scale_a = grad_hidden_a * norm_a
    grad_token_mod = jnp.concatenate(
        [grad_hidden_a, grad_scale_a, grad_gate_a, grad_hidden_b, grad_scale_b, grad_gate_b],
        axis=-1,
    )
    grad_modulation = jnp.einsum("rti,rtm->rim", image_picks, grad_token_mod, precision=HIGHEST)
    grad_w_mod = jnp.einsum(
        "rid,rim->dm", silu_cond.astype(jnp.float32), grad_modulation, precision=HIGHEST
    )
    grad_b_mod = jnp.sum(grad_modulation, axis=(0, 1))
    grad_silu = jnp.einsum(
        "rim,dm->rid", grad_modulation, mod_full.astype(jnp.float32), precision=HIGHEST
    )
    silu_unused, silu_pull = jax.vjp(jax.nn.silu, condition)
    grad_condition = silu_pull(grad_silu)[0]
    grad_table = jnp.einsum(
        "ric,rid->cd", class_hot.astype(jnp.float32), grad_condition, precision=HIGHEST
    )
    wide_list = [grad_w_mod, grad_w_qkv, grad_w_out, grad_w_up, grad_w_down.T]
    widths = [member.shape[1] for member in wide_list]
    packed_grads = pack_columns(wide_list, band_count)
    first_sum = lax.psum_scatter(
        packed_grads.astype(jnp.bfloat16), "band", scatter_dimension=1, tiled=True
    )
    final_sum = lax.psum_scatter(first_sum, "dp", scatter_dimension=0, tiled=True).astype(
        jnp.float32
    )
    final_mod, final_qkv, final_out, final_up, final_down_t = unpack_columns(
        final_sum, widths, band_count
    )
    final_down = final_down_t.T
    small_grads = lax.psum(
        (grad_b_mod, grad_b_query, grad_b_value, grad_b_out, grad_b_up, grad_b_down, grad_table),
        ("dp", "band"),
    )
    return (
        output,
        grad_tokens,
        small_grads[6],
        final_mod,
        final_qkv,
        final_out,
        final_up,
        final_down,
        small_grads[0],
        small_grads[1],
        small_grads[2],
        small_grads[3],
        small_grads[4],
        small_grads[5],
    )


def solution(mesh):
    placed = (
        P("dp", "band", None),
        P("dp", "band", None),
        P("dp", None),
        P("dp", None),
        P(),
        P(None, "dp"),
        P(),
        P(None, "dp"),
        P(),
        P(),
        P(None, "dp"),
        P(),
        P(None, "dp"),
        P(),
        P(None, "dp"),
        P(),
    )
    return jax.shard_map(
        shards,
        mesh=mesh,
        in_specs=placed,
        out_specs=(
            P("dp", "band", None),
            P("dp", "band", None),
            P(),
            P("dp", "band"),
            P("dp", "band"),
            P("dp", "band"),
            P("dp", "band"),
            P("band", "dp"),
            P(),
            P(),
            P(),
            P(),
            P(),
            P(),
        ),
        check_vma=False,
    )
```

profile of v0, /device:TPU:4, one launch (start us, length us, event | category | flops | bytes accessed | tf_op | source)
XLA Modules:
  0.0 1854.1 jit_solution(13860237718100078601)
XLA Ops:
  10.6 100.2 %all-gather.8.cloned.1.call-done = bf16[1152,6912]{0,1:T(8,128)(2,1)} async-done(((bf16[1152,1728]{0,1:T(8,128)(2,1)}), bf16[1152,6912]{0,1:T(8,128)(2,1)}) %all-gather.8.cloned.1.call-update) | async-done | bytes 15925264 | tf_op jit(solution)/shard_map/all_gather | solution.py:128
  110.8 9.8 fusion.74
  127.6 40.6 %all-gather.10.cloned.1.call-done = bf16[1152,3456]{0,1:T(8,128)(2,1)} async-done(((bf16[1152,864]{0,1:T(8,128)(2,1)}), bf16[1152,3456]{0,1:T(8,128)(2,1)}) %all-gather.10.cloned.1.call-update) | async-done | bytes 7962640 | tf_op jit(solution)/shard_map/all_gather | solution.py:129
  181.9 75.4 %all-gather.12.cloned.1.call-done = bf16[2,1024,1152]{2,1,0:T(8,128)(2,1)} async-done(((bf16[2,128,1152]{2,1,0:T(8,128)(2,1)}), bf16[2,1024,1152]{2,1,0:T(8,128)(2,1)}) %all-gather.12.cloned.1.call-update) | async-done | bytes 4718608 | tf_op jit(solution)/shard_map/all_gather | solution.py:162
  257.3 6.7 copy.96
  264.0 74.0 %all-gather.14.cloned.1.call-done = bf16[2,1024,1152]{2,1,0:T(8,128)(2,1)} async-done(((bf16[2,128,1152]{2,1,0:T(8,128)(2,1)}), bf16[2,1024,1152]{2,1,0:T(8,128)(2,1)}) %all-gather.14.cloned.1.call-update) | async-done | bytes 4718608 | tf_op jit(solution)/shard_map/all_gather | solution.py:161
  344.6 17.3 while.30
  372.1 62.4 %all-gather.18.cloned.1.call-done = bf16[1152,4608]{1,0:T(8,128)(2,1)} async-done(((bf16[1152,1152]{1,0:T(8,128)(2,1)}), bf16[1152,4608]{1,0:T(8,128)(2,1)}) %all-gather.18.cloned.1.call-update) | async-done | bytes 10616848 | tf_op jit(solution)/shard_map/all_gather | solution.py:131
  434.5 9.1 fusion.77
  443.6 63.5 %all-gather.20.cloned.1.call-done = bf16[4608,1152]{0,1:T(8,128)(2,1)} async-done(((bf16[4608,288]{0,1:T(8,128)(2,1)}), bf16[4608,1152]{0,1:T(8,128)(2,1)}) %all-gather.20.cloned.1.call-update) | async-done | bytes 10616848 | tf_op jit(solution)/shard_map/all_gather | solution.py:132
  507.1 10.3 convert_reduce_fusion
  517.4 8.5 multiply_reduce_fusion
  526.0 11.2 fusion.144
  546.4 31.2 %while.31 = (s32[]{:T(128)}, bf16[2,128,16,72]{1,3,2,0:T(8,128)(2,1)S(1)}, bf16[2,1024,16,72]{1,3,2,0:T(8,128)(2,1)}, bf16[2,1024,16,72]{1,3,2,0:T(8,128)(2,1)},...) while((s32[]{:T(128)}, ...), condition=%wide.region_15.16_spmd.clone, body=%wide.region_14.15_spmd.sunk.clone | while | flops 1528184832 | bytes 164916048 | solution.py:217
  577.6 6.9 copy.104
  591.1 9.0 pad_maximum_fusion
  603.6 8.8 fusion.55
  612.4 15.5 copy.113
  627.9 9.4 fusion.56
  637.3 15.4 copy.115
  652.7 112.1 %reduce-scatter.6.cloned.1.call-done = bf16[2,128,2304]{2,1,0:T(8,128)(2,1)} async-done(((bf16[2,1024,2304]{2,1,0:T(8,128)(2,1)}), bf16[2,128,2304]{2,1,0:T(8,128)(2,1)}) %reduce-scatter.6.cloned.1.call-update) | async-done | bytes 1179664 | tf_op jit(solution)/shard_map/reduce_scatter | solution.py:238
  780.5 15.8 bitcast_convert_fusion
  796.3 21.6 %copy.106 = bf16[1152,6912]{0,1:T(8,128)(2,1)} copy(bf16[1152,6912]{1,0:T(8,128)(2,1)} %bitcast_convert_fusion) | data formatting | bytes 31850496 | tf_op jit(solution)/shard_map/convert.8
  817.8 13.6 constant_dynamic-update-slice_fusion.5
  836.9 11.5 copy.108
  848.4 7.2 constant_dynamic-update-slice_fusion.4
  858.1 10.3 constant_dynamic-update-slice_fusion.3
  873.3 750.6 %reduce-scatter.8.cloned.1.call-done = bf16[1152,2592]{0,1:T(8,128)(2,1)} async-done(((bf16[1152,20736]{0,1:T(8,128)(2,1)}), bf16[1152,2592]{0,1:T(8,128)(2,1)}) %reduce-scatter.8.cloned.1.call-update) | async-done | bytes 5971984 | tf_op jit(solution)/shard_map/reduce_scatter | solution.py:280
  1623.9 9.1 copy.127
  1633.2 10.3 fusion.57
  1648.6 43.0 %all-reduce = (f32[6912]{0:T(1024)}, f32[1152]{0:T(1024)}, f32[1152]{0:T(1024)}, f32[1152]{0:T(1024)}, f32[4608]{0:T(1024)}, /*index=5*/f32[1152]{0:T(1024)}) all-reduce(f32[6912]{0:T(1024)S(1)} %get-tuple-element.295, f32[1152]{0:T(1024)S(1)} %reduce_sum.209, ...), channel_id=1, replica_groups=mesh['dp'=4,'band'=8] {'dp','band'}, use_global_device_ids=true, to_apply=%region_23.24 | all-reduce | flops 16128 | bytes 129024 | tf_op jit(solution)/shard_map/psum | solution.py:290
  1708.7 133.5 %all-reduce.3.cloned.1.call-done = f32[1000,1152]{1,0:T(8,128)} async-done(((f32[1000,1152]{1,0:T(8,128)}), f32[1000,1152]{1,0:T(8,128)}) %all-reduce.3.cloned.1.call-update) | async-done | bytes 4608016 | tf_op jit(solution)/shard_map/psum | solution.py:290
  (287 shorter events, 162.9 us)
Async XLA Ops:
  7.2 103.6 %copy-start.44 = (f32[6912]{0:T(1024)S(1)}, f32[6912]{0:T(1024)}, u32[]{:S(2)}) copy-start(f32[6912]{0:T(1024)} %param.26) | copy-start | bytes 82948
  7.2 103.6 %all-gather.8.cloned.1.call-start = ((), (), s32[]{:S(2)}) async-start(), calls=%async_computation.3 | async-start | bytes 19906560 | tf_op jit(solution)/shard_map/all_gather | solution.py:128
  8.0 160.3 %all-gather.10.cloned.1.call-start = ((), (), s32[]{:S(2)}) async-start(), calls=%async_computation.4 | async-start | bytes 9953280 | tf_op jit(solution)/shard_map/all_gather | solution.py:129
  8.7 248.6 %all-gather.12.cloned.1.call-start = ((), (), s32[]{:S(2)}) async-start(), calls=%async_computation.5 | async-start | bytes 5308416 | tf_op jit(solution)/shard_map/all_gather | solution.py:162
  9.2 114.4 %copy-start.45 = (f32[2,128]{1,0:T(2,128)}, f32[2,128]{1,0:T(2,128)S(1)}, u32[]{:S(2)}) copy-start(f32[2,128]{1,0:T(2,128)S(1)} %broadcast_multiply_fusion.1) | copy-start | bytes 3076
  10.1 113.6 %copy-start.48 = (f32[2,128]{1,0:T(2,128)}, f32[2,128]{1,0:T(2,128)S(1)}, u32[]{:S(2)}) copy-start(f32[2,128]{1,0:T(2,128)S(1)} %fusion.138) | copy-start | bytes 3076
  10.6 110.0 %copy-start.37 = (f32[2,4,1152]{2,1,0:T(4,128)}, f32[2,4,1152]{2,1,0:T(4,128)S(1)}, u32[]{:S(2)}) copy-start(f32[2,4,1152]{2,1,0:T(4,128)S(1)} %fusion.104) | copy-start | bytes 110596
  127.6 46.5 %copy-start.30 = (bf16[2,128,1152]{2,1,0:T(8,128)(2,1)}, bf16[2,128,1152]{2,1,0:T(8,128)(2,1)S(1)}, u32[]{:S(2)}) copy-start(bf16[2,128,1152]{2,1,0:T(8,128)(2,1)S(1)} %fusion.113) | copy-start | bytes 1769476
  127.6 46.5 %copy-start.58 = (f32[1152]{0:T(1024)S(1)}, f32[1152]{0:T(1024)}, u32[]{:S(2)}) copy-start(f32[1152]{0:T(1024)} %param.28) | copy-start | bytes 13828
  127.6 46.5 %copy-start.59 = (f32[1152]{0:T(1024)S(1)}, f32[1152]{0:T(1024)}, u32[]{:S(2)}) copy-start(f32[1152]{0:T(1024)} %param.29) | copy-start | bytes 13828
  176.1 161.9 %all-gather.14.cloned.1.call-start = ((), (), s32[]{:S(2)}) async-start(), calls=%async_computation.6 | async-start | bytes 5308416 | tf_op jit(solution)/shard_map/all_gather | solution.py:161
  178.4 184.9 %all-gather.16.cloned.1.call-start = ((), (), s32[]{:S(2)}) async-start(), calls=%async_computation.7 | async-start | bytes 3317760 | tf_op jit(solution)/shard_map/all_gather | solution.py:130
  179.0 255.6 %all-gather.18.cloned.1.call-start = ((), (), s32[]{:S(2)}) async-start(), calls=%async_computation.8 | async-start | bytes 13271040 | tf_op jit(solution)/shard_map/all_gather | solution.py:131
  179.5 327.5 %all-gather.20.cloned.1.call-start = ((), (), s32[]{:S(2)}) async-start(), calls=%async_computation.9 | async-start | bytes 13271040 | tf_op jit(solution)/shard_map/all_gather | solution.py:132
  180.3 584.6 %reduce-scatter.6.cloned.1.call-start = ((), (), s32[]{:S(2)}) async-start(), calls=%async_computation.10 | async-start | bytes 10616832 | tf_op jit(solution)/shard_map/reduce_scatter | solution.py:238
  367.8 158.1 %copy-start.8 = (f32[2,128,1152]{2,1,0:T(8,128)}, f32[2,128,1152]{2,1,0:T(8,128)S(1)}, u32[]{:S(2)}) copy-start(f32[2,128,1152]{2,1,0:T(8,128)S(1)} %get-tuple-element.273) | copy-start | bytes 3538948
  367.9 66.7 %copy-start.64 = (f32[4608]{0:T(1024)S(1)}, f32[4608]{0:T(1024)}, u32[]{:S(2)}) copy-start(f32[4608]{0:T(1024)} %param.33) | copy-start | bytes 55300
  367.9 158.1 %copy-start.50 = (f32[2,128]{1,0:T(2,128)}, f32[2,128]{1,0:T(2,128)S(1)}, u32[]{:S(2)}) copy-start(f32[2,128]{1,0:T(2,128)S(1)} %broadcast_multiply_fusion) | copy-start | bytes 3076
  368.2 157.8 %copy-start.54 = (f32[2,128]{1,0:T(2,128)}, f32[2,128]{1,0:T(2,128)S(1)}, u32[]{:S(2)}) copy-start(f32[2,128]{1,0:T(2,128)S(1)} %fusion.139) | copy-start | bytes 3076
  372.1 71.5 %copy-start.28 = (bf16[2,128,1152]{2,1,0:T(8,128)(2,1)}, bf16[2,128,1152]{2,1,0:T(8,128)(2,1)S(1)}, u32[]{:S(2)}) copy-start(bf16[2,128,1152]{2,1,0:T(8,128)(2,1)S(1)} %get-tuple-element.281) | copy-start | bytes 1769476
  577.6 24.7 %copy-start.18 = (bf16[2,128,16,72]{1,3,2,0:T(8,128)(2,1)}, bf16[2,128,16,72]{1,3,2,0:T(8,128)(2,1)S(1)}, u32[]{:S(2)}) copy-start(bf16[2,128,16,72]{1,3,2,0:T(8,128)(2,1)S(1)} %get-tuple-element.135) | copy-start | bytes 1769476
  600.1 1023.8 %reduce-scatter.8.cloned.1.call-start = ((), (), s32[]{:S(2)}) async-start(), calls=%async_computation.12 | async-start | bytes 53747712 | tf_op jit(solution)/shard_map/reduce_scatter | solution.py:280
  602.5 162.3 %copy-start.33 = (bf16[2,128,1152]{2,1,0:T(8,128)(2,1)}, bf16[2,128,1152]{2,1,0:T(8,128)(2,1)S(1)}, u32[]{:S(2)}) copy-start(bf16[2,128,1152]{2,1,0:T(8,128)(2,1)S(1)} %copy.105) | copy-start | bytes 1769476
  637.3 127.5 %copy-start.7 = (bf16[2,128,1152]{2,1,0:T(8,128)(2,1)S(1)}, bf16[2,128,1152]{2,1,0:T(8,128)(2,1)}, u32[]{:S(2)}) copy-start(bf16[2,128,1152]{2,1,0:T(8,128)(2,1)} %param.20) | copy-start | bytes 1769476
  637.3 127.5 %copy-start.46 = (f32[2,128]{1,0:T(2,128)S(1)}, f32[2,128]{1,0:T(2,128)}, u32[]{:S(2)}) copy-start(f32[2,128]{1,0:T(2,128)} %copy-done.45) | copy-start | bytes 3076
  652.7 118.6 %copy-start.57 = (f32[2,128]{1,0:T(2,128)S(1)}, f32[2,128]{1,0:T(2,128)}, u32[]{:S(2)}) copy-start(f32[2,128]{1,0:T(2,128)} %copy-done.56) | copy-start | bytes 3076
  652.7 118.7 %copy-start.49 = (f32[2,128]{1,0:T(2,128)S(1)}, f32[2,128]{1,0:T(2,128)}, u32[]{:S(2)}) copy-start(f32[2,128]{1,0:T(2,128)} %copy-done.48) | copy-start | bytes 3076
  652.7 120.6 %copy-start.11 = (bf16[2,128,1152]{2,1,0:T(8,128)(2,1)S(1)}, bf16[2,128,1152]{2,1,0:T(8,128)(2,1)}, u32[]{:S(2)}) copy-start(bf16[2,128,1152]{2,1,0:T(8,128)(2,1)} %param.21) | copy-start | bytes 1769476
  652.7 120.6 %copy-start.16 = (f32[2,128,1152]{2,1,0:T(8,128)S(1)}, f32[2,128,1152]{2,1,0:T(8,128)}, u32[]{:S(2)}) copy-start(f32[2,128,1152]{2,1,0:T(8,128)} %copy-done.15) | copy-start | bytes 3538948
  652.7 120.6 %copy-start.53 = (f32[2,128]{1,0:T(2,128)S(1)}, f32[2,128]{1,0:T(2,128)}, u32[]{:S(2)}) copy-start(f32[2,128]{1,0:T(2,128)} %copy-done.52) | copy-start | bytes 3076
  873.3 818.4 %reduce-scatter.10.cloned.1.call-start = ((), (), s32[]{:S(2)}) async-start(), calls=%async_computation.13 | async-start | bytes 7741440
  1633.1 209.1 %all-reduce.3.cloned.1.call-start = ((), (), s32[]{:S(2)}) async-start(), calls=%async_computation.11 | async-start | bytes 9216000 | tf_op jit(solution)/shard_map/psum | solution.py:290
  (58 other events, 309.6 us)
Sparse Core Ops, SparseCore 0:
  9.6 101.1 all-gather.7
  112.4 55.8 all-gather.9
  176.3 81.0 all-gather.11
  260.0 78.0 all-gather.13
  339.4 22.7 all-gather.15
  363.6 70.8 all-gather.17
  436.1 70.9 all-gather.19
  600.2 164.5 reduce-scatter.5
  873.4 750.5 reduce-scatter.7
  1633.2 56.8 reduce-scatter.9
  1697.4 144.7 all-reduce.2
where the time goes:
time: 1870 us; the launch traced here: 1850 us
  waiting for transfers between devices  1420 us (76%)
  local copies, waits for them, and re-layouts  183 us (10%)
  matrix products  161 us (9%)
  blocking collectives  43 us (2%)
  other arithmetic  34.3 us (2%)
    reduce_scatter x1, waiting for transfers between devices, shards(): lax.psum_scatter(packed_grads.astype(jnp.bfloat16), 'band', scatter_dimen...  751 us
    psum x1, waiting for transfers between devices, shards(): lax.psum((grad_b_mod, grad_b_query, grad_b_value, grad_b_out, grad_b_up,...  134 us
    reduce_scatter x1, waiting for transfers between devices, shards(): lax.psum_scatter(joined_row.astype(jnp.bfloat16), 'band', scatter_dimensi...  112 us
    all_gather x1, waiting for transfers between devices, shards(): lax.all_gather(w_mod, 'dp', axis=1, tiled=True)  100 us
    all_gather x1, waiting for transfers between devices, shards(): lax.all_gather(values_local, 'band', axis=1, tiled=True)  75.4 us
    all_gather x1, waiting for transfers between devices, shards(): lax.all_gather(keys_local, 'band', axis=1, tiled=True)  74 us
    another operation x4, local copies, waits for them, and re-layouts  63.9 us
    all_gather x1, waiting for transfers between devices, shards(): lax.all_gather(w_down, 'dp', axis=1, tiled=True)  63.5 us
  transfers between devices with their start and end apart: 11, of which 9 were waited for; matrix products, arithmetic and copies ran while one was open for 8% of the time, Pallas kernels for 0%

commit v1 on v0

v1 whole, which is shorter than its diff:
```python
import functools
import math

import jax
import jax.numpy as jnp
from jax import lax
from jax.experimental import pallas as pl
from jax.experimental.pallas import tpu as pltpu
from jax.sharding import PartitionSpec as P

H = 16
HD = 72

EPSILON = 1e-06
HIGHEST = lax.Precision.HIGHEST
NEGATIVE = -1e30
GELU_COEF = 0.7978845608028654
FACTOR = 1.0 / math.sqrt(HD)
VMEM_LIMIT = 56 * 1024 * 1024
F32 = jnp.float32
BF16 = jnp.bfloat16


def dot(left, right, left_dim=1, right_dim=0):
    return lax.dot_general(
        left, right, (((left_dim,), (right_dim,)), ((), ())), preferred_element_type=F32
    )


def reverse_bits(value, count):
    result = 0
    while count > 1:
        result = result * 2 + value % 2
        value, count = value // 2, count // 2
    return result


def bits_up(count):
    return [1 << place for place in range(count.bit_length() - 1)]


def xor_perm(count, mask):
    return [(place, place ^ mask) for place in range(count)]


def pick(stack, place, axis=0):
    return lax.dynamic_index_in_dim(stack, place, axis, keepdims=False)


def xor_order(count):
    order = [0]
    for bit in reversed(bits_up(count)):
        order = order + [place ^ bit for place in order]
    return order


def gather_xor(part, axis, count):
    held = part[None]
    for bit in reversed(bits_up(count)):
        held = jnp.concatenate([held, lax.ppermute(held, axis, xor_perm(count, bit))], axis=0)
    return held


def gather_all(part, axis, count):
    held = gather_xor(part, axis, count)
    order = xor_order(count)
    me = lax.axis_index(axis)
    place_of = jnp.array([order.index(place) for place in range(count)], jnp.int32)
    return jnp.stack([pick(held, place_of[me ^ place]) for place in range(count)])


def scatter_sum_xor(parts, axis, count):
    held = parts
    for bit in bits_up(count):
        half = held.shape[0] // 2
        came = lax.ppermute(held[half:].astype(BF16), axis, xor_perm(count, bit))
        held = held[:half].astype(F32) + came.astype(F32)
    return held[0]


def exchange_columns(parts, axis, count):
    me = lax.axis_index(axis)
    got = [pick(parts, me)]
    for mask in range(1, count):
        got.append(lax.ppermute(pick(parts, me ^ mask), axis, xor_perm(count, mask)))
    return got


def attend_kernel(heads, piece, segq_ref, q_ref, k_ref, v_ref, segk_ref, out_ref, prob_ref):
    step = pl.program_id(0)
    pieces = q_ref.shape[0] // piece
    parts = []
    seg_key = segk_ref[...]
    for head in range(heads):
        lanes = slice(head * HD, (head + 1) * HD)
        scores = dot(q_ref[:, lanes], k_ref[:, lanes], 1, 1) * FACTOR
        masked = [
            jnp.where(
                seg_key == segq_ref[step * pieces + at],
                scores[at * piece : (at + 1) * piece],
                NEGATIVE,
            )
            for at in range(pieces)
        ]
        scores = jnp.concatenate(masked, axis=0)
        top = jnp.max(scores, axis=-1, keepdims=True)
        exponent = jnp.exp(scores - top)
        total = jnp.sum(exponent, axis=-1, keepdims=True)
        prob = (exponent * (1.0 / total)).astype(BF16)
        prob_ref[head] = prob
        parts.append(dot(prob, v_ref[:, lanes]))
    out_ref[...] = jnp.concatenate(parts, axis=-1).astype(BF16)


def attend(queries, keys, values, seg_query, seg_key, piece):
    count, width = queries.shape
    keys_len = keys.shape[0]
    heads = width // HD
    rows = min(256, count)
    whole = lambda step, seg: (0, 0)
    chunk = lambda step, seg: (step, 0)
    return pl.pallas_call(
        functools.partial(attend_kernel, heads, piece),
        grid_spec=pltpu.PrefetchScalarGridSpec(
            num_scalar_prefetch=1,
            grid=(count // rows,),
            in_specs=[
                pl.BlockSpec((rows, width), chunk),
                pl.BlockSpec((keys_len, width), whole),
                pl.BlockSpec((keys_len, width), whole),
                pl.BlockSpec((1, keys_len), whole),
            ],
            out_specs=[
                pl.BlockSpec((rows, width), chunk),
                pl.BlockSpec((heads, rows, keys_len), lambda step, seg: (0, step, 0)),
            ],
        ),
        out_shape=[
            jax.ShapeDtypeStruct((count, width), BF16),
            jax.ShapeDtypeStruct((heads, count, keys_len), BF16),
        ],
        compiler_params=pltpu.CompilerParams(vmem_limit_bytes=VMEM_LIMIT),
        cost_estimate=pl.CostEstimate(
            flops=8 * count * keys_len * heads * 128,
            bytes_accessed=2 * heads * count * keys_len,
            transcendentals=heads * count * keys_len,
        ),
        name="attend",
    )(seg_query, queries, keys, values, seg_key[None])


def attend_back_kernel(
    heads, q_ref, k_ref, v_ref, out_ref, grad_ref, prob_ref, dq_ref, dk_ref, dv_ref, dk_sum, dv_sum
):
    step = pl.program_id(0)

    @pl.when(step == 0)
    def _():
        dk_sum[...] = jnp.zeros_like(dk_sum)
        dv_sum[...] = jnp.zeros_like(dv_sum)

    dq_parts, dk_parts, dv_parts = [], [], []
    for head in range(heads):
        lanes = slice(head * HD, (head + 1) * HD)
        grad = grad_ref[:, lanes]
        prob = prob_ref[head]
        grad_prob = dot(grad, v_ref[:, lanes], 1, 1)
        delta = jnp.sum(grad.astype(F32) * out_ref[:, lanes].astype(F32), axis=-1, keepdims=True)
        grad_score = (prob.astype(F32) * (grad_prob - delta)).astype(BF16)
        dq_parts.append(dot(grad_score, k_ref[:, lanes]))
        dk_parts.append(dot(grad_score, q_ref[:, lanes], 0, 0))
        dv_parts.append(dot(prob, grad, 0, 0))
    dq_ref[...] = (jnp.concatenate(dq_parts, axis=-1) * FACTOR).astype(BF16)
    dk_sum[...] += jnp.concatenate(dk_parts, axis=-1)
    dv_sum[...] += jnp.concatenate(dv_parts, axis=-1)

    @pl.when(step == pl.num_programs(0) - 1)
    def _():
        dk_ref[...] = (dk_sum[...] * FACTOR).astype(BF16)
        dv_ref[...] = dv_sum[...].astype(BF16)


def attend_back(queries, keys, values, attended, grad, prob):
    count, width = queries.shape
    keys_len = keys.shape[0]
    heads = width // HD
    rows = min(256, count)
    whole = lambda step: (0, 0)
    chunk = lambda step: (step, 0)
    return pl.pallas_call(
        functools.partial(attend_back_kernel, heads),
        grid=(count // rows,),
        in_specs=[
            pl.BlockSpec((rows, width), chunk),
            pl.BlockSpec((keys_len, width), whole),
            pl.BlockSpec((keys_len, width), whole),
            pl.BlockSpec((rows, width), chunk),
            pl.BlockSpec((rows, width), chunk),
            pl.BlockSpec((heads, rows, keys_len), lambda step: (0, step, 0)),
        ],
        out_specs=[
            pl.BlockSpec((rows, width), chunk),
            pl.BlockSpec((keys_len, width), whole),
            pl.BlockSpec((keys_len, width), whole),
        ],
        out_shape=[
            jax.ShapeDtypeStruct((count, width), BF16),
            jax.ShapeDtypeStruct((keys_len, width), BF16),
            jax.ShapeDtypeStruct((keys_len, width), BF16),
        ],
        scratch_shapes=[
            pltpu.VMEM((keys_len, width), F32),
            pltpu.VMEM((keys_len, width), F32),
        ],
        compiler_params=pltpu.CompilerParams(vmem_limit_bytes=VMEM_LIMIT),
        cost_estimate=pl.CostEstimate(
            flops=16 * count * keys_len * heads * 128,
            bytes_accessed=2 * heads * count * keys_len,
            transcendentals=0,
        ),
        name="attend_back",
    )(queries, keys, values, attended, grad, prob)


def gelu_pair(inputs):
    square = inputs * inputs
    tanh = jnp.tanh(GELU_COEF * (inputs + 0.044715 * inputs * square))
    value = 0.5 * inputs * (1.0 + tanh)
    slope = 0.5 * (1.0 + tanh) + 0.5 * inputs * (1.0 - tanh * tanh) * (
        GELU_COEF * (1.0 + 3.0 * 0.044715 * square)
    )
    return value, slope


def layer_norm(inputs):
    average = jnp.mean(inputs, axis=-1, keepdims=True)
    centred = inputs - average
    spread = jnp.mean(centred * centred, axis=-1, keepdims=True)
    scale = lax.rsqrt(spread + EPSILON)
    return centred * scale, scale


def layer_norm_back(grad, norm, scale):
    first = jnp.mean(grad, axis=-1, keepdims=True)
    second = jnp.mean(grad * norm, axis=-1, keepdims=True)
    return (grad - first - norm * second) * scale


def shards(
    tokens,
    cotangent,
    lengths,
    cond_index,
    cond_table,
    w_mod,
    b_mod,
    w_qkv,
    b_query,
    b_value,
    w_out,
    b_out,
    w_up,
    b_up,
    w_down,
    b_down,
):
    rows_dev, piece, width = tokens.shape
    dp, band = lax.axis_size("dp"), lax.axis_size("band")
    me, group = lax.axis_index("dp"), lax.axis_index("band")
    images = lengths.shape[1]
    rows = rows_dev * dp
    spans = band // rows
    assert band % rows == 0 and dp & (dp - 1) == 0 and band & (band - 1) == 0
    across = band // dp
    head_width = width // dp
    mod_width = w_mod.shape[1]
    hidden_width = w_up.shape[1]

    def turned(index, count=dp):
        table = jnp.array([reverse_bits(place, count) for place in range(count)], jnp.int32)
        return table[index]

    def target(d, b, turn):
        slot = (b % rows) // dp
        local = (slot + turn) % rows_dev
        home = reverse_bits(b % dp, dp)
        to_group = (rows_dev * reverse_bits(d, dp) + local) * spans + b // rows
        return home * band + to_group

    outward = [
        [(d * band + b, target(d, b, turn)) for d in range(dp) for b in range(band)]
        for turn in range(rows_dev)
    ]
    inward = [[(there, here) for here, there in pairs] for pairs in outward]
    both = ("dp", "band")
    my_slot = (group % rows) // dp

    def to_groups(local):
        return jnp.stack(
            [
                lax.ppermute(pick(local, (my_slot + turn) % rows_dev), both, outward[turn])
                for turn in range(rows_dev)
            ]
        )

    def from_groups(held):
        came = jnp.stack(
            [lax.ppermute(held[turn], both, inward[turn]) for turn in range(rows_dev)]
        )
        return jnp.stack([pick(came, (local - my_slot) % rows_dev) for local in range(rows_dev)])

    group_row = group // spans
    my_local = group_row % rows_dev
    my_row = rows_dev * turned(group_row // rows_dev) + my_local

    def piece_of(turn, mask):
        slot = (my_local - turn) % rows_dev
        return (group % spans) * rows + slot * dp + turned(me ^ mask)

    order = xor_order(dp)

    tokens_own = to_groups(tokens)
    facts = gather_all(jnp.concatenate([lengths, cond_index], axis=1), "dp", dp)
    facts = facts.reshape(rows, 2 * images)
    lengths_all, index_all = facts[:, :images], facts[:, images:]
    image_ends = jnp.cumsum(pick(lengths_all, my_row))
    class_hot = (
        index_all.reshape(-1)[:, None] == jnp.arange(cond_table.shape[0], dtype=jnp.int32)
    ).astype(BF16)
    condition = dot(class_hot, cond_table)
    silu_all = jax.nn.silu(condition).astype(BF16)
    silu_own = pick(silu_all.reshape(rows, images, width), my_row)
    b_mod_own = lax.dynamic_slice_in_dim(b_mod, me * mod_width, mod_width)
    mod_part = dot(silu_own, w_mod) + b_mod_own
    modulation = jnp.transpose(gather_all(mod_part, "dp", dp), (1, 0, 2)).reshape(images, 6, width)

    def segment(piece_index):
        return jnp.sum((image_ends <= piece_index * piece).astype(jnp.int32))

    seg_own = [segment(piece_of(turn, 0)) for turn in range(rows_dev)]
    seg_all = jnp.stack(
        [segment(piece_of(turn, mask)) for mask in order for turn in range(rows_dev)]
    )
    mod_own = jnp.stack([pick(modulation, seg) for seg in seg_own])[:, :, None, :]
    shift_a, scale_a, gate_a, shift_b, scale_b, gate_b = [mod_own[:, at] for at in range(6)]

    blocks = 3
    kind_of = [
        [next(kind for kind in range(3) if (kind * dp + d) % 3 == slot) for slot in range(3)]
        for d in range(dp)
    ]
    w_slots = [
        lax.ppermute(
            w_qkv[:, slot * head_width : (slot + 1) * head_width],
            "dp",
            [(d, (blocks * d + slot) % dp) for d in range(dp)],
        )
        for slot in range(3)
    ]
    kinds = jnp.array(kind_of, jnp.int32)[me]
    slot_of = [(kind * dp + me) % 3 for kind in range(3)]
    bias_kinds = jnp.stack(
        [
            lax.dynamic_slice_in_dim(b_query, me * head_width, head_width),
            jnp.zeros((head_width,), F32),
            lax.dynamic_slice_in_dim(b_value, me * head_width, head_width),
        ]
    )

    def to_rows(matrix):
        depth = matrix.shape[0] // dp
        parted = matrix.reshape(dp, depth, matrix.shape[1])
        got = jnp.stack(exchange_columns(parted, "dp", dp))
        return jnp.concatenate([pick(got, me ^ place) for place in range(dp)], axis=1)

    inputs = tokens_own.astype(F32)
    norm_a, spread_a = layer_norm(inputs)
    hidden_a = (norm_a * (1.0 + scale_a) + shift_a).astype(BF16)
    hidden_a_all = gather_xor(hidden_a, "dp", dp).reshape(-1, width)
    count = hidden_a_all.shape[0]
    projected = jnp.stack(
        [
            (dot(hidden_a_all, w_slots[slot]) + pick(bias_kinds, kinds[slot])).astype(BF16)
            for slot in range(3)
        ]
    )
    queries, keys, values = [pick(projected, slot_of[kind]) for kind in range(3)]
    keys_row, values_row, seg_row = keys, values, seg_all
    if spans > 1:
        mates = [[at * spans + span for span in range(spans)] for at in range(rows)]
        keys_row, values_row, seg_row = [
            lax.all_gather(member, "band", axis=0, tiled=True, axis_index_groups=mates)
            for member in (keys, values, seg_all)
        ]
    attended, prob_low = attend(
        queries, keys_row, values_row, seg_all, jnp.repeat(seg_row, piece), piece
    )
    w_out_rows = to_rows(w_out)

    def split_own(partial):
        return partial.reshape((dp, rows_dev, piece, width))

    branch = scatter_sum_xor(split_own(dot(attended, w_out_rows)), "dp", dp) + b_out
    middle = inputs + gate_a * branch
    norm_b, spread_b = layer_norm(middle)
    hidden_b = (norm_b * (1.0 + scale_b) + shift_b).astype(BF16)
    hidden_b_all = gather_xor(hidden_b, "dp", dp).reshape(count, width)

    grad_output = to_groups(cotangent).astype(F32)
    grad_mlp = (gate_b * grad_output).astype(BF16)
    grad_mlp_all = gather_xor(grad_mlp, "dp", dp).reshape(count, width)
    w_down_rows = to_rows(w_down)
    b_up_own = lax.dynamic_slice_in_dim(b_up, me * hidden_width, hidden_width)
    pre_act = dot(hidden_b_all, w_up) + b_up_own
    value, slope = gelu_pair(pre_act)
    activated = value.astype(BF16)
    slope = slope.astype(BF16)
    grad_act = dot(grad_mlp_all, w_down_rows, 1, 1)
    grad_pre = (grad_act * slope.astype(F32)).astype(BF16)
    grad_hidden_b = scatter_sum_xor(split_own(dot(grad_pre, w_up, 1, 1)), "dp", dp)
    mlp_out = scatter_sum_xor(split_own(dot(activated, w_down_rows)), "dp", dp) + b_down
    output = from_groups((middle + gate_b * mlp_out).astype(BF16))
    grad_w_down = dot(activated, grad_mlp_all, 0, 0).astype(BF16)
    grad_w_up = dot(hidden_b_all, grad_pre, 0, 0).astype(BF16)

    grad_middle = grad_output + layer_norm_back(grad_hidden_b * (1.0 + scale_b), norm_b, spread_b)
    grad_branch = (gate_a * grad_middle).astype(BF16)
    grad_branch_all = gather_xor(grad_branch, "dp", dp).reshape(count, width)
    grad_attended = dot(grad_branch_all, w_out_rows, 1, 1).astype(BF16)
    grad_w_out = dot(attended, grad_branch_all, 0, 0).astype(BF16)
    grad_q, grad_k, grad_v = attend_back(
        queries, keys_row, values_row, attended, grad_attended, prob_low
    )
    if spans > 1:
        grad_k, grad_v = [
            lax.psum_scatter(
                member, "band", scatter_dimension=0, tiled=True, axis_index_groups=mates
            )
            for member in (grad_k, grad_v)
        ]
    grad_kinds = jnp.stack([grad_q, grad_k, grad_v])
    grad_slots = [pick(grad_kinds, kinds[slot]) for slot in range(3)]
    grad_hidden_a = sum(dot(grad_slots[slot], w_slots[slot], 1, 1) for slot in range(3))
    grad_hidden_a = scatter_sum_xor(split_own(grad_hidden_a), "dp", dp)
    grad_w_slots = [dot(hidden_a_all, grad_slots[slot], 0, 0).astype(BF16) for slot in range(3)]
    grad_tokens = grad_middle + layer_norm_back(grad_hidden_a * (1.0 + scale_a), norm_a, spread_a)
    grad_tokens = from_groups(grad_tokens.astype(BF16))

    deep, unit = width // dp, width // band

    def sum_groups(pieces):
        return lax.psum_scatter(pieces, "band", scatter_dimension=0, tiled=False)

    swap = [
        (d * band + across * to + at, to * band + across * d + at)
        for d in range(dp)
        for to in range(dp)
        for at in range(across)
    ]
    up_pieces = grad_w_up.reshape(dp, deep, across, hidden_width // across)
    up_pieces = jnp.transpose(up_pieces, (0, 2, 1, 3)).reshape(band, deep, -1)
    down_pieces = grad_w_down.reshape(across, hidden_width // across, dp, deep)
    down_pieces = jnp.transpose(down_pieces, (2, 0, 1, 3)).reshape(band, -1, deep)
    final_up = lax.ppermute(sum_groups(up_pieces), both, swap).astype(F32)
    final_down = lax.ppermute(sum_groups(down_pieces), both, swap).astype(F32)
    out_pieces = jnp.transpose(grad_w_out.reshape(deep, band, unit), (1, 0, 2))
    final_out = sum_groups(out_pieces).astype(F32)
    slot_table = {}
    for turn in range(3):
        for at in range(across):
            slots = {
                slot
                for d in range(dp)
                for slot in range(3)
                if (band * kind_of[d][slot] + across * d + at) % 3 == turn
            }
            assert len(slots) == 1
            slot_table[turn, at] = slots.pop()
    unit_slots = [
        jnp.transpose(member.reshape(dp, deep, across, unit), (0, 2, 1, 3))
        for member in grad_w_slots
    ]
    qkv_pieces = jnp.stack(
        [
            jnp.stack([unit_slots[slot_table[turn, at]][:, at] for at in range(across)], axis=1)
            for turn in range(3)
        ],
        axis=2,
    ).reshape(band, 3, deep, unit)
    qkv_sum = sum_groups(qkv_pieces)
    final_qkv = []
    for turn in range(3):
        pairs = []
        for d in range(dp):
            for at in range(across):
                kind = kind_of[d][slot_table[turn, at]]
                place = band * kind + across * d + at
                assert place % 3 == turn
                for to in range(dp):
                    pairs.append((d * band + across * to + at, to * band + place // 3))
        final_qkv.append(lax.ppermute(qkv_sum[turn], both, pairs))
    final_qkv = jnp.concatenate(final_qkv, axis=1).astype(F32)

    grad_mod_pieces = jnp.stack(
        [
            jnp.sum(member, axis=1)
            for member in (
                grad_hidden_a,
                grad_hidden_a * norm_a,
                grad_middle * branch,
                grad_hidden_b,
                grad_hidden_b * norm_b,
                grad_output * mlp_out,
            )
        ],
        axis=1,
    )
    grad_mod = sum(
        jnp.where(
            (jnp.arange(images, dtype=jnp.int32) == seg_own[turn])[:, None, None],
            grad_mod_pieces[turn][None],
            0.0,
        )
        for turn in range(rows_dev)
    )
    grad_mod = jnp.transpose(grad_mod.reshape(images, dp, mod_width), (1, 0, 2))
    grad_mod_own = sum(exchange_columns(grad_mod, "dp", dp))
    high = grad_mod_own.astype(BF16)
    low = (grad_mod_own - high.astype(F32)).astype(BF16)
    grad_silu = dot(jnp.concatenate([high, low], axis=0), w_mod, 1, 1)
    grad_silu = grad_silu[:images] + grad_silu[images:]
    bias_own = jnp.concatenate(
        [
            jnp.sum(grad_mlp.astype(F32), axis=(0, 1)),
            jnp.sum(grad_branch.astype(F32), axis=(0, 1)),
            jnp.sum(grad_pre.astype(F32), axis=0),
            jnp.sum(grad_q.astype(F32), axis=0),
            jnp.sum(grad_v.astype(F32), axis=0),
        ]
    )
    packed = jnp.concatenate([grad_mod_own.reshape(-1), grad_silu.reshape(-1), bias_own])
    packed = gather_all(packed, "band", band)
    mod_size, silu_size = images * mod_width, images * width
    grad_mod_groups = packed[:, :mod_size].reshape(band * images, mod_width)
    grad_silu_groups = packed[:, mod_size : mod_size + silu_size].reshape(rows, spans, -1).sum(1)
    bias_sum = jnp.sum(packed[:, mod_size + silu_size :], axis=0)
    final_pack = jnp.concatenate(
        [grad_silu_groups.reshape(-1), jnp.sum(grad_mod_groups, axis=0), bias_sum]
    )
    final_pack = gather_all(final_pack, "dp", dp)
    silu_end = rows * silu_size
    grad_silu_rows = jnp.sum(final_pack[:, :silu_end], axis=0).reshape(rows, images, width)
    final_b_mod = final_pack[:, silu_end : silu_end + mod_width].reshape(-1)
    rest = final_pack[:, silu_end + mod_width :]
    final_b_down = jnp.sum(rest[:, :width], axis=0)
    final_b_out = jnp.sum(rest[:, width : 2 * width], axis=0)
    at = 2 * width
    final_b_up = rest[:, at : at + hidden_width].reshape(-1)
    at = at + hidden_width
    final_b_query = rest[:, at : at + head_width].reshape(-1)
    final_b_value = rest[:, at + head_width :].reshape(-1)
    row_order = jnp.array(
        [
            rows_dev * reverse_bits(place // rows_dev, dp) + place % rows_dev
            for place in range(rows)
        ],
        jnp.int32,
    )
    sigmoid = jax.nn.sigmoid(condition)
    silu_slope = sigmoid * (1.0 + condition * (1.0 - sigmoid))
    grad_condition = grad_silu_rows * silu_slope.reshape(rows, images, width)[row_order]
    index_groups = index_all[row_order].reshape(-1)
    table_hot = (
        jnp.arange(cond_table.shape[0], dtype=jnp.int32)[:, None] == index_groups[None]
    ).astype(F32)
    final_table = jnp.dot(table_hot, grad_condition.reshape(-1, width), precision=HIGHEST)
    mod_share = lax.dynamic_slice_in_dim(
        grad_mod_groups, (group % across) * (mod_width // across), mod_width // across, axis=1
    )
    mod_share = lax.ppermute(mod_share, both, swap)
    silu_groups = jnp.repeat(silu_all.reshape(rows, images, width)[row_order], spans, axis=0)
    silu_share = lax.dynamic_slice_in_dim(
        silu_groups.reshape(band * images, width), me * deep, deep, axis=1
    )
    final_mod = lax.dot_general(
        silu_share.astype(F32),
        mod_share,
        (((0,), (0,)), ((), ())),
        precision=HIGHEST,
        preferred_element_type=F32,
    )
    return (
        output,
        grad_tokens,
        final_table,
        final_mod,
        final_qkv,
        final_out,
        final_up,
        final_down,
        final_b_mod,
        final_b_query,
        final_b_value,
        final_b_out,
        final_b_up,
        final_b_down,
    )


def solution(mesh):
    rows = P("dp", "band", None)
    split = P(None, "dp")
    spread = P("dp", "band")
    return jax.shard_map(
        shards,
        mesh=mesh,
        in_specs=(
            rows,
            rows,
            P("dp", None),
            P("dp", None),
            P(),
            split,
            P(),
            split,
            P(),
            P(),
            split,
            P(),
            split,
            P(),
            split,
            P(),
        ),
        out_specs=(
            rows,
            rows,
            P(),
            spread,
            spread,
            spread,
            spread,
            P("band", "dp"),
            P(),
            P(),
            P(),
            P(),
            P(),
            P(),
        ),
        check_vma=False,
    )
```

time: 1870 us -> 713 us (0.38)
  waiting for transfers between devices: 1420 us -> 240 us
  starting transfers between devices: 0.61 us -> 88.1 us
  matrix products: 161 us -> 75.7 us
  local copies, waits for them, and re-layouts: 183 us -> 134 us
  blocking collectives: 43 us -> 0 us
  Pallas kernels: 0 us -> 40.6 us
  between operations: 15.1 us -> 54.1 us
  other arithmetic: 34.3 us -> 71.9 us
    reduce_scatter x2 -> x4, waiting for transfers between devices: 863 us -> 69.3 us  [sum_groups(): return lax.psum_scatter(pieces, 'band', scatter_dimension=0, tiled=False)]
    all_gather x7 -> x0, waiting for transfers between devices: 416 us -> none  [the longest x1 100 us: shards(): lax.all_gather(w_mod, 'dp', axis=1, tiled=True)]
    ppermute x0 -> x51, waiting for transfers between devices: none -> 171 us  [the longest x17 71.8 us: gather_xor(): lax.ppermute(held, axis, xor_perm(count, bit))]
    psum x1 -> x0, waiting for transfers between devices: 134 us -> none  [shards(): lax.psum((grad_b_mod, grad_b_query, grad_b_value, grad_b_out, grad_b_up,...]
    ppermute x0 -> x51, starting transfers between devices: none -> 87.6 us  [the longest x17 24.7 us: gather_xor(): lax.ppermute(held, axis, xor_perm(count, bit))]
    dot_general x33 -> x23, matrix products: 161 us -> 75.7 us  [the longest x21 68 us: dot(): lax.dot_general(left, right, (((left_dim,), (right_dim,)), ((), ())), pre...]
    unnamed x137 -> x185, local copies, waits for them, and re-layouts: 63.4 us -> 12.5 us
    psum x1 -> x0, blocking collectives: 43 us -> none  [shards(): lax.psum((grad_b_mod, grad_b_query, grad_b_value, grad_b_out, grad_b_up,...]
  transfers between devices with their start and end apart: 11 -> 55, of which waited for: 9 -> 26; matrix products, arithmetic and copies ran while one was open for 8% -> 32% of each run, Pallas kernels for 0% -> 4%
where the time goes in v1:
time: 713 us; the launch traced here: 705 us
  waiting for transfers between devices  240 us (34%)
  local copies, waits for them, and re-layouts  134 us (19%)
  starting transfers between devices  88.1 us (12%)
  matrix products  75.7 us (11%)
  other arithmetic  71.9 us (10%)
  between operations  54.1 us (8%)
  Pallas kernels  40.6 us (6%)
    ppermute x17, waiting for transfers between devices, gather_xor(): lax.ppermute(held, axis, xor_perm(count, bit))  71.8 us
    reduce_scatter x4, waiting for transfers between devices, sum_groups(): return lax.psum_scatter(pieces, 'band', scatter_dimension=0, tiled=False)  69.3 us
    dot_general x21, matrix products, dot(): lax.dot_general(left, right, (((left_dim,), (right_dim,)), ((), ())), pre...  68 us
    ppermute x8, waiting for transfers between devices, scatter_sum_xor(): came = lax.ppermute(held[half:].astype(BF16), axis, xor_perm(count, bit))  40.1 us
    pallas_call x1, Pallas kernels, attend_back(): pl.pallas_call(functools.partial(attend_back_kernel, heads), grid=(count...  25.4 us
    ppermute x17, starting transfers between devices, gather_xor(): lax.ppermute(held, axis, xor_perm(count, bit))  24.7 us
    dynamic_slice x13, local copies, waits for them, and re-layouts, pick(): return lax.dynamic_index_in_dim(stack, place, axis, keepdims=False)  23.6 us
    ppermute x9, waiting for transfers between devices, exchange_columns(): lax.ppermute(pick(parts, me ^ mask), axis, xor_perm(count, mask))  21.5 us
  transfers between devices with their start and end apart: 55, of which 26 were waited for; matrix products, arithmetic and copies ran while one was open for 32% of the time, Pallas kernels for 4%

profile of v1, /device:TPU:4, one launch (start us, length us, event | category | flops | bytes accessed | tf_op | source)
XLA Modules:
  0.0 704.8 jit_solution(14250948716880725479)
XLA Ops:
  58.2 9.7 %collective-permute-done.6 = bf16[1,2,128,1152]{3,2,1,0:T(8,128)(2,1)} collective-permute-done((bf16[1,2,128,1152]{3,2,1,0:T(8,128)(2,1)}, bf16[1,2,128,1152]{3,2,1,0:T(8,128)(2,1)}, u32[]{:S(2)}, u32[]{:S(2)}) %collective-permute-start.6) | collective-permute-done | bytes 589856 | tf_op jit(solution)/shard_map/ppermute | solution.py:60
  71.6 6.7 collective-permute-start.8
  87.2 5.1 stack.237.segq_ref
  118.2 15.3 %attend.1 = (bf16[1024,288]{1,0:T(8,128)(2,1)}, bf16[4,1024,1024]{2,1,0:T(8,128)(2,1)}) custom-call(s32[8]{0:T(128)} %copy-done.80, bf16[1024,288]{1,0:T(8,128)(2,1)} %bitcast.340, bf16[1024,288]{1,0:T(8,128)(2,1)} %bitcast.338, bf16[1024,288]{1,0:T(8,128)(2,1)} %bitcast.336, s32[1,1024]{1,0:T(1,128)} %bitcast.372), custom_call_target="tpu_custom_call" | custom-call | flops 4294967296 | bytes 8388608 | tf_op jit(solution)/shard_map/attend/pallas_call | solution.py:122
  146.5 5.7 reshape.426
  155.9 6.3 constant_dynamic-slice_fusion.20
  180.5 9.2 %collective-permute-done.19 = bf16[1152,288]{0,1:T(8,128)(2,1)} collective-permute-done((bf16[1152,288]{0,1:T(8,128)(2,1)}, bf16[1152,288]{0,1:T(8,128)(2,1)}, u32[]{:S(2)}, u32[]{:S(2)}) %collective-permute-start.19) | collective-permute-done | bytes 663584 | tf_op jit(solution)/shard_map/ppermute | solution.py:85
  191.8 12.1 %collective-permute-done.20 = bf16[1152,288]{0,1:T(8,128)(2,1)} collective-permute-done((bf16[1152,288]{0,1:T(8,128)(2,1)}, bf16[1152,288]{0,1:T(8,128)(2,1)}, u32[]{:S(2)}, u32[]{:S(2)}) %collective-permute-start.20) | collective-permute-done | bytes 663584 | tf_op jit(solution)/shard_map/ppermute | solution.py:85
  206.0 10.5 %collective-permute-done.27 = bf16[1,2,128,1152]{3,2,1,0:T(8,128)(2,1)} collective-permute-done((bf16[1,2,128,1152]{3,2,1,0:T(8,128)(2,1)}, bf16[1,2,128,1152]{3,2,1,0:T(8,128)(2,1)}, u32[]{:S(2)}, u32[]{:S(2)}) %collective-permute-start.27) | collective-permute-done | bytes 589856 | tf_op jit(solution)/shard_map/ppermute | solution.py:60
  218.0 11.1 %collective-permute-done.16 = bf16[1,2,128,1152]{3,2,1,0:T(8,128)(2,1)} collective-permute-done((bf16[1,2,128,1152]{3,2,1,0:T(8,128)(2,1)}, bf16[1,2,128,1152]{3,2,1,0:T(8,128)(2,1)}, u32[]{:S(2)}, u32[]{:S(2)}) %collective-permute-start.16) | collective-permute-done | bytes 589856 | tf_op jit(solution)/shard_map/ppermute | solution.py:60
  230.7 6.2 pad_maximum_fusion.1
  236.9 6.0 constant_dynamic-slice_fusion.16
  250.8 7.1 %convert_reduce_fusion = (f32[1152]{0:T(1024)}, bf16[1024,1152]{1,0:T(8,128)(2,1)S(1)}) fusion(f32[1024,1152]{1,0:T(8,128)S(1)} %convolution_add_fusion.1, bf16[1024,1152]{1,0:T(8,128)(2,1)S(1)} %bitcast.331, bf16[1152,288]{0,1:T(8,128)(2,1)S(1)} %bitcast.344, bf16[1152,288]{0,1:T(8,128)(2,1)S(1)} %bitcast.346, bf16[1152,288]{0,1:T(8,128)(2,1)S(1)} %bitcast.348, ...), kind=kOutput, calls=%fused_computation.8 | convolution fusion | flops 2754477056 | bytes 12096000 | tf_op jit(solution)/shard_map/dot_general | solution.py:25
  271.4 13.7 %collective-permute-done.30 = bf16[1,2,128,1152]{3,2,1,0:T(8,128)(2,1)S(1)} collective-permute-done((bf16[1,2,128,1152]{3,2,1,0:T(8,128)(2,1)S(1)}, bf16[1,2,128,1152]{3,2,1,0:T(8,128)(2,1)S(1)}, u32[]{:S(2)}, u32[]{:S(2)}) %collective-permute-start.30) | collective-permute-done | bytes 589856 | tf_op jit(solution)/shard_map/ppermute | solution.py:76
  285.8 11.1 %collective-permute-done.22 = bf16[1,2,128,1152]{3,2,1,0:T(8,128)(2,1)S(1)} collective-permute-done((bf16[1,2,128,1152]{3,2,1,0:T(8,128)(2,1)S(1)}, bf16[1,2,128,1152]{3,2,1,0:T(8,128)(2,1)S(1)}, u32[]{:S(2)}, u32[]{:S(2)}) %collective-permute-start.22) | collective-permute-done | bytes 589856 | tf_op jit(solution)/shard_map/ppermute | solution.py:76
  302.7 14.2 %collective-permute-done.31 = bf16[1,2,128,1152]{3,2,1,0:T(8,128)(2,1)S(1)} collective-permute-done((bf16[1,2,128,1152]{3,2,1,0:T(8,128)(2,1)S(1)}, bf16[1,2,128,1152]{3,2,1,0:T(8,128)(2,1)S(1)}, u32[]{:S(2)}, u32[]{:S(2)}) %collective-permute-start.31) | collective-permute-done | bytes 589856 | tf_op jit(solution)/shard_map/ppermute | solution.py:60
  326.2 8.3 %convolution_convert_fusion = bf16[1152,1152]{1,0:T(8,128)(2,1)} fusion(bf16[1024,1152]{1,0:T(8,128)(2,1)} %bitcast.332, f32[1024,1152]{1,0:T(8,128)} %copy-done.82), kind=kOutput, calls=%fused_computation.3 | convolution fusion | flops 2729852928 | bytes 9732096 | tf_op jit(solution)/shard_map/dot_general | solution.py:25
  334.5 5.2 copy.115
  339.7 7.4 %reshape.441 = bf16[2,576,4,288]{1,0,3,2:T(2,128)(2,1)} reshape(bf16[1152,1152]{0,1:T(8,128)(2,1)} %copy.115) | data formatting | bytes 5308416 | tf_op jit(solution)/shard_map/reshape | solution.py:462
  374.5 7.1 %convolution_convert_fusion.1 = bf16[1152,1152]{1,0:T(8,128)(2,1)} fusion(bf16[1024,1152]{1,0:T(8,128)(2,1)} %bitcast.330, bf16[1024,1152]{1,0:T(8,128)(2,1)} %copy-done.83), kind=kOutput, calls=%fused_computation.4 | convolution fusion | flops 2719236096 | bytes 7372800 | tf_op jit(solution)/shard_map/dot_general | solution.py:25
  381.7 7.4 %reshape.439 = bf16[4,288,2,576]{3,2,1,0:T(2,128)(2,1)} reshape(bf16[1152,1152]{1,0:T(8,128)(2,1)} %convolution_convert_fusion.1) | data formatting | bytes 5308416 | tf_op jit(solution)/shard_map/reshape | solution.py:460
  407.2 25.4 %attend_back.1 = (bf16[1024,288]{1,0:T(8,128)(2,1)}, bf16[1024,288]{1,0:T(8,128)(2,1)}, bf16[1024,288]{1,0:T(8,128)(2,1)}) custom-call(bf16[1024,288]{1,0:T(8,128)(2,1)} %bitcast.341, bf16[1024,288]{1,0:T(8,128)(2,1)} %bitcast.339, bf16[1024,288]{1,0:T(8,128)(2,1)} %bitcast.337, bf16[1024,288]{1,0:T(8,128)(2,1)} %get-tuple-element.19.out_ref, ...), custom_call_target="tpu_custom_call" | custom-call | flops 8589934592 | bytes 8388608 | tf_op jit(solution)/shard_map/attend_back/pallas_call | solution.py:190
  475.5 10.3 %collective-permute-done.34 = bf16[1,2,128,1152]{3,2,1,0:T(8,128)(2,1)} collective-permute-done((bf16[1,2,128,1152]{3,2,1,0:T(8,128)(2,1)}, bf16[1,2,128,1152]{3,2,1,0:T(8,128)(2,1)}, u32[]{:S(2)}, u32[]{:S(2)}) %collective-permute-start.34) | collective-permute-done | bytes 589856 | tf_op jit(solution)/shard_map/ppermute | solution.py:76
  501.8 10.6 %collective-permute-done.40 = f32[1,15552]{1,0:T(1,128)S(1)} collective-permute-done((f32[1,15552]{1,0:T(1,128)S(1)}, f32[1,15552]{1,0:T(1,128)S(1)}, u32[]{:S(2)}, u32[]{:S(2)}) %collective-permute-start.40) | collective-permute-done | bytes 62240 | tf_op jit(solution)/shard_map/ppermute | solution.py:60
  512.5 16.7 %collective-permute-start.41 = (f32[2,15552]{1,0:T(2,128)S(1)}, f32[2,15552]{1,0:T(2,128)S(1)}, u32[]{:S(2)}, u32[]{:S(2)}) collective-permute-start(f32[2,15552]{1,0:T(2,128)S(1)} %pad_maximum_fusion.30), channel_id=1, source_target_pairs={{0,2},{1,3},{2,0},{3,1},{4,6},{5,7},{6,4},{7,5},{8,10},{9,11},{10,... | collective-permute-start | bytes 373256 | tf_op jit(solution)/shard_map/ppermute | solution.py:60
  533.3 6.7 collective-permute-start.35
  540.8 36.2 %reduce-scatter.9.cloned.1.call-done = bf16[1,288,576]{2,1,0:T(8,128)(2,1)} async-done(((bf16[8,288,576]{2,1,0:T(8,128)(2,1)}), bf16[1,288,576]{2,1,0:T(8,128)(2,1)}) %reduce-scatter.9.cloned.1.call-update) | async-done | bytes 331792 | tf_op jit(solution)/shard_map/reduce_scatter | solution.py:452
  583.3 6.0 collective-permute-done.42
  600.6 19.9 %collective-permute-done.49 = bf16[288,576]{1,0:T(8,128)(2,1)S(1)} collective-permute-done((bf16[288,576]{1,0:T(8,128)(2,1)}, bf16[288,576]{1,0:T(8,128)(2,1)S(1)}, u32[]{:S(2)}, u32[]{:S(2)}) %collective-permute-start.49) | collective-permute-done | bytes 331808 | tf_op jit(solution)/shard_map/ppermute | solution.py:464
  621.4 6.3 collective-permute-done.45
  635.1 5.4 fusion.51
  640.4 33.1 %reduce-scatter.5.cloned.1.call-done = bf16[1,3,288,144]{3,2,1,0:T(8,128)(2,1)} async-done(((bf16[8,3,288,144]{3,2,1,0:T(8,128)(2,1)}), bf16[1,3,288,144]{3,2,1,0:T(8,128)(2,1)}) %reduce-scatter.5.cloned.1.call-update) | async-done | bytes 248848 | tf_op jit(solution)/shard_map/reduce_scatter | solution.py:452
  (479 shorter events, 289.0 us)
Async XLA Ops:
  7.2 466.7 %reduce-scatter.7.cloned.1.call-start = ((), (), s32[]{:S(2)}) async-start(), calls=%async_computation.5 | async-start | bytes 995328 | tf_op jit(solution)/shard_map/reduce_scatter | solution.py:452
  8.2 22.9 %collective-permute-start.2 = (s32[1,2,8]{2,1,0:T(2,128)S(1)}, s32[1,2,8]{2,1,0:T(2,128)S(1)}, u32[]{:S(2)}, u32[]{:S(2)}) collective-permute-start(s32[1,2,8]{2,1,0:T(2,128)S(1)} %add_bitcast_fusion), channel_id=1, source_target_pairs={{0,16},{8,24},{16,0},{24,8},{1,17},{9,25},{17,1},{25,9},{2,18},{10... | collective-permute-start | bytes 200 | tf_op jit(solution)/shard_map/ppermute | solution.py:60
  10.1 39.7 %collective-permute-start = (bf16[128,1152]{1,0:T(8,128)(2,1)}, bf16[128,1152]{1,0:T(8,128)(2,1)S(1)}, u32[]{:S(2)}, u32[]{:S(2)}) collective-permute-start(bf16[128,1152]{1,0:T(8,128)(2,1)} %get-tuple-element.104), channel_id=1, source_target_pairs={{0,0},{1,16},{2,8},{3,24},{4,1},{5,17},{6,9},{7,25},{8,4},{9,20},{... | collective-permute-start | bytes 884744 | tf_op jit(solution)/shard_map/ppermute | solution.py:301
  15.0 34.8 %collective-permute-start.1 = (bf16[128,1152]{1,0:T(8,128)(2,1)}, bf16[128,1152]{1,0:T(8,128)(2,1)S(1)}, u32[]{:S(2)}, u32[]{:S(2)}) collective-permute-start(bf16[128,1152]{1,0:T(8,128)(2,1)} %get-tuple-element.105), channel_id=1, source_target_pairs={{0,1},{1,17},{2,9},{3,25},{4,0},{5,16},{6,8},{7,24},{8,5},{9,21},{... | collective-permute-start | bytes 884744 | tf_op jit(solution)/shard_map/ppermute | solution.py:301
  56.1 36.2 %collective-permute-start.13 = (bf16[288,288]{1,0:T(8,128)(2,1)}, bf16[288,288]{1,0:T(8,128)(2,1)}, u32[]{:S(2)}, u32[]{:S(2)}) collective-permute-start(bf16[288,288]{1,0:T(8,128)(2,1)} %get-tuple-element.84), channel_id=1, source_target_pairs={{0,24},{8,16},{16,8},{24,0},{1,25},{9,17},{17,9},{25,1},{2,26},{10... | collective-permute-start | bytes 497672 | tf_op jit(solution)/shard_map/ppermute | solution.py:85
  57.9 36.6 %collective-permute-start.12 = (bf16[288,288]{1,0:T(8,128)(2,1)}, bf16[288,288]{1,0:T(8,128)(2,1)}, u32[]{:S(2)}, u32[]{:S(2)}) collective-permute-start(bf16[288,288]{1,0:T(8,128)(2,1)} %get-tuple-element.85), channel_id=1, source_target_pairs={{0,16},{8,24},{16,0},{24,8},{1,17},{9,25},{17,1},{25,9},{2,18},{10... | collective-permute-start | bytes 497672 | tf_op jit(solution)/shard_map/ppermute | solution.py:85
  58.2 36.9 %collective-permute-start.11 = (bf16[288,288]{1,0:T(8,128)(2,1)}, bf16[288,288]{1,0:T(8,128)(2,1)}, u32[]{:S(2)}, u32[]{:S(2)}) collective-permute-start(bf16[288,288]{1,0:T(8,128)(2,1)} %get-tuple-element.86), channel_id=1, source_target_pairs={{0,8},{8,0},{16,24},{24,16},{1,9},{9,1},{17,25},{25,17},{2,10},{10... | collective-permute-start | bytes 497672 | tf_op jit(solution)/shard_map/ppermute | solution.py:85
  70.3 29.2 %collective-permute-start.7 = (bf16[2,2,128,1152]{3,2,1,0:T(8,128)(2,1)}, bf16[2,2,128,1152]{3,2,1,0:T(8,128)(2,1)}, u32[]{:S(2)}, u32[]{:S(2)}) collective-permute-start(bf16[2,2,128,1152]{3,2,1,0:T(8,128)(2,1)} %pad_maximum_fusion.9), channel_id=1, source_target_pairs={{0,8},{8,0},{16,24},{24,16},{1,9},{9,1},{17,25},{25,17},{2,10},{10... | collective-permute-start | bytes 3538952 | tf_op jit(solution)/shard_map/ppermute | solution.py:60
  71.6 29.7 %collective-permute-start.8 = (bf16[1152,288]{0,1:T(8,128)(2,1)}, bf16[1152,288]{0,1:T(8,128)(2,1)}, u32[]{:S(2)}, u32[]{:S(2)}) collective-permute-start(bf16[1152,288]{0,1:T(8,128)(2,1)} %get-tuple-element.64), channel_id=1, source_target_pairs={{0,0},{8,24},{16,16},{24,8},{1,1},{9,25},{17,17},{25,9},{2,2},{10,... | collective-permute-start | bytes 1990664 | tf_op jit(solution)/shard_map/ppermute | solution.py:353
  140.3 27.0 %collective-permute-start.25 = (bf16[128,1152]{1,0:T(8,128)(2,1)}, bf16[128,1152]{1,0:T(8,128)(2,1)S(1)}, u32[]{:S(2)}, u32[]{:S(2)}) collective-permute-start(bf16[128,1152]{1,0:T(8,128)(2,1)} %get-tuple-element.98), channel_id=1, source_target_pairs={{0,0},{1,16},{2,8},{3,24},{4,1},{5,17},{6,9},{7,25},{8,4},{9,20},{... | collective-permute-start | bytes 884744 | tf_op jit(solution)/shard_map/ppermute | solution.py:301
  143.1 24.4 %collective-permute-start.26 = (bf16[128,1152]{1,0:T(8,128)(2,1)}, bf16[128,1152]{1,0:T(8,128)(2,1)}, u32[]{:S(2)}, u32[]{:S(2)}) collective-permute-start(bf16[128,1152]{1,0:T(8,128)(2,1)} %get-tuple-element.99), channel_id=1, source_target_pairs={{0,1},{1,17},{2,9},{3,25},{4,0},{5,16},{6,8},{7,24},{8,5},{9,21},{... | collective-permute-start | bytes 884744 | tf_op jit(solution)/shard_map/ppermute | solution.py:301
  155.6 19.7 %collective-permute-start.15 = (bf16[1,2,128,1152]{3,2,1,0:T(8,128)(2,1)S(1)}, bf16[1,2,128,1152]{3,2,1,0:T(8,128)(2,1)S(1)}, u32[]{:S(2)}, u32[]{:S(2)}) collective-permute-start(bf16[1,2,128,1152]{3,2,1,0:T(8,128)(2,1)S(1)} %slice.378), channel_id=1, source_target_pairs={{0,16},{8,24},{16,0},{24,8},{1,17},{9,25},{17,1},{25,9},{2,18},{10... | collective-permute-start | bytes 1769480 | tf_op jit(solution)/shard_map/ppermute | solution.py:76
  164.8 24.8 %collective-permute-start.19 = (bf16[1152,288]{0,1:T(8,128)(2,1)}, bf16[1152,288]{0,1:T(8,128)(2,1)}, u32[]{:S(2)}, u32[]{:S(2)}) collective-permute-start(bf16[1152,288]{0,1:T(8,128)(2,1)} %bitcast.272), channel_id=1, source_target_pairs={{0,16},{8,24},{16,0},{24,8},{1,17},{9,25},{17,1},{25,9},{2,18},{10... | collective-permute-start | bytes 1990664 | tf_op jit(solution)/shard_map/ppermute | solution.py:85
  167.3 36.5 %collective-permute-start.20 = (bf16[1152,288]{0,1:T(8,128)(2,1)}, bf16[1152,288]{0,1:T(8,128)(2,1)}, u32[]{:S(2)}, u32[]{:S(2)}) collective-permute-start(bf16[1152,288]{0,1:T(8,128)(2,1)} %bitcast.271), channel_id=1, source_target_pairs={{0,24},{8,16},{16,8},{24,0},{1,25},{9,17},{17,9},{25,1},{2,26},{10... | collective-permute-start | bytes 1990664 | tf_op jit(solution)/shard_map/ppermute | solution.py:85
  169.3 47.2 %collective-permute-start.27 = (bf16[1,2,128,1152]{3,2,1,0:T(8,128)(2,1)}, bf16[1,2,128,1152]{3,2,1,0:T(8,128)(2,1)}, u32[]{:S(2)}, u32[]{:S(2)}) collective-permute-start(bf16[1,2,128,1152]{3,2,1,0:T(8,128)(2,1)} %fusion.27), channel_id=1, source_target_pairs={{0,16},{8,24},{16,0},{24,8},{1,17},{9,25},{17,1},{25,9},{2,18},{10... | collective-permute-start | bytes 1769480 | tf_op jit(solution)/shard_map/ppermute | solution.py:60
  177.5 51.7 %collective-permute-start.16 = (bf16[1,2,128,1152]{3,2,1,0:T(8,128)(2,1)}, bf16[1,2,128,1152]{3,2,1,0:T(8,128)(2,1)}, u32[]{:S(2)}, u32[]{:S(2)}) collective-permute-start(bf16[1,2,128,1152]{3,2,1,0:T(8,128)(2,1)} %add_convert_fusion.2), channel_id=1, source_target_pairs={{0,16},{8,24},{16,0},{24,8},{1,17},{9,25},{17,1},{25,9},{2,18},{10... | collective-permute-start | bytes 1769480 | tf_op jit(solution)/shard_map/ppermute | solution.py:60
  217.9 25.4 %collective-permute-start.28 = (bf16[2,2,128,1152]{3,2,1,0:T(8,128)(2,1)S(1)}, bf16[2,2,128,1152]{3,2,1,0:T(8,128)(2,1)S(1)}, u32[]{:S(2)}, u32[]{:S(2)}) collective-permute-start(bf16[2,2,128,1152]{3,2,1,0:T(8,128)(2,1)S(1)} %pad_maximum_fusion.11), channel_id=1, source_target_pairs={{0,8},{8,0},{16,24},{24,16},{1,9},{9,1},{17,25},{25,17},{2,10},{10... | collective-permute-start | bytes 3538952 | tf_op jit(solution)/shard_map/ppermute | solution.py:60
  270.6 26.3 %collective-permute-start.22 = (bf16[1,2,128,1152]{3,2,1,0:T(8,128)(2,1)S(1)}, bf16[1,2,128,1152]{3,2,1,0:T(8,128)(2,1)S(1)}, u32[]{:S(2)}, u32[]{:S(2)}) collective-permute-start(bf16[1,2,128,1152]{3,2,1,0:T(8,128)(2,1)S(1)} %slice.377), channel_id=1, source_target_pairs={{0,16},{8,24},{16,0},{24,8},{1,17},{9,25},{17,1},{25,9},{2,18},{10... | collective-permute-start | bytes 1769480 | tf_op jit(solution)/shard_map/ppermute | solution.py:76
  325.8 166.2 %reduce-scatter.11.cloned.1.call-start = ((), (), s32[]{:S(2)}) async-start(), calls=%async_computation.7 | async-start | bytes 3317760 | tf_op jit(solution)/shard_map/reduce_scatter | solution.py:452
  350.9 226.1 %reduce-scatter.9.cloned.1.call-start = ((), (), s32[]{:S(2)}) async-start(), calls=%async_computation.6 | async-start | bytes 3317760 | tf_op jit(solution)/shard_map/reduce_scatter | solution.py:452
  392.9 280.6 %reduce-scatter.5.cloned.1.call-start = ((), (), s32[]{:S(2)}) async-start(), calls=%async_computation.4 | async-start | bytes 3981312 | tf_op jit(solution)/shard_map/reduce_scatter | solution.py:452
  401.0 139.9 %collective-permute-start.24 = (bf16[128,1152]{1,0:T(8,128)(2,1)}, bf16[128,1152]{1,0:T(8,128)(2,1)S(1)}, u32[]{:S(2)}, u32[]{:S(2)}) collective-permute-start(bf16[128,1152]{1,0:T(8,128)(2,1)} %get-tuple-element.102), channel_id=1, source_target_pairs={{1,0},{17,1},{9,2},{25,3},{0,4},{16,5},{8,6},{24,7},{5,8},{21,9},{... | collective-permute-start | bytes 884744 | tf_op jit(solution)/shard_map/ppermute | solution.py:308
  401.2 179.1 %collective-permute-start.23 = (bf16[128,1152]{1,0:T(8,128)(2,1)}, bf16[128,1152]{1,0:T(8,128)(2,1)}, u32[]{:S(2)}, u32[]{:S(2)}) collective-permute-start(bf16[128,1152]{1,0:T(8,128)(2,1)} %get-tuple-element.103), channel_id=1, source_target_pairs={{0,0},{16,1},{8,2},{24,3},{1,4},{17,5},{9,6},{25,7},{4,8},{20,9},{... | collective-permute-start | bytes 884744 | tf_op jit(solution)/shard_map/ppermute | solution.py:308
  443.5 22.6 %collective-permute-start.33 = (bf16[2,2,128,1152]{3,2,1,0:T(8,128)(2,1)}, bf16[2,2,128,1152]{3,2,1,0:T(8,128)(2,1)}, u32[]{:S(2)}, u32[]{:S(2)}) collective-permute-start(bf16[2,2,128,1152]{3,2,1,0:T(8,128)(2,1)} %bitcast.80), channel_id=1, source_target_pairs={{0,8},{8,0},{16,24},{24,16},{1,9},{9,1},{17,25},{25,17},{2,10},{10... | collective-permute-start | bytes 3538952 | tf_op jit(solution)/shard_map/ppermute | solution.py:76
  469.4 16.5 %collective-permute-start.34 = (bf16[1,2,128,1152]{3,2,1,0:T(8,128)(2,1)}, bf16[1,2,128,1152]{3,2,1,0:T(8,128)(2,1)}, u32[]{:S(2)}, u32[]{:S(2)}) collective-permute-start(bf16[1,2,128,1152]{3,2,1,0:T(8,128)(2,1)} %slice.375), channel_id=1, source_target_pairs={{0,16},{8,24},{16,0},{24,8},{1,17},{9,25},{17,1},{25,9},{2,18},{10... | collective-permute-start | bytes 1769480 | tf_op jit(solution)/shard_map/ppermute | solution.py:76
  491.9 106.8 %collective-permute-start.50 = (bf16[576,288]{0,1:T(8,128)(2,1)}, bf16[576,288]{0,1:T(8,128)(2,1)}, u32[]{:S(2)}, u32[]{:S(2)}) collective-permute-start(bf16[576,288]{0,1:T(8,128)(2,1)} %bitcast.373), channel_id=1, source_target_pairs={{0,0},{1,1},{2,8},{3,9},{4,16},{5,17},{6,24},{7,25},{8,2},{9,3},{1... | collective-permute-start | bytes 995336 | tf_op jit(solution)/shard_map/ppermute | solution.py:465
  512.5 20.9 %collective-permute-start.41 = (f32[2,15552]{1,0:T(2,128)S(1)}, f32[2,15552]{1,0:T(2,128)S(1)}, u32[]{:S(2)}, u32[]{:S(2)}) collective-permute-start(f32[2,15552]{1,0:T(2,128)S(1)} %pad_maximum_fusion.30), channel_id=1, source_target_pairs={{0,2},{1,3},{2,0},{3,1},{4,6},{5,7},{6,4},{7,5},{8,10},{9,11},{10,... | collective-permute-start | bytes 373256 | tf_op jit(solution)/shard_map/ppermute | solution.py:60
  529.2 52.7 %collective-permute-start.36 = (bf16[128,1152]{1,0:T(8,128)(2,1)S(1)}, bf16[128,1152]{1,0:T(8,128)(2,1)S(1)}, u32[]{:S(2)}, u32[]{:S(2)}) collective-permute-start(bf16[128,1152]{1,0:T(8,128)(2,1)S(1)} %get-tuple-element.96), channel_id=1, source_target_pairs={{1,0},{17,1},{9,2},{25,3},{0,4},{16,5},{8,6},{24,7},{5,8},{21,9},{... | collective-permute-start | bytes 884744 | tf_op jit(solution)/shard_map/ppermute | solution.py:308
  533.3 48.5 %collective-permute-start.35 = (bf16[128,1152]{1,0:T(8,128)(2,1)S(1)}, bf16[128,1152]{1,0:T(8,128)(2,1)S(1)}, u32[]{:S(2)}, u32[]{:S(2)}) collective-permute-start(bf16[128,1152]{1,0:T(8,128)(2,1)S(1)} %get-tuple-element.97), channel_id=1, source_target_pairs={{0,0},{16,1},{8,2},{24,3},{1,4},{17,5},{9,6},{25,7},{4,8},{20,9},{... | collective-permute-start | bytes 884744 | tf_op jit(solution)/shard_map/ppermute | solution.py:308
  577.0 43.5 %collective-permute-start.49 = (bf16[288,576]{1,0:T(8,128)(2,1)}, bf16[288,576]{1,0:T(8,128)(2,1)S(1)}, u32[]{:S(2)}, u32[]{:S(2)}) collective-permute-start(bf16[288,576]{1,0:T(8,128)(2,1)} %bitcast.374), channel_id=1, source_target_pairs={{0,0},{1,1},{2,8},{3,9},{4,16},{5,17},{6,24},{7,25},{8,2},{9,3},{1... | collective-permute-start | bytes 995336 | tf_op jit(solution)/shard_map/ppermute | solution.py:464
  592.2 35.5 %collective-permute-start.45 = (f32[32,864]{1,0:T(8,128)S(1)}, f32[32,864]{1,0:T(8,128)S(1)}, u32[]{:S(2)}, u32[]{:S(2)}) collective-permute-start(f32[32,864]{1,0:T(8,128)S(1)} %constant_dynamic-slice_fusion.39), channel_id=1, source_target_pairs={{0,0},{1,1},{2,8},{3,9},{4,16},{5,17},{6,24},{7,25},{8,2},{9,3},{1... | collective-permute-start | bytes 331784 | tf_op jit(solution)/shard_map/ppermute | solution.py:580
  597.8 32.4 %collective-permute-start.44 = (f32[2,42624]{1,0:T(2,128)S(1)}, f32[2,42624]{1,0:T(2,128)S(1)}, u32[]{:S(2)}, u32[]{:S(2)}) collective-permute-start(f32[2,42624]{1,0:T(2,128)S(1)} %pad_maximum_fusion.28), channel_id=1, source_target_pairs={{0,8},{8,0},{16,24},{24,16},{1,9},{9,1},{17,25},{25,17},{2,10},{10... | collective-permute-start | bytes 1022984 | tf_op jit(solution)/shard_map/ppermute | solution.py:60
  (109 other events, 1222.8 us)
Sparse Core Ops, SparseCore 0:
  325.9 60.2 reduce-scatter.6
  389.8 85.1 reduce-scatter.10
  478.9 98.0 reduce-scatter.8
  580.5 92.9 reduce-scatter.4

commit v2 on v1

v2 whole, which is shorter than its diff:
```python
import functools
import math

import jax
import jax.numpy as jnp
from jax import lax
from jax.experimental import pallas as pl
from jax.experimental.pallas import tpu as pltpu
from jax.sharding import PartitionSpec as P

H = 16
HD = 72

EPSILON = 1e-06
HIGHEST = lax.Precision.HIGHEST
NEGATIVE = -1e30
GELU_COEF = 0.7978845608028654
FACTOR = 1.0 / math.sqrt(HD)
LOG2E = math.log2(math.e)
VMEM_LIMIT = 56 * 1024 * 1024
F32 = jnp.float32
BF16 = jnp.bfloat16


def dot(left, right, left_dim=1, right_dim=0):
    return lax.dot_general(
        left, right, (((left_dim,), (right_dim,)), ((), ())), preferred_element_type=F32
    )


def log2(count):
    assert count & (count - 1) == 0
    return count.bit_length() - 1


def reverse_bits(value, count):
    width = log2(count)
    return sum(((value >> at) & 1) << (width - 1 - at) for at in range(width)) if width else 0


def bits_up(count):
    return [1 << place for place in range(log2(count))]


def xor_perm(count, mask):
    return [(place, place ^ mask) for place in range(count)]


def pick(stack, place, axis=0):
    return lax.dynamic_index_in_dim(
        stack, place, axis, keepdims=False, allow_negative_indices=False
    )


def cut(array, start, size, axis=0):
    return lax.dynamic_slice_in_dim(array, start, size, axis, allow_negative_indices=False)


def xor_shuffle(array, mask):
    return jnp.stack([pick(array, mask ^ place) for place in range(array.shape[0])])


def after(array, *others):
    return lax.optimization_barrier((array, *others))[0]


def gather_parts(part, axis, count, *waits):
    held = part[None]
    for bit in reversed(bits_up(count)):
        came = lax.ppermute(held, axis, xor_perm(count, bit))
        if waits and held.shape[0] == 1:
            came = after(came, *waits)
        held = jnp.concatenate([held, came])
    return held


def gather_stack(part, axis, count):
    held = part[None]
    for bit in bits_up(count):
        held = jnp.concatenate([held, lax.ppermute(held, axis, xor_perm(count, bit))], axis=0)
    return held


def gather_all(part, axis, count):
    return xor_shuffle(gather_stack(part, axis, count), lax.axis_index(axis))


def mask_order(count):
    order = [0]
    for bit in reversed(bits_up(count)):
        order = order + [place ^ bit for place in order]
    return order


def scatter_sum(near, far, axis, count, *waits):
    held = near.astype(F32) + lax.ppermute(far, axis, xor_perm(count, 1)).astype(F32)
    for bit in bits_up(count)[1:]:
        half = held.shape[0] // 2
        came = lax.ppermute(held[half:].astype(BF16), axis, xor_perm(count, bit))
        if waits and half == 1:
            came = after(came, *waits)
        held = held[:half] + came.astype(F32)
    return held[0]


def exchange(parts, axis, count):
    held = xor_shuffle(parts, lax.axis_index(axis))[None]
    for bit in reversed(bits_up(count)):
        half = held.shape[1] // 2
        came = lax.ppermute(held[:, half:], axis, xor_perm(count, bit))
        held = jnp.concatenate([held[:, :half], came])
    return held[:, 0]


def scatter_blocks(parts, axis, count):
    me = lax.axis_index(axis)
    held = parts
    for at, bit in enumerate(bits_up(count)):
        held = held.reshape((-1, 2) + parts.shape[1:])
        mine = (me >> at) & 1
        held = pick(held, mine, 1) + lax.ppermute(
            pick(held, mine ^ 1, 1), axis, xor_perm(count, bit)
        )
    return held[0]


def attend_kernel(piece, facts_ref, q_ref, k_ref, v_ref, out_ref, prob_ref):
    step = pl.program_id(1)
    keys_len, lanes = k_ref.shape[-1], q_ref.shape[-1]
    pieces_key, pieces_query = keys_len // piece, lanes // piece
    values = v_ref[0]

    def finish(scores):
        top = jnp.max(scores, axis=0, keepdims=True)
        exponent = jnp.exp2(scores * (FACTOR * LOG2E) - top * (FACTOR * LOG2E))
        total = jnp.sum(exponent, axis=0, keepdims=True)
        prob = (exponent * (1.0 / total)).astype(BF16)
        prob_ref[0] = prob
        out_ref[0] = dot(values, prob).astype(BF16)

    scores = dot(k_ref[0], q_ref[0], 0, 0)

    @pl.when(facts_ref[0] == 1)
    def _():
        finish(scores)

    @pl.when(facts_ref[0] != 1)
    def _():
        seg_key = jnp.concatenate(
            [jnp.full((piece, 1), facts_ref[1 + at], jnp.int32) for at in range(pieces_key)], axis=0
        )
        base = 1 + pieces_key + step * pieces_query
        seg_query = jnp.concatenate(
            [jnp.full((1, piece), facts_ref[base + at], jnp.int32) for at in range(pieces_query)],
            axis=1,
        )
        finish(jnp.where(seg_key == seg_query, scores, NEGATIVE))


def attend(queries, keys, values, facts, piece):
    heads, depth, count = queries.shape
    keys_len = keys.shape[2]
    lanes = min(512, count)
    chunk = lambda head, step, facts: (head, 0, step)
    whole = lambda head, step, facts: (head, 0, 0)
    return pl.pallas_call(
        functools.partial(attend_kernel, piece),
        grid_spec=pltpu.PrefetchScalarGridSpec(
            num_scalar_prefetch=1,
            grid=(heads, count // lanes),
            in_specs=[
                pl.BlockSpec((1, depth, lanes), chunk),
                pl.BlockSpec((1, depth, keys_len), whole),
                pl.BlockSpec((1, depth, keys_len), whole),
            ],
            out_specs=[
                pl.BlockSpec((1, depth, lanes), chunk),
                pl.BlockSpec((1, keys_len, lanes), chunk),
            ],
        ),
        out_shape=[
            jax.ShapeDtypeStruct((heads, depth, count), BF16),
            jax.ShapeDtypeStruct((heads, keys_len, count), BF16),
        ],
        compiler_params=pltpu.CompilerParams(vmem_limit_bytes=VMEM_LIMIT),
        cost_estimate=pl.CostEstimate(
            flops=4 * count * keys_len * heads * 128,
            bytes_accessed=2 * heads * count * keys_len,
            transcendentals=heads * count * keys_len,
        ),
        name="attend",
    )(facts, queries, keys, values)


def attend_back_kernel(
    q_ref, k_ref, v_ref, out_ref, grad_ref, prob_ref, dq_ref, dk_ref, dv_ref, dk_sum, dv_sum
):
    step = pl.program_id(1)
    grad = grad_ref[0]
    prob = prob_ref[0]
    delta = jnp.sum(grad.astype(F32) * out_ref[0].astype(F32), axis=0, keepdims=True)
    grad_prob = dot(v_ref[0], grad, 0, 0)
    grad_score = (prob.astype(F32) * (grad_prob - delta)).astype(BF16)
    dq_ref[0] = (dot(k_ref[0], grad_score) * FACTOR).astype(BF16)
    dk_part = dot(grad_score, q_ref[0], 1, 1)
    dv_part = dot(prob, grad, 1, 1)

    @pl.when(step == 0)
    def _():
        dk_sum[...] = dk_part
        dv_sum[...] = dv_part

    @pl.when(step != 0)
    def _():
        dk_sum[...] += dk_part
        dv_sum[...] += dv_part

    @pl.when(step == pl.num_programs(1) - 1)
    def _():
        dk_ref[0] = jnp.transpose(dk_sum[...] * FACTOR).astype(BF16)
        dv_ref[0] = jnp.transpose(dv_sum[...]).astype(BF16)


def attend_back(queries, keys, values, attended, grad, prob):
    heads, depth, count = queries.shape
    keys_len = keys.shape[2]
    lanes = min(512, count)
    chunk = lambda head, step: (head, 0, step)
    whole = lambda head, step: (head, 0, 0)
    return pl.pallas_call(
        attend_back_kernel,
        grid=(heads, count // lanes),
        in_specs=[
            pl.BlockSpec((1, depth, lanes), chunk),
            pl.BlockSpec((1, depth, keys_len), whole),
            pl.BlockSpec((1, depth, keys_len), whole),
            pl.BlockSpec((1, depth, lanes), chunk),
            pl.BlockSpec((1, depth, lanes), chunk),
            pl.BlockSpec((1, keys_len, lanes), chunk),
        ],
        out_specs=[
            pl.BlockSpec((1, depth, lanes), chunk),
            pl.BlockSpec((1, depth, keys_len), whole),
            pl.BlockSpec((1, depth, keys_len), whole),
        ],
        out_shape=[
            jax.ShapeDtypeStruct((heads, depth, count), BF16),
            jax.ShapeDtypeStruct((heads, depth, keys_len), BF16),
            jax.ShapeDtypeStruct((heads, depth, keys_len), BF16),
        ],
        scratch_shapes=[pltpu.VMEM((keys_len, depth), F32), pltpu.VMEM((keys_len, depth), F32)],
        compiler_params=pltpu.CompilerParams(vmem_limit_bytes=VMEM_LIMIT),
        cost_estimate=pl.CostEstimate(
            flops=4 * count * keys_len * heads * 128,
            bytes_accessed=2 * heads * count * keys_len,
            transcendentals=0,
        ),
        name="attend_back",
    )(queries, keys, values, attended, grad, prob)


def gelu_pair(inputs):
    square = inputs * inputs
    tanh = jnp.tanh(GELU_COEF * (inputs + 0.044715 * inputs * square))
    value = 0.5 * inputs * (1.0 + tanh)
    slope = 0.5 * (1.0 + tanh) + 0.5 * inputs * (1.0 - tanh * tanh) * (
        GELU_COEF * (1.0 + 3.0 * 0.044715 * square)
    )
    return value, slope


def layer_norm(inputs):
    average = jnp.mean(inputs, axis=-1, keepdims=True)
    centred = inputs - average
    spread = jnp.mean(centred * centred, axis=-1, keepdims=True)
    scale = lax.rsqrt(spread + EPSILON)
    return centred * scale, scale


def layer_norm_back(grad, norm, scale):
    first = jnp.mean(grad, axis=-1, keepdims=True)
    second = jnp.mean(grad * norm, axis=-1, keepdims=True)
    return (grad - first - norm * second) * scale


def shards(
    tokens,
    cotangent,
    lengths,
    cond_index,
    cond_table,
    w_mod,
    b_mod,
    w_qkv,
    b_query,
    b_value,
    w_out,
    b_out,
    w_up,
    b_up,
    w_down,
    b_down,
):
    rows_dev, piece, width = tokens.shape
    dp, band = lax.axis_size("dp"), lax.axis_size("band")
    me, group = lax.axis_index("dp"), lax.axis_index("band")
    images = lengths.shape[1]
    rows = rows_dev * dp
    spans = band // rows
    assert band % rows == 0
    across = band // dp
    unit = width // band
    heads = H // dp
    head_width = width // dp
    mod_width = w_mod.shape[1]
    hidden_width = w_up.shape[1]
    both = ("dp", "band")
    me_turned = reverse_bits(me, dp)

    def target(d, b, turn):
        local = ((b >> log2(dp)) & (rows_dev - 1)) ^ turn
        to_group = (rows_dev * reverse_bits(d, dp) + local) * spans + b // rows
        return reverse_bits(b % dp, dp) * band + to_group

    outward = [
        [(d * band + b, target(d, b, turn)) for d in range(dp) for b in range(band)]
        for turn in range(rows_dev)
    ]
    inward = [[(there, here) for here, there in pairs] for pairs in outward]
    my_slot = (group >> log2(dp)) & (rows_dev - 1)

    def to_groups(local):
        return jnp.stack(
            [
                lax.ppermute(pick(local, my_slot ^ turn), both, outward[turn])
                for turn in range(rows_dev)
            ]
        )

    def from_groups(held):
        came = jnp.stack(
            [lax.ppermute(held[turn], both, inward[turn]) for turn in range(rows_dev)]
        )
        return xor_shuffle(came, my_slot)

    group_row = group >> log2(spans)
    my_local = group_row & (rows_dev - 1)
    order = mask_order(dp)
    places = jnp.arange(dp, dtype=jnp.int32)[:, None]
    turns = jnp.arange(rows_dev, dtype=jnp.int32)[None]
    piece_first = piece * (
        (group & (spans - 1)) * rows + ((my_local ^ turns) * dp) + (me_turned ^ places)
    )

    facts = jnp.concatenate([lengths, cond_index], axis=1)
    facts_own = lax.ppermute(pick(facts, my_slot), both, outward[0])
    tokens_own = to_groups(tokens)
    slot_to = [[(3 * d + slot) % dp for d in range(dp)] for slot in range(3)]
    w_qkv, w_out, w_down = lax.optimization_barrier((w_qkv, w_out, w_down, facts_own))[:3]
    w_slots = [w_qkv.T[slot * head_width : (slot + 1) * head_width] for slot in range(3)]
    stay = [[d == to for d, to in enumerate(target)] for target in slot_to]
    if all(first != last for first, last in zip(stay[0], stay[2], strict=True)):
        keeps_first = functools.reduce(
            jnp.logical_or, [me == d for d in range(dp) if stay[0][d]]
        )
        came = lax.ppermute(
            jnp.where(keeps_first, w_slots[2], w_slots[0]),
            "dp",
            [(d, slot_to[2 if stay[0][d] else 0][d]) for d in range(dp)],
        )
        w_slots = [
            jnp.where(keeps_first, w_slots[0], came),
            lax.ppermute(w_slots[1], "dp", list(enumerate(slot_to[1]))),
            jnp.where(keeps_first, came, w_slots[2]),
        ]
    else:
        w_slots = [
            lax.ppermute(w_slots[slot], "dp", list(enumerate(slot_to[slot]))) for slot in range(3)
        ]
    out_blocks = jnp.stack(jnp.split(w_out.T, dp, axis=1))
    out_parts = exchange(out_blocks, "dp", dp)
    out_parts = jnp.stack([out_parts[reverse_bits(mask, dp)] for mask in range(dp)])
    down_blocks = jnp.stack(jnp.split(after(w_down, tokens_own).T, dp, axis=1))
    w_down_parts = [
        pick(down_blocks, me),
        lax.ppermute(pick(down_blocks, me ^ 1), "dp", xor_perm(dp, 1)),
    ]
    far = dp - 2
    if band % far == 0 and (head_width * far) % band == 0:
        each = band // far
        share = head_width // each
        mask = 2 + lax.div(group, each)
        first = lax.rem(group, each) * share
        sent = lax.dynamic_slice(
            w_down.T,
            (first, (me ^ mask) * hidden_width),
            (share, hidden_width),
            allow_negative_indices=False,
        )
        sent = lax.ppermute(
            sent,
            both,
            [
                (d * band + b, (d ^ (2 + b // each)) * band + b)
                for d in range(dp)
                for b in range(band)
            ],
        )
        w_down_far = lax.all_gather(sent, "band", axis=0, tiled=True)
    else:
        w_down_far = jnp.concatenate(
            [
                lax.ppermute(pick(down_blocks, me ^ mask), "dp", xor_perm(dp, mask))
                for mask in range(2, dp)
            ]
        )

    image_ends = jnp.cumsum(facts_own[:images])
    classes = jnp.arange(cond_table.shape[0], dtype=jnp.int32)

    def conditions(index):
        return dot((index[:, None] == classes[None]).astype(BF16), cond_table)

    silu_own = jax.nn.silu(conditions(facts_own[images:])).astype(BF16)
    mod_part = dot(silu_own, w_mod) + cut(b_mod, me * mod_width, mod_width)
    modulation = gather_stack(mod_part, "dp", dp)
    tokens_all = gather_parts(tokens_own, "dp", dp)
    modulation = xor_shuffle(after(modulation, tokens_all), me)
    tokens_all = tokens_all.reshape((-1,) + tokens_own.shape[1:])
    seg_all = jnp.sum(
        (image_ends[None, None] <= piece_first[..., None]).astype(jnp.int32), axis=-1
    ).reshape(-1)
    image_ids = jnp.arange(images, dtype=jnp.int32)
    hot_all = seg_all[:, None] == image_ids[None]
    mod_all = jnp.sum(jnp.where(hot_all[:, None, :, None], modulation[None], 0.0), axis=2)
    mod_all = mod_all.reshape(-1, 1, 6, width)
    shift_a_all, scale_a_all, gate_b_all = [mod_all[:, :, at] for at in (0, 1, 5)]
    scale_a, gate_a, shift_b, scale_b, gate_b = [
        mod_all[:rows_dev, :, at] for at in (1, 2, 3, 4, 5)
    ]
    own_hot = hot_all[:rows_dev]

    def gather_tokens(own, *waits):
        return gather_parts(own, "dp", dp, *waits).reshape((-1,) + own.shape[1:])

    slot_of = [lax.rem(me + kind * (dp % 3), 3) for kind in range(3)]
    w_heads = jnp.concatenate(
        [
            jnp.where(
                slot_of[kind] == 0,
                w_slots[0],
                jnp.where(slot_of[kind] == 1, w_slots[1], w_slots[2]),
            )
            for kind in range(3)
        ]
    )
    bias_heads = jnp.concatenate(
        [
            cut(b_query, me * head_width, head_width),
            jnp.zeros((head_width,), F32),
            cut(b_value, me * head_width, head_width),
        ]
    )
    norm_all = layer_norm(tokens_all.astype(F32))[0]
    hidden_a_all = (norm_all * (1.0 + scale_a_all) + shift_a_all).astype(BF16).reshape(-1, width)
    norm_low = norm_all.astype(BF16).reshape(-1, width)
    cotangent_own = to_groups(after(cotangent, tokens_own))
    count = hidden_a_all.shape[0]
    half = count // 2
    projected = (dot(w_heads, hidden_a_all, 1, 1) + bias_heads[:, None]).astype(BF16)
    projected = projected.reshape(3, heads, HD, count)
    queries, keys, values = after(projected, cotangent_own)
    cotangent_all = gather_tokens(cotangent_own)
    seg_row = seg_all
    if spans > 1:
        mates = [[at * spans + span for span in range(spans)] for at in range(rows)]
        keys, values, seg_row = [
            lax.all_gather(
                member, "band", axis=member.ndim - 1, tiled=True, axis_index_groups=mates
            )
            for member in (keys, values, seg_row)
        ]
    one_image = jnp.all(seg_row == seg_row[0]).astype(jnp.int32)
    attend_facts = jnp.concatenate([one_image[None], seg_row, seg_all])
    attended, prob_low = attend(queries, keys, values, attend_facts, piece)
    attended = after(attended, cotangent_all).reshape(head_width, count)
    w_out_rows = jnp.concatenate(list(xor_shuffle(out_parts, me)))

    def split_own(partial):
        return partial.astype(BF16).reshape(dp // 2, rows_dev, piece, width)

    def products(product, left):
        return split_own(product(left(half, count))), split_own(product(left(0, half)))

    far_half, near_half = products(
        lambda part: dot(part, w_out_rows, 0, 1), lambda low, high: attended[:, low:high]
    )
    branch = scatter_sum(near_half, far_half, "dp", dp) + b_out
    middle = tokens_own.astype(F32) + gate_a * branch
    norm_b, spread_b = layer_norm(middle)
    hidden_b = (norm_b * (1.0 + scale_b) + shift_b).astype(BF16)
    hidden_b_all = gather_tokens(hidden_b).reshape(count, width)

    grad_mlp_all = (gate_b_all * cotangent_all.astype(F32)).astype(BF16).reshape(count, width)
    grad_output = cotangent_own.astype(F32)
    w_down_rows = jnp.zeros((dp, head_width, hidden_width), BF16)
    w_down_far = after(w_down_far, hidden_b).reshape(far, head_width, hidden_width)
    for mask in range(dp):
        part = w_down_parts[mask] if mask < 2 else w_down_far[mask - 2]
        w_down_rows = lax.dynamic_update_slice(
            w_down_rows, part[None], (me ^ mask, 0, 0), allow_negative_indices=False
        )
    w_down_rows = w_down_rows.reshape(width, hidden_width)
    b_up_own = cut(b_up, me * hidden_width, hidden_width)
    pre_act = dot(hidden_b_all, w_up) + b_up_own
    value, slope = gelu_pair(pre_act)
    activated, slope = lax.optimization_barrier((value.astype(BF16), slope.astype(BF16)))
    grad_act = dot(grad_mlp_all, w_down_rows)
    grad_pre = (grad_act * slope.astype(F32)).astype(BF16)
    far_half, near_half = products(
        lambda part: dot(part, w_up, 1, 1), lambda low, high: grad_pre[low:high]
    )
    grad_hidden_b = scatter_sum(near_half, far_half, "dp", dp)
    stages = log2(band)
    near_first = list(range(stages))
    far_first = [log2(across)] + [at for at in near_first if at != log2(across)]

    def halves(held, axis):
        size = held.shape[axis] // 2
        return [lax.slice_in_dim(held, at * size, (at + 1) * size, axis=axis) for at in range(2)]

    def choose(held, axis, bit):
        upper = ((group >> bit) & 1) == 1
        first, second = halves(held, axis)
        return jnp.where(upper, second, first), jnp.where(upper, first, second)

    def send(part, bit):
        return lax.ppermute(part, "band", xor_perm(band, 1 << bit))

    def joined(mine, came):
        return (mine.astype(F32) + came.astype(F32)).astype(BF16)

    def sum_groups(term, axes, bits, *waits):
        held = term
        for at, (axis, bit) in enumerate(zip(axes, bits, strict=True)):
            mine, far = choose(held, axis, bit)
            came = send(far, bit)
            if at < len(waits):
                came = after(came, *waits[at])
            held = joined(mine, came)
        return held

    def index_of(b, bits):
        return sum(((b >> bit) & 1) << (stages - 1 - at) for at, bit in enumerate(bits))

    def owner_pairs(bits, owner):
        return [
            (d * band + b, owner(d, index_of(b, bits))) for d in range(dp) for b in range(band)
        ]

    def by_rows(d, index):
        return (index // across) * band + across * d + index % across

    rows_then_units = [0] * log2(dp) + [1] * log2(across)
    grad_w_up = dot(hidden_b_all, after(grad_pre, near_half), 0, 0).astype(BF16)
    grad_w_down = dot(grad_mlp_all, after(activated, near_half), 0, 0).astype(BF16)
    up_mine, up_far = choose(grad_w_up, 0, near_first[0])
    down_mine, down_far = choose(grad_w_down, 0, far_first[0])
    up_far, down_far = halves(up_far, 0), halves(down_far, 0)
    up_came = [send(up_far[0], near_first[0])]
    down_came = [send(down_far[0], far_first[0])]
    grad_hidden_b = after(grad_hidden_b, up_came[0], down_came[0])
    up_came.append(send(after(up_far[1], grad_hidden_b), near_first[0]))
    down_came.append(send(after(down_far[1], grad_hidden_b), far_first[0]))

    grad_middle = grad_output + layer_norm_back(grad_hidden_b * (1.0 + scale_b), norm_b, spread_b)
    grad_branch = (gate_a * grad_middle).astype(BF16)
    grad_branch_all = gather_tokens(grad_branch, up_came[1], down_came[1]).reshape(count, width)
    far_mlp, near_mlp = products(
        lambda part: dot(part, w_down_rows, 1, 1),
        lambda low, high: after(activated, grad_branch)[low:high],
    )
    up_mine, up_far = choose(joined(up_mine, jnp.concatenate(up_came)), 0, near_first[1])
    down_mine, down_far = choose(joined(down_mine, jnp.concatenate(down_came)), 0, far_first[1])
    up_came, down_came = send(up_far, near_first[1]), send(down_far, far_first[1])
    grad_attended = dot(w_out_rows, grad_branch_all, 0, 1).astype(BF16)
    final_out = lax.psum_scatter(
        dot(grad_branch_all, attended, 0, 1).astype(BF16), "band", scatter_dimension=0, tiled=True
    )
    grad_q, grad_k, grad_v = attend_back(
        queries,
        keys,
        values,
        attended.reshape(heads, HD, count),
        grad_attended.reshape(heads, HD, count),
        prob_low,
    )
    if spans > 1:
        grad_k, grad_v = [
            lax.psum_scatter(
                member, "band", scatter_dimension=2, tiled=True, axis_index_groups=mates
            )
            for member in (grad_k, grad_v)
        ]
    grad_heads = jnp.concatenate(
        [member.reshape(head_width, count) for member in (grad_q, grad_k, grad_v)]
    )
    mlp_out = scatter_sum(near_mlp, after(far_mlp, grad_branch_all), "dp", dp, grad_heads) + b_down
    grad_heads = after(grad_heads, mlp_out, up_came, down_came)
    up_half, down_half = joined(up_mine, up_came), joined(down_mine, down_came)
    far_half, near_half = products(
        lambda part: dot(part, w_heads, 0, 0), lambda low, high: grad_heads[:, low:high]
    )
    grad_hidden_a = scatter_sum(near_half, far_half, "dp", dp)
    output = from_groups((middle + gate_b * mlp_out).astype(BF16))

    hot_tokens = jnp.broadcast_to(
        hot_all.T.astype(BF16)[:, :, None], (images, hot_all.shape[0], piece)
    ).reshape(images, count)

    def image_sums(near, far):
        return dot(hot_tokens[:, :half], near) + dot(hot_tokens[:, half:], far)

    near_half, far_half = near_half.reshape(half, width), far_half.reshape(half, width)
    grad_shift_a = image_sums(near_half, far_half)
    grad_scale_a = image_sums(near_half * norm_low[:half], far_half * norm_low[half:])

    def own_sums(member):
        pieces = jnp.sum(member, axis=1)
        return jnp.sum(jnp.where(own_hot[:, :, None], pieces[:, None], 0.0), axis=0)

    grad_mod = jnp.concatenate(
        [
            grad_shift_a,
            grad_scale_a,
            own_sums(grad_middle * branch),
            own_sums(grad_hidden_b),
            own_sums(grad_hidden_b * norm_b),
            own_sums(grad_output * mlp_out),
        ],
        axis=1,
    )
    grad_mod = jnp.transpose(grad_mod.reshape(images, dp, mod_width), (1, 0, 2))
    grad_mod_own = scatter_blocks(grad_mod, "dp", dp)
    high = grad_mod_own.astype(BF16)
    low = (grad_mod_own - high.astype(F32)).astype(BF16)
    grad_silu = dot(jnp.concatenate([high, low], axis=0), w_mod, 1, 1)
    grad_silu = grad_silu[:images] + grad_silu[images:]
    ones = jnp.ones((8, count), BF16)
    bias_own = jnp.concatenate(
        [
            jnp.sum(grad_mlp_all[: rows_dev * piece].astype(F32), axis=0),
            jnp.sum(grad_branch.astype(F32), axis=(0, 1)),
            dot(ones, grad_pre)[0],
            dot(ones, grad_heads, 1, 1)[0],
        ]
    )
    inputs = tokens_own.astype(F32)
    norm_a, spread_a = layer_norm(inputs)
    grad_tokens = grad_middle + layer_norm_back(grad_hidden_a * (1.0 + scale_a), norm_a, spread_a)
    grad_tokens = after(grad_tokens.astype(BF16), output)
    packed = jnp.concatenate([grad_mod_own.reshape(-1), grad_silu.reshape(-1), bias_own])
    packed = gather_all(after(packed, grad_tokens), "band", band)
    mod_size, silu_size = images * mod_width, images * width
    grad_mod_groups = packed[:, :mod_size].reshape(band * images, mod_width)
    grad_silu_groups = packed[:, mod_size : mod_size + silu_size].reshape(rows, spans, -1).sum(1)
    bias_sum = jnp.sum(packed[:, mod_size + silu_size :], axis=0)
    final_pack = jnp.concatenate(
        [grad_silu_groups.reshape(-1), jnp.sum(grad_mod_groups, axis=0), bias_sum]
    )
    final_pack = gather_all(final_pack, "dp", dp)

    grad_tokens_sent = grad_tokens
    grad_tokens = from_groups(grad_tokens)

    final_out = after(final_out, final_pack).T.astype(F32)
    final_up = sum_groups(up_half, rows_then_units[2:], near_first[2:], (packed,))
    final_up = lax.ppermute(final_up, both, owner_pairs(near_first, by_rows)).astype(F32)
    final_down = sum_groups(down_half, rows_then_units[2:], far_first[2:], (packed,))
    final_down = lax.ppermute(final_down.T, both, owner_pairs(far_first, by_rows)).astype(F32)
    hidden_a_late = after(hidden_a_all, near_half)
    grad_w_heads = dot(grad_heads, hidden_a_late).astype(BF16).reshape(3, across, unit, width)
    qkv_sum = sum_groups(
        after(grad_w_heads, grad_hidden_a),
        [1] * log2(across) + [3] * log2(dp),
        near_first,
        (packed,),
        (final_pack,),
    )
    qkv_sum = qkv_sum.reshape(3, unit, head_width)
    kind_of = [
        [next(kind for kind in range(3) if (kind * dp + d) % 3 == slot) for slot in range(3)]
        for d in range(dp)
    ]
    kind_now = [
        sum(
            jnp.where(slot_of[kind] == slot, kind, 0).astype(jnp.int32) for kind in range(3)
        )
        for slot in range(3)
    ]
    my_index = index_of(group, near_first)
    my_unit = my_index >> log2(dp)
    final_qkv = []
    for turn in range(3):
        slots = []
        for at in range(across):
            options = {
                slot
                for d in range(dp)
                for slot in range(3)
                if (band * kind_of[d][slot] + across * d + at) % 3 == turn
            }
            assert len(options) == 1
            slots.append(options.pop())

        def owner(d, index, slots=slots, turn=turn):
            at = index // dp
            start = band * kind_of[d][slots[at]] + across * d + at
            assert start % 3 == turn
            return (index % dp) * band + start // 3

        kind = sum(
            jnp.where(my_unit == at, kind_now[slots[at]], 0).astype(jnp.int32)
            for at in range(across)
        )
        final_qkv.append(
            lax.ppermute(pick(qkv_sum, kind), both, owner_pairs(near_first, owner))
        )
    final_qkv = jnp.concatenate(final_qkv).T.astype(F32)

    facts_all = gather_stack(after(facts, hidden_a_all), "dp", dp)
    facts_all = jnp.stack([facts_all[mask] for mask in order])
    index_all = xor_shuffle(facts_all, me_turned).reshape(rows, 2 * images)[:, images:].reshape(-1)
    condition = conditions(after(index_all, grad_branch))
    silu_all = jax.nn.silu(condition).astype(BF16)
    silu_end = rows * silu_size
    grad_silu_rows = jnp.sum(final_pack[:, :silu_end], axis=0).reshape(rows * images, width)
    ends = [silu_end]
    for size in (mod_width, width, width, hidden_width, head_width, head_width, head_width):
        ends.append(ends[-1] + size)
    tail = [final_pack[:, low:high] for low, high in zip(ends[:-1], ends[1:], strict=True)]
    final_b_mod = tail[0].reshape(-1)
    final_b_down = jnp.sum(tail[1], axis=0)
    final_b_out = jnp.sum(tail[2], axis=0)
    final_b_up = tail[3].reshape(-1)
    final_b_query = tail[4].reshape(-1)
    final_b_value = tail[6].reshape(-1)
    sigmoid = jax.nn.sigmoid(condition)
    grad_condition = grad_silu_rows * (sigmoid * (1.0 + condition * (1.0 - sigmoid)))
    table_hot = (
        classes[:, None] == index_all[None]
    ).astype(F32)
    final_table = jnp.dot(table_hot, grad_condition, precision=HIGHEST)
    mod_share = mod_width // across
    grad_mod_share = lax.ppermute(
        cut(grad_mod_groups, (my_index & (across - 1)) * mod_share, mod_share, 1),
        both,
        owner_pairs(near_first, by_rows),
    )
    silu_share = cut(silu_all, me * head_width, head_width, 1).astype(F32)
    silu_share = jnp.repeat(silu_share.reshape(rows, images, -1), spans, axis=0)
    final_mod = lax.dot_general(
        silu_share.reshape(band * images, -1),
        grad_mod_share,
        (((0,), (0,)), ((), ())),
        precision=HIGHEST,
        preferred_element_type=F32,
    )
    return (
        output,
        grad_tokens,
        final_table,
        final_mod,
        final_qkv,
        final_out,
        final_up,
        final_down,
        final_b_mod,
        final_b_query,
        final_b_value,
        final_b_out,
        final_b_up,
        final_b_down,
    )


def solution(mesh):
    rows = P("dp", "band", None)
    split = P(None, "dp")
    spread = P("dp", "band")
    return jax.shard_map(
        shards,
        mesh=mesh,
        in_specs=(
            rows,
            rows,
            P("dp", None),
            P("dp", None),
            P(),
            split,
            P(),
            split,
            P(),
            P(),
            split,
            P(),
            split,
            P(),
            split,
            P(),
        ),
        out_specs=(
            rows,
            rows,
            P(),
            spread,
            spread,
            spread,
            spread,
            P("band", "dp"),
            P(),
            P(),
            P(),
            P(),
            P(),
            P(),
        ),
        check_vma=False,
    )
```

time: 713 us -> 511 us (0.72)
  local copies, waits for them, and re-layouts: 134 us -> 50.3 us
  waiting for transfers between devices: 240 us -> 167 us
  between operations: 54.1 us -> 16.8 us
  matrix products: 75.7 us -> 62.4 us
  Pallas kernels: 40.6 us -> 27.8 us
  starting transfers between devices: 88.1 us -> 99.4 us
  other arithmetic: 71.9 us -> 81.2 us
    reduce_scatter x4 -> x1, waiting for transfers between devices: 69.3 us -> 0.01 us  [shards(): lax.psum_scatter(dot(grad_branch_all, attended, 0, 1).astype(BF16), 'band...]
    dynamic_slice x21 -> x16, local copies, waits for them, and re-layouts: 29.6 us -> 7.01 us  [the longest x5 3.8 us: cut(): lax.dynamic_slice_in_dim(array, start, size, axis, allow_negative_indices...]
    reshape x15 -> x8, local copies, waits for them, and re-layouts: 28 us -> 5.7 us  [the longest x1 1.88 us: shards(): mod_all = mod_all.reshape(-1, 1, 6, width)]
    another operation x21 -> x5, local copies, waits for them, and re-layouts: 21 us -> 5.63 us  [the longest x1 1.91 us: shards(): down_blocks = jnp.stack(jnp.split(after(w_down, tokens_own).T, dp, axis=1))]
    another operation x13 -> x11, other arithmetic: 16.8 us -> 3.51 us  [the longest x5 2.45 us: xor_shuffle(): jnp.stack([pick(array, mask ^ place) for place in range(array.shape[0])])]
    ppermute x47 -> x55, starting transfers between devices: 74.2 us -> 87.1 us  [the longest x11 21.2 us: send(): return lax.ppermute(part, 'band', xor_perm(band, 1 << bit))]
    pallas_call x2, Pallas kernels: 40.6 us -> 27.8 us  [the longest x1 13.9 us: attend(): pl.pallas_call(functools.partial(attend_kernel, piece), grid_spec=pltpu.P...]
    dot_general x21 -> x25, matrix products: 68 us -> 55.4 us  [dot(): lax.dot_general(left, right, (((left_dim,), (right_dim,)), ((), ())), pre...]
  transfers between devices with their start and end apart: 55 -> 61, of which waited for: 26 -> 24; matrix products, arithmetic and copies ran while one was open for 32% -> 32% of each run, Pallas kernels for 4% -> 6%
where the time goes in v2:
time: 511 us; the launch traced here: 505 us
  waiting for transfers between devices  167 us (33%)
  starting transfers between devices  99.4 us (19%)
  other arithmetic  81.2 us (16%)
  matrix products  62.4 us (12%)
  local copies, waits for them, and re-layouts  50.3 us (10%)
  Pallas kernels  27.8 us (5%)
  between operations  16.8 us (3%)
    dot_general x25, matrix products, dot(): lax.dot_general(left, right, (((left_dim,), (right_dim,)), ((), ())), pre...  55.4 us
    ppermute x11, waiting for transfers between devices, send(): return lax.ppermute(part, 'band', xor_perm(band, 1 << bit))  42 us
    ppermute x4, waiting for transfers between devices, scatter_sum(): came = lax.ppermute(held[half:].astype(BF16), axis, xor_perm(count, bit))  39.4 us
    ppermute x8, waiting for transfers between devices, gather_parts(): came = lax.ppermute(held, axis, xor_perm(count, bit))  29.3 us
    ppermute x9, waiting for transfers between devices, gather_stack(): lax.ppermute(held, axis, xor_perm(count, bit))  24.2 us
    ppermute x11, starting transfers between devices, send(): return lax.ppermute(part, 'band', xor_perm(band, 1 << bit))  21.2 us
    ppermute x1, starting transfers between devices, shards(): lax.ppermute(pick(down_blocks, me ^ 1), 'dp', xor_perm(dp, 1))  14.5 us
    ppermute x4, starting transfers between devices, to_groups(): lax.ppermute(pick(local, my_slot ^ turn), both, outward[turn])  13.9 us
  transfers between devices with their start and end apart: 61, of which 24 were waited for; matrix products, arithmetic and copies ran while one was open for 32% of the time, Pallas kernels for 6%

profile of v2, /device:TPU:4, one launch (start us, length us, event | category | flops | bytes accessed | tf_op | source)
XLA Modules:
  0.0 504.7 jit_solution(18194571022852725035)
XLA Ops:
  9.3 3.4 collective-permute-start.2
  16.4 5.6 %collective-permute-start.1 = (bf16[128,1152]{1,0:T(8,128)(2,1)S(1)}, bf16[128,1152]{1,0:T(8,128)(2,1)S(1)}, u32[]{:S(2)}, u32[]{:S(2)}) collective-permute-start(bf16[128,1152]{1,0:T(8,128)(2,1)S(1)} %get-tuple-element.171), channel_id=1, source_target_pairs={{0,1},{1,17},{2,9},{3,25},{4,0},{5,16},{6,8},{7,24},{8,5},{9,21},{... | collective-permute-start | bytes 884744 | tf_op jit(solution)/shard_map/ppermute | solution.py:335
  36.0 5.0 fusion.8
  67.0 4.5 collective-permute-start.10
  76.5 14.5 %collective-permute-start.19 = (bf16[288,1152]{1,0:T(8,128)(2,1)S(1)}, bf16[288,1152]{1,0:T(8,128)(2,1)S(1)}, u32[]{:S(2)}, u32[]{:S(2)}) collective-permute-start(bf16[288,1152]{1,0:T(8,128)(2,1)S(1)} %get-tuple-element.115), channel_id=1, source_target_pairs={{0,8},{8,0},{16,24},{24,16},{1,9},{9,1},{17,25},{25,17},{2,10},{10... | collective-permute-start | bytes 1990664 | tf_op jit(solution)/shard_map/ppermute | solution.py:386
  91.7 5.2 %collective-permute-done.7 = bf16[288,1152]{1,0:T(8,128)(2,1)} collective-permute-done((bf16[288,1152]{1,0:T(8,128)(2,1)}, bf16[288,1152]{1,0:T(8,128)(2,1)}, u32[]{:S(2)}, u32[]{:S(2)}) %collective-permute-start.7) | collective-permute-done | bytes 663584 | tf_op jit(solution)/shard_map/ppermute | solution.py:366
  101.4 8.0 %collective-permute-done.5 = bf16[1,2,128,1152]{3,2,1,0:T(8,128)(2,1)S(1)} collective-permute-done((bf16[1,2,128,1152]{3,2,1,0:T(8,128)(2,1)S(1)}, bf16[1,2,128,1152]{3,2,1,0:T(8,128)(2,1)S(1)}, u32[]{:S(2)}, u32[]{:S(2)}) %collective-permute-start.5) | collective-permute-done | bytes 589856 | tf_op jit(solution)/shard_map/ppermute | solution.py:70
  111.0 10.1 %collective-permute-done.11 = bf16[1,2,128,1152]{3,2,1,0:T(8,128)(2,1)S(1)} collective-permute-done((bf16[1,2,128,1152]{3,2,1,0:T(8,128)(2,1)S(1)}, bf16[1,2,128,1152]{3,2,1,0:T(8,128)(2,1)S(1)}, u32[]{:S(2)}, u32[]{:S(2)}) %collective-permute-start.11) | collective-permute-done | bytes 589856 | tf_op jit(solution)/shard_map/ppermute | solution.py:70
  139.4 13.9 %attend.1 = (bf16[4,72,1024]{2,1,0:T(8,128)(2,1)}, bf16[4,1024,1024]{2,1,0:T(8,128)(2,1)}) custom-call(s32[17]{0:T(128)} %pad_add_fusion.4.facts_ref, bf16[4,72,1024]{2,1,0:T(8,128)(2,1)} %get-tuple-element.129.q_ref, bf16[4,72,1024]{2,1,0:T(8,128)(2,1)} %get-tuple-element.128.k_ref, bf16[4,72,1024]{2,1,0:T(8,128)(2,1)} %get-tuple-element.127.v_ref), custom_call_target="tpu_custom_call" | custom-call | flops 2147483648 | bytes 8388608 | tf_op jit(solution)/shard_map/attend/pallas_call | solution.py:166
  171.4 10.0 %collective-permute-done.16 = bf16[1,2,128,1152]{3,2,1,0:T(8,128)(2,1)} collective-permute-done((bf16[1,2,128,1152]{3,2,1,0:T(8,128)(2,1)}, bf16[1,2,128,1152]{3,2,1,0:T(8,128)(2,1)}, u32[]{:S(2)}, u32[]{:S(2)}) %collective-permute-start.16) | collective-permute-done | bytes 589856 | tf_op jit(solution)/shard_map/ppermute | solution.py:99
  189.5 10.6 %collective-permute-done.17 = bf16[1,2,128,1152]{3,2,1,0:T(8,128)(2,1)} collective-permute-done((bf16[1,2,128,1152]{3,2,1,0:T(8,128)(2,1)}, bf16[1,2,128,1152]{3,2,1,0:T(8,128)(2,1)}, u32[]{:S(2)}, u32[]{:S(2)}) %collective-permute-start.17) | collective-permute-done | bytes 589856 | tf_op jit(solution)/shard_map/ppermute | solution.py:70
  206.0 5.1 %add_convert_fusion = (bf16[1024,1152]{1,0:T(8,128)(2,1)S(1)}, bf16[1024,1152]{1,0:T(8,128)(2,1)S(1)}) fusion(f32[1152]{0:T(1024)S(1)} %copy-done.91, bf16[1024,1152]{1,0:T(8,128)(2,1)S(1)} %bitcast.287, bf16[1152,1152]{1,0:T(8,128)(2,1)S(1)} %copy-done), kind=kOutput, calls=%fused_computation.14 | convolution fusion | flops 2741501952 | bytes 9736704 | tf_op jit(solution)/shard_map/dot_general | solution.py:26
  211.1 4.0 fusion.5
  228.5 13.8 %collective-permute-done.22 = bf16[1,2,128,1152]{3,2,1,0:T(8,128)(2,1)S(1)} collective-permute-done((bf16[1,2,128,1152]{3,2,1,0:T(8,128)(2,1)S(1)}, bf16[1,2,128,1152]{3,2,1,0:T(8,128)(2,1)S(1)}, u32[]{:S(2)}, u32[]{:S(2)}) %collective-permute-start.22) | collective-permute-done | bytes 589856 | tf_op jit(solution)/shard_map/ppermute | solution.py:99
  251.1 3.3 convolution_convert_fusion.5
  258.7 6.2 %collective-permute-done.26 = bf16[288,1152]{1,0:T(8,128)(2,1)S(1)} collective-permute-done((bf16[288,1152]{1,0:T(8,128)(2,1)S(1)}, bf16[288,1152]{1,0:T(8,128)(2,1)S(1)}, u32[]{:S(2)}, u32[]{:S(2)}) %collective-permute-start.26) | collective-permute-done | bytes 663584 | tf_op jit(solution)/shard_map/ppermute | solution.py:538
  268.4 12.0 %collective-permute-done.33 = bf16[288,1152]{1,0:T(8,128)(2,1)S(1)} collective-permute-done((bf16[288,1152]{1,0:T(8,128)(2,1)S(1)}, bf16[288,1152]{1,0:T(8,128)(2,1)S(1)}, u32[]{:S(2)}, u32[]{:S(2)}) %collective-permute-start.33) | collective-permute-done | bytes 663584 | tf_op jit(solution)/shard_map/ppermute | solution.py:538
  294.4 13.9 %attend_back.1 = (bf16[4,72,1024]{2,1,0:T(8,128)(2,1)}, bf16[4,72,1024]{2,1,0:T(8,128)(2,1)}, bf16[4,72,1024]{2,1,0:T(8,128)(2,1)}) custom-call(bf16[4,72,1024]{2,1,0:T(8,128)(2,1)} %get-tuple-element.129.q_ref, bf16[4,72,1024]{2,1,0:T(8,128)(2,1)} %get-tuple-element.128.k_ref, bf16[4,72,1024]{2,1,0:T(8,128)(2,1)} %get-tuple-element.127.v_ref, ...), custom_call_target="tpu_custom_call" | custom-call | flops 2147483648 | bytes 8388608 | tf_op jit(solution)/shard_map/attend_back/pallas_call | solution.py:230
  312.8 3.7 collective-permute-start.32
  325.8 3.7 convolution_convert_fusion.2
  329.5 15.6 %collective-permute-done.36 = bf16[1,2,128,1152]{3,2,1,0:T(8,128)(2,1)S(1)} collective-permute-done((bf16[1,2,128,1152]{3,2,1,0:T(8,128)(2,1)S(1)}, bf16[1,2,128,1152]{3,2,1,0:T(8,128)(2,1)S(1)}, u32[]{:S(2)}, u32[]{:S(2)}) %collective-permute-start.36) | collective-permute-done | bytes 589856 | tf_op jit(solution)/shard_map/ppermute | solution.py:99
  362.7 4.3 collective-permute-start.38
  371.5 10.6 %collective-permute-done.44 = f32[2,15840]{1,0:T(2,128)S(1)} collective-permute-done((f32[2,15840]{1,0:T(2,128)S(1)}, f32[2,15840]{1,0:T(2,128)S(1)}, u32[]{:S(2)}, u32[]{:S(2)}) %collective-permute-start.44) | collective-permute-done | bytes 126752 | tf_op jit(solution)/shard_map/ppermute | solution.py:80
  385.4 10.7 %collective-permute-done.45 = f32[4,15840]{1,0:T(4,128)S(1)} collective-permute-done((f32[4,15840]{1,0:T(4,128)S(1)}, f32[4,15840]{1,0:T(4,128)S(1)}, u32[]{:S(2)}, u32[]{:S(2)}) %collective-permute-start.45) | collective-permute-done | bytes 253472 | tf_op jit(solution)/shard_map/ppermute | solution.py:80
  403.8 5.4 %collective-permute-start.56 = (bf16[288,576]{1,0:T(8,128)(2,1)S(1)}, bf16[288,576]{1,0:T(8,128)(2,1)S(1)}, u32[]{:S(2)}, u32[]{:S(2)}) collective-permute-start(bf16[288,576]{1,0:T(8,128)(2,1)S(1)} %add_convert_fusion.11), channel_id=1, source_target_pairs={{0,0},{1,16},{2,8},{3,24},{4,1},{5,17},{6,9},{7,25},{8,2},{9,18},{... | collective-permute-start | bytes 995336 | tf_op jit(solution)/shard_map/ppermute | solution.py:678
  414.8 11.3 %collective-permute-done.56 = bf16[288,576]{1,0:T(8,128)(2,1)S(1)} collective-permute-done((bf16[288,576]{1,0:T(8,128)(2,1)S(1)}, bf16[288,576]{1,0:T(8,128)(2,1)S(1)}, u32[]{:S(2)}, u32[]{:S(2)}) %collective-permute-start.56) | collective-permute-done | bytes 331808 | tf_op jit(solution)/shard_map/ppermute | solution.py:678
  429.7 12.1 %collective-permute-start.50 = (bf16[3,1,144,576]{3,2,1,0:T(8,128)(2,1)S(1)}, bf16[3,1,144,576]{3,2,1,0:T(8,128)(2,1)}, u32[]{:S(2)}, u32[]{:S(2)}) collective-permute-start(bf16[3,1,144,576]{3,2,1,0:T(8,128)(2,1)S(1)} %broadcast_select_fusion.8), channel_id=1, source_target_pairs={{0,2},{1,3},{2,0},{3,1},{4,6},{5,7},{6,4},{7,5},{8,10},{9,11},{10,... | collective-permute-start | bytes 1493000 | tf_op jit(solution)/shard_map/ppermute | solution.py:538
  443.9 4.3 fusion.32
  448.3 6.3 %collective-permute-done.50 = bf16[3,1,144,576]{3,2,1,0:T(8,128)(2,1)} collective-permute-done((bf16[3,1,144,576]{3,2,1,0:T(8,128)(2,1)S(1)}, bf16[3,1,144,576]{3,2,1,0:T(8,128)(2,1)}, u32[]{:S(2)}, u32[]{:S(2)}) %collective-permute-start.50) | collective-permute-done | bytes 497696 | tf_op jit(solution)/shard_map/ppermute | solution.py:538
  456.9 4.4 collective-permute-start.51
  463.8 13.1 %collective-permute-done.51 = bf16[3,1,144,288]{3,2,1,0:T(8,128)(2,1)} collective-permute-done((bf16[3,1,144,288]{3,2,1,0:T(8,128)(2,1)}, bf16[3,1,144,288]{3,2,1,0:T(8,128)(2,1)}, u32[]{:S(2)}, u32[]{:S(2)}) %collective-permute-start.51) | collective-permute-done | bytes 248864 | tf_op jit(solution)/shard_map/ppermute | solution.py:538
  488.7 6.1 %collective-permute-done.54 = bf16[144,288]{0,1:T(8,128)(2,1)} collective-permute-done((bf16[144,288]{0,1:T(8,128)(2,1)S(1)}, bf16[144,288]{0,1:T(8,128)(2,1)}, u32[]{:S(2)}, u32[]{:S(2)}) %collective-permute-start.54) | collective-permute-done | bytes 82976 | tf_op jit(solution)/shard_map/ppermute | solution.py:727
  (519 shorter events, 227.2 us)
Async XLA Ops:
  7.2 182.3 %all-gather.2.cloned.1.call-start = ((), (), s32[]{:S(2)}) async-start(), calls=%async_computation.1 | async-start | bytes 1492992 | tf_op jit(solution)/shard_map/all_gather | solution.py:409
  9.3 17.8 %collective-permute-start.2 = (s32[8]{0:T(128)}, s32[8]{0:T(128)}, u32[]{:S(2)}, u32[]{:S(2)}) collective-permute-start(s32[8]{0:T(128)} %fusion.72), channel_id=1, source_target_pairs={{0,0},{1,16},{2,8},{3,24},{4,1},{5,17},{6,9},{7,25},{8,4},{9,20},{... | collective-permute-start | bytes 104 | tf_op jit(solution)/shard_map/ppermute | solution.py:356
  14.5 46.1 %collective-permute-start = (bf16[128,1152]{1,0:T(8,128)(2,1)}, bf16[128,1152]{1,0:T(8,128)(2,1)S(1)}, u32[]{:S(2)}, u32[]{:S(2)}) collective-permute-start(bf16[128,1152]{1,0:T(8,128)(2,1)} %get-tuple-element.170), channel_id=1, source_target_pairs={{0,0},{1,16},{2,8},{3,24},{4,1},{5,17},{6,9},{7,25},{8,4},{9,20},{... | collective-permute-start | bytes 884744 | tf_op jit(solution)/shard_map/ppermute | solution.py:335
  16.4 44.2 %collective-permute-start.1 = (bf16[128,1152]{1,0:T(8,128)(2,1)S(1)}, bf16[128,1152]{1,0:T(8,128)(2,1)S(1)}, u32[]{:S(2)}, u32[]{:S(2)}) collective-permute-start(bf16[128,1152]{1,0:T(8,128)(2,1)S(1)} %get-tuple-element.171), channel_id=1, source_target_pairs={{0,1},{1,17},{2,9},{3,25},{4,0},{5,16},{6,8},{7,24},{8,5},{9,21},{... | collective-permute-start | bytes 884744 | tf_op jit(solution)/shard_map/ppermute | solution.py:335
  55.2 41.7 %collective-permute-start.7 = (bf16[288,1152]{1,0:T(8,128)(2,1)}, bf16[288,1152]{1,0:T(8,128)(2,1)}, u32[]{:S(2)}, u32[]{:S(2)}) collective-permute-start(bf16[288,1152]{1,0:T(8,128)(2,1)} %get-tuple-element.125), channel_id=1, source_target_pairs={{0,16},{8,24},{16,0},{24,8},{1,17},{9,25},{17,1},{25,9},{2,18},{10... | collective-permute-start | bytes 1990664 | tf_op jit(solution)/shard_map/ppermute | solution.py:366
  60.5 36.3 %collective-permute-start.8 = (bf16[288,1152]{1,0:T(8,128)(2,1)}, bf16[288,1152]{1,0:T(8,128)(2,1)}, u32[]{:S(2)}, u32[]{:S(2)}) collective-permute-start(bf16[288,1152]{1,0:T(8,128)(2,1)} %get-tuple-element.126), channel_id=1, source_target_pairs={{0,8},{8,0},{16,24},{24,16},{1,9},{9,1},{17,25},{25,17},{2,10},{10... | collective-permute-start | bytes 1990664 | tf_op jit(solution)/shard_map/ppermute | solution.py:373
  60.6 401.4 %reduce-scatter.2.cloned.1.call-start = ((), (), s32[]{:S(2)}) async-start(), calls=%async_computation.2 | async-start | bytes 995328 | tf_op jit(solution)/shard_map/reduce_scatter | solution.py:587
  67.0 24.0 %collective-permute-start.10 = (bf16[128,1152]{1,0:T(8,128)(2,1)S(1)}, bf16[128,1152]{1,0:T(8,128)(2,1)S(1)}, u32[]{:S(2)}, u32[]{:S(2)}) collective-permute-start(bf16[128,1152]{1,0:T(8,128)(2,1)S(1)} %get-tuple-element.167), channel_id=1, source_target_pairs={{0,1},{1,17},{2,9},{3,25},{4,0},{5,16},{6,8},{7,24},{8,5},{9,21},{... | collective-permute-start | bytes 884744 | tf_op jit(solution)/shard_map/ppermute | solution.py:335
  71.5 37.9 %collective-permute-start.5 = (bf16[1,2,128,1152]{3,2,1,0:T(8,128)(2,1)S(1)}, bf16[1,2,128,1152]{3,2,1,0:T(8,128)(2,1)S(1)}, u32[]{:S(2)}, u32[]{:S(2)}) collective-permute-start(bf16[1,2,128,1152]{3,2,1,0:T(8,128)(2,1)S(1)} %pad_maximum_fusion.16), channel_id=1, source_target_pairs={{0,16},{8,24},{16,0},{24,8},{1,17},{9,25},{17,1},{25,9},{2,18},{10... | collective-permute-start | bytes 1769480 | tf_op jit(solution)/shard_map/ppermute | solution.py:70
  76.5 34.4 %collective-permute-start.19 = (bf16[288,1152]{1,0:T(8,128)(2,1)S(1)}, bf16[288,1152]{1,0:T(8,128)(2,1)S(1)}, u32[]{:S(2)}, u32[]{:S(2)}) collective-permute-start(bf16[288,1152]{1,0:T(8,128)(2,1)S(1)} %get-tuple-element.115), channel_id=1, source_target_pairs={{0,8},{8,0},{16,24},{24,16},{1,9},{9,1},{17,25},{25,17},{2,10},{10... | collective-permute-start | bytes 1990664 | tf_op jit(solution)/shard_map/ppermute | solution.py:386
  91.0 18.6 %collective-permute-start.14 = (bf16[2,1,288,288]{3,2,1,0:T(8,128)(2,1)S(1)}, bf16[2,1,288,288]{3,2,1,0:T(8,128)(2,1)S(1)}, u32[]{:S(2)}, u32[]{:S(2)}) collective-permute-start(bf16[2,1,288,288]{3,2,1,0:T(8,128)(2,1)S(1)} %pad_maximum_fusion.21), channel_id=1, source_target_pairs={{0,8},{8,0},{16,24},{24,16},{1,9},{9,1},{17,25},{25,17},{2,10},{10... | collective-permute-start | bytes 995336 | tf_op jit(solution)/shard_map/ppermute | solution.py:110
  96.9 24.2 %collective-permute-start.11 = (bf16[1,2,128,1152]{3,2,1,0:T(8,128)(2,1)S(1)}, bf16[1,2,128,1152]{3,2,1,0:T(8,128)(2,1)S(1)}, u32[]{:S(2)}, u32[]{:S(2)}) collective-permute-start(bf16[1,2,128,1152]{3,2,1,0:T(8,128)(2,1)S(1)} %fusion.78), channel_id=1, source_target_pairs={{0,16},{8,24},{16,0},{24,8},{1,17},{9,25},{17,1},{25,9},{2,18},{10... | collective-permute-start | bytes 1769480 | tf_op jit(solution)/shard_map/ppermute | solution.py:70
  122.3 45.1 %collective-permute-start.12 = (bf16[2,2,128,1152]{3,2,1,0:T(8,128)(2,1)}, bf16[2,2,128,1152]{3,2,1,0:T(8,128)(2,1)}, u32[]{:S(2)}, u32[]{:S(2)}) collective-permute-start(bf16[2,2,128,1152]{3,2,1,0:T(8,128)(2,1)} %pad_maximum_fusion.8), channel_id=1, source_target_pairs={{0,8},{8,0},{16,24},{24,16},{1,9},{9,1},{17,25},{25,17},{2,10},{10... | collective-permute-start | bytes 3538952 | tf_op jit(solution)/shard_map/ppermute | solution.py:70
  135.1 25.5 %collective-permute-start.39 = (s32[1,2,8]{2,1,0:T(2,128)S(1)}, s32[1,2,8]{2,1,0:T(2,128)S(1)}, u32[]{:S(2)}, u32[]{:S(2)}) collective-permute-start(s32[1,2,8]{2,1,0:T(2,128)S(1)} %bitcast.329), channel_id=1, source_target_pairs={{0,8},{8,0},{16,24},{24,16},{1,9},{9,1},{17,25},{25,17},{2,10},{10... | collective-permute-start | bytes 200 | tf_op jit(solution)/shard_map/ppermute | solution.py:80
  222.7 19.7 %collective-permute-start.24 = (bf16[288,1152]{1,0:T(8,128)(2,1)S(1)}, bf16[288,1152]{1,0:T(8,128)(2,1)S(1)}, u32[]{:S(2)}, u32[]{:S(2)}) collective-permute-start(bf16[288,1152]{1,0:T(8,128)(2,1)S(1)} %get-tuple-element.131), channel_id=1, source_target_pairs={{0,2},{1,3},{2,0},{3,1},{4,6},{5,7},{6,4},{7,5},{8,10},{9,11},{10,... | collective-permute-start | bytes 1990664 | tf_op jit(solution)/shard_map/ppermute | solution.py:538
  247.6 19.3 %collective-permute-start.25 = (bf16[1,2,128,1152]{3,2,1,0:T(8,128)(2,1)S(1)}, bf16[1,2,128,1152]{3,2,1,0:T(8,128)(2,1)S(1)}, u32[]{:S(2)}, u32[]{:S(2)}) collective-permute-start(bf16[1,2,128,1152]{3,2,1,0:T(8,128)(2,1)S(1)} %bitcast.270), channel_id=1, source_target_pairs={{0,16},{8,24},{16,0},{24,8},{1,17},{9,25},{17,1},{25,9},{2,18},{10... | collective-permute-start | bytes 1769480 | tf_op jit(solution)/shard_map/ppermute | solution.py:70
  249.4 17.6 %collective-permute-start.27 = (bf16[288,1152]{1,0:T(8,128)(2,1)S(1)}, bf16[288,1152]{1,0:T(8,128)(2,1)S(1)}, u32[]{:S(2)}, u32[]{:S(2)}) collective-permute-start(bf16[288,1152]{1,0:T(8,128)(2,1)S(1)} %get-tuple-element.66), channel_id=1, source_target_pairs={{0,2},{1,3},{2,0},{3,1},{4,6},{5,7},{6,4},{7,5},{8,10},{9,11},{10,... | collective-permute-start | bytes 1990664 | tf_op jit(solution)/shard_map/ppermute | solution.py:538
  267.7 17.4 %collective-permute-start.34 = (bf16[288,1152]{1,0:T(8,128)(2,1)S(1)}, bf16[288,1152]{1,0:T(8,128)(2,1)S(1)}, u32[]{:S(2)}, u32[]{:S(2)}) collective-permute-start(bf16[288,1152]{1,0:T(8,128)(2,1)S(1)} %broadcast_select_fusion.3), channel_id=1, source_target_pairs={{0,1},{1,0},{2,3},{3,2},{4,5},{5,4},{6,7},{7,6},{8,9},{9,8},{10,11... | collective-permute-start | bytes 1990664 | tf_op jit(solution)/shard_map/ppermute | solution.py:538
  282.5 116.4 %collective-permute-start.55 = (bf16[288,576]{1,0:T(8,128)(2,1)}, bf16[288,576]{1,0:T(8,128)(2,1)}, u32[]{:S(2)}, u32[]{:S(2)}) collective-permute-start(bf16[288,576]{1,0:T(8,128)(2,1)} %broadcast_select_fusion.10), channel_id=1, source_target_pairs={{0,4},{1,5},{2,6},{3,7},{4,0},{5,1},{6,2},{7,3},{8,12},{9,13},{10,... | collective-permute-start | bytes 995336 | tf_op jit(solution)/shard_map/ppermute | solution.py:538
  287.2 110.4 %collective-permute-start.57 = (bf16[288,576]{1,0:T(8,128)(2,1)}, bf16[288,576]{1,0:T(8,128)(2,1)}, u32[]{:S(2)}, u32[]{:S(2)}) collective-permute-start(bf16[288,576]{1,0:T(8,128)(2,1)} %broadcast_select_fusion.9), channel_id=1, source_target_pairs={{0,4},{1,5},{2,6},{3,7},{4,0},{5,1},{6,2},{7,3},{8,12},{9,13},{10,... | collective-permute-start | bytes 995336 | tf_op jit(solution)/shard_map/ppermute | solution.py:538
  291.7 18.2 %collective-permute-start.30 = (bf16[1,2,128,1152]{3,2,1,0:T(8,128)(2,1)S(1)}, bf16[1,2,128,1152]{3,2,1,0:T(8,128)(2,1)}, u32[]{:S(2)}, u32[]{:S(2)}) collective-permute-start(bf16[1,2,128,1152]{3,2,1,0:T(8,128)(2,1)S(1)} %slice.589), channel_id=1, source_target_pairs={{0,16},{8,24},{16,0},{24,8},{1,17},{9,25},{17,1},{25,9},{2,18},{10... | collective-permute-start | bytes 1769480 | tf_op jit(solution)/shard_map/ppermute | solution.py:99
  312.8 39.6 %collective-permute-start.32 = (bf16[128,1152]{1,0:T(8,128)(2,1)}, bf16[128,1152]{1,0:T(8,128)(2,1)S(1)}, u32[]{:S(2)}, u32[]{:S(2)}) collective-permute-start(bf16[128,1152]{1,0:T(8,128)(2,1)} %get-tuple-element.164), channel_id=1, source_target_pairs={{1,0},{17,1},{9,2},{25,3},{0,4},{16,5},{8,6},{24,7},{5,8},{21,9},{... | collective-permute-start | bytes 884744 | tf_op jit(solution)/shard_map/ppermute | solution.py:342
  316.4 35.9 %collective-permute-start.31 = (bf16[128,1152]{1,0:T(8,128)(2,1)S(1)}, bf16[128,1152]{1,0:T(8,128)(2,1)}, u32[]{:S(2)}, u32[]{:S(2)}) collective-permute-start(bf16[128,1152]{1,0:T(8,128)(2,1)S(1)} %get-tuple-element.165), channel_id=1, source_target_pairs={{0,0},{16,1},{8,2},{24,3},{1,4},{17,5},{9,6},{25,7},{4,8},{20,9},{... | collective-permute-start | bytes 884744 | tf_op jit(solution)/shard_map/ppermute | solution.py:342
  323.9 21.2 %collective-permute-start.36 = (bf16[1,2,128,1152]{3,2,1,0:T(8,128)(2,1)S(1)}, bf16[1,2,128,1152]{3,2,1,0:T(8,128)(2,1)S(1)}, u32[]{:S(2)}, u32[]{:S(2)}) collective-permute-start(bf16[1,2,128,1152]{3,2,1,0:T(8,128)(2,1)S(1)} %slice.588), channel_id=1, source_target_pairs={{0,16},{8,24},{16,0},{24,8},{1,17},{9,25},{17,1},{25,9},{2,18},{10... | collective-permute-start | bytes 1769480 | tf_op jit(solution)/shard_map/ppermute | solution.py:99
  362.7 19.6 %collective-permute-start.38 = (bf16[128,1152]{1,0:T(8,128)(2,1)S(1)}, bf16[128,1152]{1,0:T(8,128)(2,1)S(1)}, u32[]{:S(2)}, u32[]{:S(2)}) collective-permute-start(bf16[128,1152]{1,0:T(8,128)(2,1)S(1)} %get-tuple-element.159), channel_id=1, source_target_pairs={{1,0},{17,1},{9,2},{25,3},{0,4},{16,5},{8,6},{24,7},{5,8},{21,9},{... | collective-permute-start | bytes 884744 | tf_op jit(solution)/shard_map/ppermute | solution.py:342
  367.0 17.2 %collective-permute-start.37 = (bf16[128,1152]{1,0:T(8,128)(2,1)S(1)}, bf16[128,1152]{1,0:T(8,128)(2,1)S(1)}, u32[]{:S(2)}, u32[]{:S(2)}) collective-permute-start(bf16[128,1152]{1,0:T(8,128)(2,1)S(1)} %get-tuple-element.160), channel_id=1, source_target_pairs={{0,0},{16,1},{8,2},{24,3},{1,4},{17,5},{9,6},{25,7},{4,8},{20,9},{... | collective-permute-start | bytes 884744 | tf_op jit(solution)/shard_map/ppermute | solution.py:342
  382.1 45.9 %collective-permute-start.49 = (bf16[3,1,144,1152]{3,2,1,0:T(8,128)(2,1)}, bf16[3,1,144,1152]{3,2,1,0:T(8,128)(2,1)}, u32[]{:S(2)}, u32[]{:S(2)}) collective-permute-start(bf16[3,1,144,1152]{3,2,1,0:T(8,128)(2,1)} %broadcast_select_fusion.2), channel_id=1, source_target_pairs={{0,1},{1,0},{2,3},{3,2},{4,5},{5,4},{6,7},{7,6},{8,9},{9,8},{10,11... | collective-permute-start | bytes 2985992 | tf_op jit(solution)/shard_map/ppermute | solution.py:538
  403.8 22.2 %collective-permute-start.56 = (bf16[288,576]{1,0:T(8,128)(2,1)S(1)}, bf16[288,576]{1,0:T(8,128)(2,1)S(1)}, u32[]{:S(2)}, u32[]{:S(2)}) collective-permute-start(bf16[288,576]{1,0:T(8,128)(2,1)S(1)} %add_convert_fusion.11), channel_id=1, source_target_pairs={{0,0},{1,16},{2,8},{3,24},{4,1},{5,17},{6,9},{7,25},{8,2},{9,18},{... | collective-permute-start | bytes 995336 | tf_op jit(solution)/shard_map/ppermute | solution.py:678
  409.3 17.7 %collective-permute-start.58 = (bf16[576,288]{0,1:T(8,128)(2,1)S(1)}, bf16[576,288]{0,1:T(8,128)(2,1)S(1)}, u32[]{:S(2)}, u32[]{:S(2)}) collective-permute-start(bf16[576,288]{0,1:T(8,128)(2,1)S(1)} %fusion.33), channel_id=1, source_target_pairs={{0,0},{1,8},{2,16},{3,24},{4,1},{5,9},{6,17},{7,25},{8,2},{9,10},{... | collective-permute-start | bytes 995336 | tf_op jit(solution)/shard_map/ppermute | solution.py:680
  414.7 27.2 %collective-permute-start.47 = (f32[2,42912]{1,0:T(2,128)S(1)}, f32[2,42912]{1,0:T(2,128)S(1)}, u32[]{:S(2)}, u32[]{:S(2)}) collective-permute-start(f32[2,42912]{1,0:T(2,128)S(1)} %pad_maximum_fusion.22), channel_id=1, source_target_pairs={{0,16},{8,24},{16,0},{24,8},{1,17},{9,25},{17,1},{25,9},{2,18},{10... | collective-permute-start | bytes 1029896 | tf_op jit(solution)/shard_map/ppermute | solution.py:80
  429.7 24.8 %collective-permute-start.50 = (bf16[3,1,144,576]{3,2,1,0:T(8,128)(2,1)S(1)}, bf16[3,1,144,576]{3,2,1,0:T(8,128)(2,1)}, u32[]{:S(2)}, u32[]{:S(2)}) collective-permute-start(bf16[3,1,144,576]{3,2,1,0:T(8,128)(2,1)S(1)} %broadcast_select_fusion.8), channel_id=1, source_target_pairs={{0,2},{1,3},{2,0},{3,1},{4,6},{5,7},{6,4},{7,5},{8,10},{9,11},{10,... | collective-permute-start | bytes 1493000 | tf_op jit(solution)/shard_map/ppermute | solution.py:538
  456.9 20.0 %collective-permute-start.51 = (bf16[3,1,144,288]{3,2,1,0:T(8,128)(2,1)}, bf16[3,1,144,288]{3,2,1,0:T(8,128)(2,1)}, u32[]{:S(2)}, u32[]{:S(2)}) collective-permute-start(bf16[3,1,144,288]{3,2,1,0:T(8,128)(2,1)} %broadcast_select_fusion.11), channel_id=1, source_target_pairs={{0,4},{1,5},{2,6},{3,7},{4,0},{5,1},{6,2},{7,3},{8,12},{9,13},{10,... | collective-permute-start | bytes 746504 | tf_op jit(solution)/shard_map/ppermute | solution.py:538
  (127 other events, 1217.4 us)
Sparse Core Ops, SparseCore 0:
  60.7 49.1 all-gather.1
  290.0 72.1 reduce-scatter.1

commit v3 on v2

--- a/solution.py
+++ b/solution.py
@@ -60,6 +60,10 @@
     return jnp.stack([pick(array, mask ^ place) for place in range(array.shape[0])])
 
 
+def together(*arrays):
+    return lax.optimization_barrier(arrays)
+
+
 def after(array, *others):
     return lax.optimization_barrier((array, *others))[0]
 
@@ -74,15 +78,16 @@
     return held
 
 
-def gather_stack(part, axis, count):
-    held = part[None]
-    for bit in bits_up(count):
-        held = jnp.concatenate([held, lax.ppermute(held, axis, xor_perm(count, bit))], axis=0)
-    return held
-
-
-def gather_all(part, axis, count):
-    return xor_shuffle(gather_stack(part, axis, count), lax.axis_index(axis))
+def gather_stack(part, axis, count, bits=None):
+    held, order = part[None], [0]
+    for bit in bits or reversed(bits_up(count)):
+        held = jnp.concatenate([held, lax.ppermute(held, axis, xor_perm(count, bit))])
+        order = order + [mask ^ bit for mask in order]
+    return jnp.stack([held[order.index(mask)] for mask in range(count)])
+
+
+def gather_all(part, axis, count, bits=None):
+    return xor_shuffle(gather_stack(part, axis, count, bits), lax.axis_index(axis))
 
 
 def mask_order(count):
@@ -92,8 +97,11 @@
     return order
 
 
-def scatter_sum(near, far, axis, count, *waits):
-    held = near.astype(F32) + lax.ppermute(far, axis, xor_perm(count, 1)).astype(F32)
+def scatter_first(near, far, axis, count):
+    return near.astype(F32) + lax.ppermute(far, axis, xor_perm(count, 1)).astype(F32)
+
+
+def scatter_rest(held, axis, count, *waits):
     for bit in bits_up(count)[1:]:
         half = held.shape[0] // 2
         came = lax.ppermute(held[half:].astype(BF16), axis, xor_perm(count, bit))
@@ -101,6 +109,10 @@
             came = after(came, *waits)
         held = held[:half] + came.astype(F32)
     return held[0]
+
+
+def scatter_sum(near, far, axis, count, *waits):
+    return scatter_rest(scatter_first(near, far, axis, count), axis, count, *waits)
 
 
 def exchange(parts, axis, count):
@@ -184,7 +196,7 @@
         ],
         compiler_params=pltpu.CompilerParams(vmem_limit_bytes=VMEM_LIMIT),
         cost_estimate=pl.CostEstimate(
-            flops=4 * count * keys_len * heads * 128,
+            flops=30 * count * keys_len * heads * 128,
             bytes_accessed=2 * heads * count * keys_len,
             transcendentals=heads * count * keys_len,
         ),
@@ -251,7 +263,7 @@
         scratch_shapes=[pltpu.VMEM((keys_len, depth), F32), pltpu.VMEM((keys_len, depth), F32)],
         compiler_params=pltpu.CompilerParams(vmem_limit_bytes=VMEM_LIMIT),
         cost_estimate=pl.CostEstimate(
-            flops=4 * count * keys_len * heads * 128,
+            flops=30 * count * keys_len * heads * 128,
             bytes_accessed=2 * heads * count * keys_len,
             transcendentals=0,
         ),
@@ -354,17 +366,21 @@
 
     facts = jnp.concatenate([lengths, cond_index], axis=1)
     facts_own = lax.ppermute(pick(facts, my_slot), both, outward[0])
-    tokens_own = to_groups(tokens)
+    tokens_sent = [pick(tokens, my_slot ^ turn) for turn in range(rows_dev)]
+    tokens_own = jnp.stack(
+        [lax.ppermute(part, both, outward[turn]) for turn, part in enumerate(tokens_sent)]
+    )
     slot_to = [[(3 * d + slot) % dp for d in range(dp)] for slot in range(3)]
-    w_qkv, w_out, w_down = lax.optimization_barrier((w_qkv, w_out, w_down, facts_own))[:3]
+    w_qkv = after(w_qkv, tokens_sent)
     w_slots = [w_qkv.T[slot * head_width : (slot + 1) * head_width] for slot in range(3)]
     stay = [[d == to for d, to in enumerate(target)] for target in slot_to]
     if all(first != last for first, last in zip(stay[0], stay[2], strict=True)):
         keeps_first = functools.reduce(
             jnp.logical_or, [me == d for d in range(dp) if stay[0][d]]
         )
+        slots_sent = jnp.where(keeps_first, w_slots[2], w_slots[0])
         came = lax.ppermute(
-            jnp.where(keeps_first, w_slots[2], w_slots[0]),
+            slots_sent,
             "dp",
             [(d, slot_to[2 if stay[0][d] else 0][d]) for d in range(dp)],
         )
@@ -374,46 +390,13 @@
             jnp.where(keeps_first, came, w_slots[2]),
         ]
     else:
+        slots_sent = w_slots[0]
         w_slots = [
             lax.ppermute(w_slots[slot], "dp", list(enumerate(slot_to[slot]))) for slot in range(3)
         ]
-    out_blocks = jnp.stack(jnp.split(w_out.T, dp, axis=1))
-    out_parts = exchange(out_blocks, "dp", dp)
-    out_parts = jnp.stack([out_parts[reverse_bits(mask, dp)] for mask in range(dp)])
-    down_blocks = jnp.stack(jnp.split(after(w_down, tokens_own).T, dp, axis=1))
-    w_down_parts = [
-        pick(down_blocks, me),
-        lax.ppermute(pick(down_blocks, me ^ 1), "dp", xor_perm(dp, 1)),
-    ]
-    far = dp - 2
-    if band % far == 0 and (head_width * far) % band == 0:
-        each = band // far
-        share = head_width // each
-        mask = 2 + lax.div(group, each)
-        first = lax.rem(group, each) * share
-        sent = lax.dynamic_slice(
-            w_down.T,
-            (first, (me ^ mask) * hidden_width),
-            (share, hidden_width),
-            allow_negative_indices=False,
-        )
-        sent = lax.ppermute(
-            sent,
-            both,
-            [
-                (d * band + b, (d ^ (2 + b // each)) * band + b)
-                for d in range(dp)
-                for b in range(band)
-            ],
-        )
-        w_down_far = lax.all_gather(sent, "band", axis=0, tiled=True)
-    else:
-        w_down_far = jnp.concatenate(
-            [
-                lax.ppermute(pick(down_blocks, me ^ mask), "dp", xor_perm(dp, mask))
-                for mask in range(2, dp)
-            ]
-        )
+    row_blocks = jnp.concatenate(
+        [jnp.stack(jnp.split(member.T, dp, axis=1)) for member in (w_down, w_out)], axis=2
+    )
 
     image_ends = jnp.cumsum(facts_own[:images])
     classes = jnp.arange(cond_table.shape[0], dtype=jnp.int32)
@@ -422,27 +405,29 @@
         return dot((index[:, None] == classes[None]).astype(BF16), cond_table)
 
     silu_own = jax.nn.silu(conditions(facts_own[images:])).astype(BF16)
-    mod_part = dot(silu_own, w_mod) + cut(b_mod, me * mod_width, mod_width)
+    mod_part = dot(after(silu_own, slots_sent), w_mod) + cut(b_mod, me * mod_width, mod_width)
     modulation = gather_stack(mod_part, "dp", dp)
-    tokens_all = gather_parts(tokens_own, "dp", dp)
-    modulation = xor_shuffle(after(modulation, tokens_all), me)
-    tokens_all = tokens_all.reshape((-1,) + tokens_own.shape[1:])
+    tokens_own, w_slots, modulation = together(tokens_own, w_slots, modulation)
+    modulation = xor_shuffle(modulation, me)
     seg_all = jnp.sum(
         (image_ends[None, None] <= piece_first[..., None]).astype(jnp.int32), axis=-1
     ).reshape(-1)
     image_ids = jnp.arange(images, dtype=jnp.int32)
     hot_all = seg_all[:, None] == image_ids[None]
-    mod_all = jnp.sum(jnp.where(hot_all[:, None, :, None], modulation[None], 0.0), axis=2)
-    mod_all = mod_all.reshape(-1, 1, 6, width)
-    shift_a_all, scale_a_all, gate_b_all = [mod_all[:, :, at] for at in (0, 1, 5)]
+    modulation = jnp.transpose(modulation, (1, 0, 2)).reshape(images, 6 * width)
+    mod_all = jnp.dot(hot_all.astype(F32), modulation, precision=HIGHEST)
+    mod_all = [part[:, None] for part in jnp.split(mod_all, 6, axis=1)]
+    shift_a_all, scale_a_all, gate_b_all = [mod_all[at] for at in (0, 1, 5)]
     scale_a, gate_a, shift_b, scale_b, gate_b = [
-        mod_all[:rows_dev, :, at] for at in (1, 2, 3, 4, 5)
+        mod_all[at][:rows_dev] for at in (1, 2, 3, 4, 5)
     ]
     own_hot = hot_all[:rows_dev]
 
     def gather_tokens(own, *waits):
         return gather_parts(own, "dp", dp, *waits).reshape((-1,) + own.shape[1:])
 
+    tokens_all = gather_tokens(tokens_own)
+    cotangent, row_blocks, _ = together(cotangent, row_blocks, tokens_own)
     slot_of = [lax.rem(me + kind * (dp % 3), 3) for kind in range(3)]
     w_heads = jnp.concatenate(
         [
@@ -464,13 +449,16 @@
     norm_all = layer_norm(tokens_all.astype(F32))[0]
     hidden_a_all = (norm_all * (1.0 + scale_a_all) + shift_a_all).astype(BF16).reshape(-1, width)
     norm_low = norm_all.astype(BF16).reshape(-1, width)
-    cotangent_own = to_groups(after(cotangent, tokens_own))
+    cotangent_own = to_groups(cotangent)
     count = hidden_a_all.shape[0]
     half = count // 2
+    row_parts = {
+        2: lax.ppermute(after(pick(row_blocks, me ^ 2), tokens_all), "dp", xor_perm(dp, 2))
+    }
     projected = (dot(w_heads, hidden_a_all, 1, 1) + bias_heads[:, None]).astype(BF16)
+    projected, row_parts = together(projected, row_parts)
     projected = projected.reshape(3, heads, HD, count)
-    queries, keys, values = after(projected, cotangent_own)
-    cotangent_all = gather_tokens(cotangent_own)
+    queries, keys, values = projected[0], projected[1], projected[2]
     seg_row = seg_all
     if spans > 1:
         mates = [[at * spans + span for span in range(spans)] for at in range(rows)]
@@ -483,8 +471,17 @@
     one_image = jnp.all(seg_row == seg_row[0]).astype(jnp.int32)
     attend_facts = jnp.concatenate([one_image[None], seg_row, seg_all])
     attended, prob_low = attend(queries, keys, values, attend_facts, piece)
-    attended = after(attended, cotangent_all).reshape(head_width, count)
-    w_out_rows = jnp.concatenate(list(xor_shuffle(out_parts, me)))
+    row_blocks = after(row_blocks, projected)
+    row_parts[0] = pick(row_blocks, me)
+    for mask in range(1, dp):
+        if mask != 2:
+            row_parts[mask] = lax.ppermute(
+                pick(row_blocks, me ^ mask), "dp", xor_perm(dp, mask)
+            )
+    attended, cotangent_own, row_parts = together(attended, cotangent_own, row_parts)
+    attended = attended.reshape(head_width, count)
+    row_parts = jnp.stack([row_parts[mask] for mask in range(dp)])
+    w_out_rows = jnp.concatenate(list(xor_shuffle(row_parts[:, :, hidden_width:], me)))
 
     def split_own(partial):
         return partial.astype(BF16).reshape(dp // 2, rows_dev, piece, width)
@@ -499,38 +496,45 @@
     middle = tokens_own.astype(F32) + gate_a * branch
     norm_b, spread_b = layer_norm(middle)
     hidden_b = (norm_b * (1.0 + scale_b) + shift_b).astype(BF16)
+    row_parts, _ = together(row_parts, far_half)
+    w_down_rows = jnp.concatenate(list(xor_shuffle(row_parts[:, :, :hidden_width], me)))
     hidden_b_all = gather_tokens(hidden_b).reshape(count, width)
 
-    grad_mlp_all = (gate_b_all * cotangent_all.astype(F32)).astype(BF16).reshape(count, width)
+    cotangent_all = gather_tokens(after(cotangent_own, hidden_b_all))
     grad_output = cotangent_own.astype(F32)
-    w_down_rows = jnp.zeros((dp, head_width, hidden_width), BF16)
-    w_down_far = after(w_down_far, hidden_b).reshape(far, head_width, hidden_width)
-    for mask in range(dp):
-        part = w_down_parts[mask] if mask < 2 else w_down_far[mask - 2]
-        w_down_rows = lax.dynamic_update_slice(
-            w_down_rows, part[None], (me ^ mask, 0, 0), allow_negative_indices=False
-        )
-    w_down_rows = w_down_rows.reshape(width, hidden_width)
     b_up_own = cut(b_up, me * hidden_width, hidden_width)
     pre_act = dot(hidden_b_all, w_up) + b_up_own
     value, slope = gelu_pair(pre_act)
     activated, slope = lax.optimization_barrier((value.astype(BF16), slope.astype(BF16)))
+    far_mlp, near_mlp = products(
+        lambda part: dot(part, w_down_rows, 1, 1), lambda low, high: activated[low:high]
+    )
+    mlp_out = scatter_first(near_mlp, far_mlp, "dp", dp)
+    cotangent_all, mlp_out = together(cotangent_all, mlp_out)
+    grad_mlp_all = (gate_b_all * cotangent_all.astype(F32)).astype(BF16).reshape(count, width)
+    mlp_out = scatter_rest(mlp_out, "dp", dp) + b_down
     grad_act = dot(grad_mlp_all, w_down_rows)
     grad_pre = (grad_act * slope.astype(F32)).astype(BF16)
     far_half, near_half = products(
         lambda part: dot(part, w_up, 1, 1), lambda low, high: grad_pre[low:high]
     )
-    grad_hidden_b = scatter_sum(near_half, far_half, "dp", dp)
+    grad_hidden_b = scatter_first(near_half, far_half, "dp", dp)
+    mlp_out, grad_hidden_b, near_half, grad_pre, activated = together(
+        mlp_out, grad_hidden_b, near_half, grad_pre, activated
+    )
+    grad_hidden_b = scatter_rest(grad_hidden_b, "dp", dp)
     stages = log2(band)
     near_first = list(range(stages))
-    far_first = [log2(across)] + [at for at in near_first if at != log2(across)]
 
     def halves(held, axis):
         size = held.shape[axis] // 2
         return [lax.slice_in_dim(held, at * size, (at + 1) * size, axis=axis) for at in range(2)]
 
-    def choose(held, axis, bit):
-        upper = ((group >> bit) & 1) == 1
+    def choose(held, axis, bit, plain=False):
+        upper = (group >> bit) & 1
+        if bit >= log2(across) and not plain:
+            upper = upper ^ ((me >> (bit - log2(across))) & 1)
+        upper = upper == 1
         first, second = halves(held, axis)
         return jnp.where(upper, second, first), jnp.where(upper, first, second)
 
@@ -540,53 +544,52 @@
     def joined(mine, came):
         return (mine.astype(F32) + came.astype(F32)).astype(BF16)
 
-    def sum_groups(term, axes, bits, *waits):
+    def sum_groups(term, axes, bits, plain=False):
         held = term
-        for at, (axis, bit) in enumerate(zip(axes, bits, strict=True)):
-            mine, far = choose(held, axis, bit)
-            came = send(far, bit)
-            if at < len(waits):
-                came = after(came, *waits[at])
-            held = joined(mine, came)
+        for axis, bit in zip(axes, bits, strict=True):
+            mine, far = choose(held, axis, bit, plain)
+            held = joined(mine, send(far, bit))
         return held
 
-    def index_of(b, bits):
-        return sum(((b >> bit) & 1) << (stages - 1 - at) for at, bit in enumerate(bits))
-
-    def owner_pairs(bits, owner):
+    def piece_at(d, b):
+        return reverse_bits((b // across) ^ d, dp), reverse_bits(b % across, across)
+
+    def owner_pairs(owner):
         return [
-            (d * band + b, owner(d, index_of(b, bits))) for d in range(dp) for b in range(band)
+            (d * band + b, owner(d, b, *piece_at(d, b))) for d in range(dp) for b in range(band)
         ]
 
-    def by_rows(d, index):
-        return (index // across) * band + across * d + index % across
-
-    rows_then_units = [0] * log2(dp) + [1] * log2(across)
-    grad_w_up = dot(hidden_b_all, after(grad_pre, near_half), 0, 0).astype(BF16)
-    grad_w_down = dot(grad_mlp_all, after(activated, near_half), 0, 0).astype(BF16)
-    up_mine, up_far = choose(grad_w_up, 0, near_first[0])
-    down_mine, down_far = choose(grad_w_down, 0, far_first[0])
+    near_bits, far_bits = near_first[: log2(across)], near_first[log2(across) :]
+    first_far = far_bits[0]
+    grad_w_up = dot(hidden_b_all, grad_pre, 0, 0).astype(BF16)
+    grad_w_down = dot(grad_mlp_all, activated, 0, 0).astype(BF16)
+    up_mine, up_far = choose(grad_w_up, 1, near_bits[0])
+    down_mine, down_far = choose(grad_w_down, 0, first_far)
     up_far, down_far = halves(up_far, 0), halves(down_far, 0)
-    up_came = [send(up_far[0], near_first[0])]
-    down_came = [send(down_far[0], far_first[0])]
+    up_came = [send(up_far[0], near_bits[0])]
+    down_came = [send(down_far[0], first_far)]
     grad_hidden_b = after(grad_hidden_b, up_came[0], down_came[0])
-    up_came.append(send(after(up_far[1], grad_hidden_b), near_first[0]))
-    down_came.append(send(after(down_far[1], grad_hidden_b), far_first[0]))
+    up_came.append(send(after(up_far[1], grad_hidden_b), near_bits[0]))
+    down_came.append(send(after(down_far[1], grad_hidden_b), first_far))
 
     grad_middle = grad_output + layer_norm_back(grad_hidden_b * (1.0 + scale_b), norm_b, spread_b)
     grad_branch = (gate_a * grad_middle).astype(BF16)
     grad_branch_all = gather_tokens(grad_branch, up_came[1], down_came[1]).reshape(count, width)
-    far_mlp, near_mlp = products(
-        lambda part: dot(part, w_down_rows, 1, 1),
-        lambda low, high: after(activated, grad_branch)[low:high],
-    )
-    up_mine, up_far = choose(joined(up_mine, jnp.concatenate(up_came)), 0, near_first[1])
-    down_mine, down_far = choose(joined(down_mine, jnp.concatenate(down_came)), 0, far_first[1])
-    up_came, down_came = send(up_far, near_first[1]), send(down_far, far_first[1])
+    middle, mlp_out, _ = together(middle, mlp_out, grad_branch)
+    output = (middle + gate_b * mlp_out).astype(BF16)
+    up_mine, up_far = choose(joined(up_mine, jnp.concatenate(up_came)), 0, first_far)
+    down_mine, down_far = choose(joined(down_mine, jnp.concatenate(down_came)), 1, near_bits[0])
+    up_came, down_came = send(up_far, first_far), send(down_far, near_bits[0])
     grad_attended = dot(w_out_rows, grad_branch_all, 0, 1).astype(BF16)
-    final_out = lax.psum_scatter(
-        dot(grad_branch_all, attended, 0, 1).astype(BF16), "band", scatter_dimension=0, tiled=True
-    )
+    out_mine, out_far = choose(
+        dot(grad_branch_all, attended, 0, 1)
+        .astype(BF16)
+        .reshape((2,) * stages + (unit, head_width)),
+        stages - 1,
+        0,
+        plain=True,
+    )
+    out_came = send(out_far, 0)
     grad_q, grad_k, grad_v = attend_back(
         queries,
         keys,
@@ -605,14 +608,37 @@
     grad_heads = jnp.concatenate(
         [member.reshape(head_width, count) for member in (grad_q, grad_k, grad_v)]
     )
-    mlp_out = scatter_sum(near_mlp, after(far_mlp, grad_branch_all), "dp", dp, grad_heads) + b_down
-    grad_heads = after(grad_heads, mlp_out, up_came, down_came)
-    up_half, down_half = joined(up_mine, up_came), joined(down_mine, down_came)
+    output_came = [
+        lax.ppermute(after(output[turn], grad_branch_all), both, inward[turn])
+        for turn in range(rows_dev - 1)
+    ]
+    grad_heads, up_came, down_came, out_came, output_came = together(
+        grad_heads, up_came, down_came, out_came, output_came
+    )
     far_half, near_half = products(
         lambda part: dot(part, w_heads, 0, 0), lambda low, high: grad_heads[:, low:high]
     )
-    grad_hidden_a = scatter_sum(near_half, far_half, "dp", dp)
-    output = from_groups((middle + gate_b * mlp_out).astype(BF16))
+    grad_hidden_a = scatter_first(near_half, far_half, "dp", dp)
+    out_came, grad_heads, near_half, far_half, _ = together(
+        out_came, grad_heads, near_half, far_half, grad_hidden_a
+    )
+    grad_hidden_a = scatter_rest(grad_hidden_a, "dp", dp)
+    up_mine, up_came, down_mine, down_came, _ = together(
+        up_mine, up_came, down_mine, down_came, near_half
+    )
+    up_down = jnp.stack([joined(up_mine, up_came), joined(down_mine, down_came)])
+    up_down_rest = [2] * (len(near_bits) - 1) + [1] * (len(far_bits) - 1), near_bits[1:] + far_bits[1:]
+    up_down_mine, up_down_far = choose(up_down, up_down_rest[0][0], up_down_rest[1][0])
+    up_down_came = send(up_down_far, up_down_rest[1][0])
+    grad_w_heads = dot(grad_heads, hidden_a_all).astype(BF16).reshape(3, across, unit, width)
+    qkv_axes = [1] * log2(across) + [3] * log2(dp)
+    qkv_mine, qkv_far = choose(grad_w_heads, qkv_axes[0], near_first[0])
+    qkv_came = send(qkv_far, near_first[0])
+    output_came = output_came + [
+        lax.ppermute(after(output[-1], grad_heads), both, inward[rows_dev - 1])
+    ]
+    out_half = joined(out_mine, out_came)
+    near_half, far_half, _ = together(near_half, far_half, (qkv_far, up_down_far))
 
     hot_tokens = jnp.broadcast_to(
         hot_all.T.astype(BF16)[:, :, None], (images, hot_all.shape[0], piece)
@@ -641,53 +667,78 @@
         axis=1,
     )
     grad_mod = jnp.transpose(grad_mod.reshape(images, dp, mod_width), (1, 0, 2))
-    grad_mod_own = scatter_blocks(grad_mod, "dp", dp)
+    grad_mod_own = jnp.sum(lax.all_to_all(grad_mod, "dp", 0, 0, tiled=True), axis=0)
     high = grad_mod_own.astype(BF16)
     low = (grad_mod_own - high.astype(F32)).astype(BF16)
     grad_silu = dot(jnp.concatenate([high, low], axis=0), w_mod, 1, 1)
     grad_silu = grad_silu[:images] + grad_silu[images:]
     ones = jnp.ones((8, count), BF16)
-    bias_own = jnp.concatenate(
-        [
-            jnp.sum(grad_mlp_all[: rows_dev * piece].astype(F32), axis=0),
-            jnp.sum(grad_branch.astype(F32), axis=(0, 1)),
-            dot(ones, grad_pre)[0],
-            dot(ones, grad_heads, 1, 1)[0],
-        ]
-    )
+    bias_rows = [
+        jnp.sum(grad_mlp_all[: rows_dev * piece].astype(F32), axis=0),
+        jnp.sum(grad_branch.astype(F32), axis=(0, 1)),
+        dot(ones, grad_pre)[0],
+        dot(ones, grad_heads, 1, 1)[0],
+    ]
+    assert images >= len(bias_rows)
+    bias_rows = [
+        jnp.pad(member, (0, width - member.shape[0])) for member in bias_rows
+    ] + [jnp.zeros((width,), F32)] * (images - len(bias_rows))
+    packed = jnp.concatenate([grad_mod_own, grad_silu, jnp.stack(bias_rows)], axis=1)
+    grad_hidden_a, output_came, packed = together(grad_hidden_a, output_came, packed)
+    output = xor_shuffle(jnp.stack(output_came), my_slot)
     inputs = tokens_own.astype(F32)
     norm_a, spread_a = layer_norm(inputs)
     grad_tokens = grad_middle + layer_norm_back(grad_hidden_a * (1.0 + scale_a), norm_a, spread_a)
-    grad_tokens = after(grad_tokens.astype(BF16), output)
-    packed = jnp.concatenate([grad_mod_own.reshape(-1), grad_silu.reshape(-1), bias_own])
-    packed = gather_all(after(packed, grad_tokens), "band", band)
-    mod_size, silu_size = images * mod_width, images * width
-    grad_mod_groups = packed[:, :mod_size].reshape(band * images, mod_width)
-    grad_silu_groups = packed[:, mod_size : mod_size + silu_size].reshape(rows, spans, -1).sum(1)
-    bias_sum = jnp.sum(packed[:, mod_size + silu_size :], axis=0)
+    grad_tokens = grad_tokens.astype(BF16)
+    grad_tokens_came = [
+        lax.ppermute(grad_tokens[turn], both, inward[turn]) for turn in range(rows_dev)
+    ]
+    packed, _ = together(packed, grad_tokens)
+    packed = gather_all(packed, "band", band, [1 << bit for bit in far_bits + near_bits])
+    packed, qkv_came, up_down_came, out_half = together(
+        packed, qkv_came, up_down_came, out_half
+    )
+    qkv_half = joined(qkv_mine, qkv_came)
+    qkv_mine, qkv_far = choose(qkv_half, qkv_axes[1], near_first[1])
+    qkv_came = send(qkv_far, near_first[1])
+    out_mine, out_far = choose(out_half, stages - 2, near_first[1], plain=True)
+    out_came = send(out_far, near_first[1])
+    up_down = sum_groups(
+        joined(up_down_mine, up_down_came), up_down_rest[0][1:], up_down_rest[1][1:]
+    )
+    grad_tokens = xor_shuffle(jnp.stack(grad_tokens_came), my_slot)
+    grad_mod_groups = packed[:, :, :mod_width].reshape(band * images, mod_width)
+    grad_silu_groups = packed[:, :, mod_width : mod_width + width]
+    grad_silu_groups = grad_silu_groups.reshape(rows, spans, images, width).sum(1)
+    mod_sum = jnp.sum(grad_mod_groups, axis=0)
+    mod_rows = -(-mod_width // width)
+    mod_sum = jnp.pad(mod_sum, (0, mod_rows * width - mod_width)).reshape(mod_rows, width)
     final_pack = jnp.concatenate(
-        [grad_silu_groups.reshape(-1), jnp.sum(grad_mod_groups, axis=0), bias_sum]
-    )
+        [
+            grad_silu_groups.reshape(rows * images, width),
+            jnp.sum(packed[:, :, mod_width + width :], axis=0),
+            mod_sum,
+        ]
+    )
+    qkv_sum = sum_groups(joined(qkv_mine, qkv_came), qkv_axes[2:], near_first[2:])
+    qkv_sum = qkv_sum.reshape(3, unit, head_width)
+    out_sum = sum_groups(
+        joined(out_mine, out_came), list(reversed(range(stages - 2))), near_first[2:], plain=True
+    )
+    final_out = out_sum.reshape(unit, head_width).T.astype(F32)
     final_pack = gather_all(final_pack, "dp", dp)
-
-    grad_tokens_sent = grad_tokens
-    grad_tokens = from_groups(grad_tokens)
-
-    final_out = after(final_out, final_pack).T.astype(F32)
-    final_up = sum_groups(up_half, rows_then_units[2:], near_first[2:], (packed,))
-    final_up = lax.ppermute(final_up, both, owner_pairs(near_first, by_rows)).astype(F32)
-    final_down = sum_groups(down_half, rows_then_units[2:], far_first[2:], (packed,))
-    final_down = lax.ppermute(final_down.T, both, owner_pairs(far_first, by_rows)).astype(F32)
-    hidden_a_late = after(hidden_a_all, near_half)
-    grad_w_heads = dot(grad_heads, hidden_a_late).astype(BF16).reshape(3, across, unit, width)
-    qkv_sum = sum_groups(
-        after(grad_w_heads, grad_hidden_a),
-        [1] * log2(across) + [3] * log2(dp),
-        near_first,
-        (packed,),
-        (final_pack,),
-    )
-    qkv_sum = qkv_sum.reshape(3, unit, head_width)
+    up_down = lax.ppermute(up_down, both, owner_pairs(lambda d, b, block, unit: block * band + b))
+    up_down = lax.ppermute(
+        after(up_down, qkv_sum),
+        both,
+        [
+            (d * band + b, d * band + ((b // across) ^ reverse_bits(d, dp)) * across + reverse_bits(b % across, across))
+            for d in range(dp)
+            for b in range(band)
+        ],
+    )
+    final_up, final_down = up_down[0].astype(F32), up_down[1].T.astype(F32)
+
     kind_of = [
         [next(kind for kind in range(3) if (kind * dp + d) % 3 == slot) for slot in range(3)]
         for d in range(dp)
@@ -698,8 +749,7 @@
         )
         for slot in range(3)
     ]
-    my_index = index_of(group, near_first)
-    my_unit = my_index >> log2(dp)
+    my_unit = reverse_bits(group & (across - 1), across)
     final_qkv = []
     for turn in range(3):
         slots = []
@@ -713,18 +763,17 @@
             assert len(options) == 1
             slots.append(options.pop())
 
-        def owner(d, index, slots=slots, turn=turn):
-            at = index // dp
+        def owner(d, b, block, at, slots=slots, turn=turn):
             start = band * kind_of[d][slots[at]] + across * d + at
             assert start % 3 == turn
-            return (index % dp) * band + start // 3
+            return block * band + start // 3
 
         kind = sum(
             jnp.where(my_unit == at, kind_now[slots[at]], 0).astype(jnp.int32)
             for at in range(across)
         )
         final_qkv.append(
-            lax.ppermute(pick(qkv_sum, kind), both, owner_pairs(near_first, owner))
+            lax.ppermute(pick(qkv_sum, kind), both, owner_pairs(owner))
         )
     final_qkv = jnp.concatenate(final_qkv).T.astype(F32)
 
@@ -733,18 +782,15 @@
     index_all = xor_shuffle(facts_all, me_turned).reshape(rows, 2 * images)[:, images:].reshape(-1)
     condition = conditions(after(index_all, grad_branch))
     silu_all = jax.nn.silu(condition).astype(BF16)
-    silu_end = rows * silu_size
-    grad_silu_rows = jnp.sum(final_pack[:, :silu_end], axis=0).reshape(rows * images, width)
-    ends = [silu_end]
-    for size in (mod_width, width, width, hidden_width, head_width, head_width, head_width):
-        ends.append(ends[-1] + size)
-    tail = [final_pack[:, low:high] for low, high in zip(ends[:-1], ends[1:], strict=True)]
-    final_b_mod = tail[0].reshape(-1)
-    final_b_down = jnp.sum(tail[1], axis=0)
-    final_b_out = jnp.sum(tail[2], axis=0)
-    final_b_up = tail[3].reshape(-1)
-    final_b_query = tail[4].reshape(-1)
-    final_b_value = tail[6].reshape(-1)
+    silu_rows = rows * images
+    grad_silu_rows = jnp.sum(final_pack[:, :silu_rows], axis=0)
+    bias_all = final_pack[:, silu_rows : silu_rows + images]
+    final_b_down = jnp.sum(bias_all[:, 0], axis=0)
+    final_b_out = jnp.sum(bias_all[:, 1], axis=0)
+    final_b_up = bias_all[:, 2, :hidden_width].reshape(-1)
+    final_b_query = bias_all[:, 3, :head_width].reshape(-1)
+    final_b_value = bias_all[:, 3, 2 * head_width : 3 * head_width].reshape(-1)
+    final_b_mod = final_pack[:, silu_rows + images :].reshape(dp, -1)[:, :mod_width].reshape(-1)
     sigmoid = jax.nn.sigmoid(condition)
     grad_condition = grad_silu_rows * (sigmoid * (1.0 + condition * (1.0 - sigmoid)))
     table_hot = (
@@ -753,9 +799,9 @@
     final_table = jnp.dot(table_hot, grad_condition, precision=HIGHEST)
     mod_share = mod_width // across
     grad_mod_share = lax.ppermute(
-        cut(grad_mod_groups, (my_index & (across - 1)) * mod_share, mod_share, 1),
+        cut(grad_mod_groups, my_unit * mod_share, mod_share, 1),
         both,
-        owner_pairs(near_first, by_rows),
+        owner_pairs(lambda d, b, block, at: block * band + across * d + at),
     )
     silu_share = cut(silu_all, me * head_width, head_width, 1).astype(F32)
     silu_share = jnp.repeat(silu_share.reshape(rows, images, -1), spans, axis=0)

time: 511 us -> 475 us (0.930)
  the two profiles are of different devices: /device:TPU:4 before, /device:TPU:1 now
where the time goes in v3:
time: 475 us; the launch traced here: 466 us
  waiting for transfers between devices  145 us (31%)
  starting transfers between devices  110 us (23%)
  other arithmetic  73.2 us (15%)
  matrix products  59.2 us (12%)
  local copies, waits for them, and re-layouts  45.5 us (10%)
  Pallas kernels  29.1 us (6%)
    dot_general x26, matrix products, dot(): lax.dot_general(left, right, (((left_dim,), (right_dim,)), ((), ())), pre...  52.1 us
    ppermute x8, waiting for transfers between devices, gather_parts(): came = lax.ppermute(held, axis, xor_perm(count, bit))  35.7 us
    ppermute x13, waiting for transfers between devices, send(): return lax.ppermute(part, 'band', xor_perm(band, 1 << bit))  30 us
    ppermute x4, waiting for transfers between devices, scatter_rest(): came = lax.ppermute(held[half:].astype(BF16), axis, xor_perm(count, bit))  27.4 us
    ppermute x9, waiting for transfers between devices, gather_stack(): lax.ppermute(held, axis, xor_perm(count, bit))  19.6 us
    ppermute x9, starting transfers between devices, gather_stack(): lax.ppermute(held, axis, xor_perm(count, bit))  19.3 us
    pallas_call x1, Pallas kernels, attend(): pl.pallas_call(functools.partial(attend_kernel, piece), grid_spec=pltpu.P...  15.2 us
    pallas_call x1, Pallas kernels, attend_back(): pl.pallas_call(attend_back_kernel, grid=(heads, count // lanes), in_specs...  13.9 us
  transfers between devices with their start and end apart: 59, of which 26 were waited for; matrix products, arithmetic and copies ran while one was open for 28% of the time, Pallas kernels for 6%

profile of v3, /device:TPU:1, one launch (start us, length us, event | category | flops | bytes accessed | tf_op | source)
XLA Modules:
  0.0 466.0 jit_solution(6048127694880844220)
XLA Ops:
  1.6 5.7 %collective-permute-start.4 = (s32[8]{0:T(128)S(1)}, s32[8]{0:T(128)S(1)}, u32[]{:S(2)}, u32[]{:S(2)}) collective-permute-start(s32[8]{0:T(128)S(1)} %fusion.69), channel_id=1, source_target_pairs={{0,0},{1,16},{2,8},{3,24},{4,1},{5,17},{6,9},{7,25},{8,4},{9,20},{... | collective-permute-start | bytes 104 | tf_op jit(solution)/shard_map/ppermute | solution.py:368
  17.2 3.8 collective-permute-start.2
  32.1 3.4 fusion.5
  36.2 8.1 %collective-permute-done.5 = f32[1,4,1728]{2,1,0:T(4,128)S(1)} collective-permute-done((f32[1,4,1728]{2,1,0:T(4,128)S(1)}, f32[1,4,1728]{2,1,0:T(4,128)S(1)}, u32[]{:S(2)}, u32[]{:S(2)}) %collective-permute-start.5) | collective-permute-done | bytes 27680 | tf_op jit(solution)/shard_map/ppermute | solution.py:84
  65.0 11.8 %collective-permute-done.7 = bf16[1,2,128,1152]{3,2,1,0:T(8,128)(2,1)} collective-permute-done((bf16[1,2,128,1152]{3,2,1,0:T(8,128)(2,1)S(1)}, bf16[1,2,128,1152]{3,2,1,0:T(8,128)(2,1)}, u32[]{:S(2)}, u32[]{:S(2)}) %collective-permute-start.7) | collective-permute-done | bytes 589856 | tf_op jit(solution)/shard_map/ppermute | solution.py:74
  88.4 7.5 %collective-permute-done.9 = bf16[288,1440]{1,0:T(8,128)(2,1)S(1)} collective-permute-done((bf16[288,1440]{1,0:T(8,128)(2,1)}, bf16[288,1440]{1,0:T(8,128)(2,1)S(1)}, u32[]{:S(2)}, u32[]{:S(2)}) %collective-permute-start.9) | collective-permute-done | bytes 829472 | tf_op jit(solution)/shard_map/ppermute | solution.py:456
  97.4 15.2 %attend.1 = (bf16[4,72,1024]{2,1,0:T(8,128)(2,1)}, bf16[4,1024,1024]{2,1,0:T(8,128)(2,1)}) custom-call(s32[17]{0:T(128)} %pad_add_fusion.4.facts_ref, bf16[4,72,1024]{2,1,0:T(8,128)(2,1)} %bitcast.267, bf16[4,72,1024]{2,1,0:T(8,128)(2,1)} %bitcast.265, bf16[4,72,1024]{2,1,0:T(8,128)(2,1)} %bitcast.263), custom_call_target="tpu_custom_call" | custom-call | flops 16106127360 | bytes 8388608 | tf_op jit(solution)/shard_map/attend/pallas_call | solution.py:178
  125.5 12.9 %collective-permute-done.15 = bf16[1,2,128,1152]{3,2,1,0:T(8,128)(2,1)S(1)} collective-permute-done((bf16[1,2,128,1152]{3,2,1,0:T(8,128)(2,1)S(1)}, bf16[1,2,128,1152]{3,2,1,0:T(8,128)(2,1)S(1)}, u32[]{:S(2)}, u32[]{:S(2)}) %collective-permute-start.15) | collective-permute-done | bytes 589856 | tf_op jit(solution)/shard_map/ppermute | solution.py:107
  143.4 12.4 %collective-permute-done.16 = bf16[1,2,128,1152]{3,2,1,0:T(8,128)(2,1)} collective-permute-done((bf16[1,2,128,1152]{3,2,1,0:T(8,128)(2,1)}, bf16[1,2,128,1152]{3,2,1,0:T(8,128)(2,1)}, u32[]{:S(2)}, u32[]{:S(2)}) %collective-permute-start.16) | collective-permute-done | bytes 589856 | tf_op jit(solution)/shard_map/ppermute | solution.py:74
  167.4 6.2 %add_convert_fusion = (bf16[1024,1152]{1,0:T(8,128)(2,1)}, bf16[1024,1152]{1,0:T(8,128)(2,1)S(1)}) fusion(f32[1152]{0:T(1024)S(1)} %dynamic_slice.180, bf16[1024,1152]{1,0:T(8,128)(2,1)S(1)} %bitcast.251, bf16[1152,1152]{1,0:T(8,128)(2,1)S(1)} %copy-done), kind=kOutput, calls=%fused_computation.10 | convolution fusion | flops 2741501952 | bytes 9736704 | tf_op jit(solution)/shard_map/dot_general | solution.py:26
  183.7 3.3 convolution_convert_fusion.8
  193.4 3.5 fusion.2
  201.7 3.5 collective-permute-done.21
  207.0 3.5 convolution_convert_fusion
  217.0 11.0 %collective-permute-done.23 = bf16[1,2,128,1152]{3,2,1,0:T(8,128)(2,1)S(1)} collective-permute-done((bf16[1,2,128,1152]{3,2,1,0:T(8,128)(2,1)S(1)}, bf16[1,2,128,1152]{3,2,1,0:T(8,128)(2,1)S(1)}, u32[]{:S(2)}, u32[]{:S(2)}) %collective-permute-start.23) | collective-permute-done | bytes 589856 | tf_op jit(solution)/shard_map/ppermute | solution.py:107
  242.1 8.4 %collective-permute-done.26 = bf16[1,2,128,1152]{3,2,1,0:T(8,128)(2,1)S(1)} collective-permute-done((bf16[1,2,128,1152]{3,2,1,0:T(8,128)(2,1)S(1)}, bf16[1,2,128,1152]{3,2,1,0:T(8,128)(2,1)S(1)}, u32[]{:S(2)}, u32[]{:S(2)}) %collective-permute-start.26) | collective-permute-done | bytes 589856 | tf_op jit(solution)/shard_map/ppermute | solution.py:74
  254.3 3.9 collective-permute-start.29
  273.2 13.9 %attend_back.1 = (bf16[4,72,1024]{2,1,0:T(8,128)(2,1)}, bf16[4,72,1024]{2,1,0:T(8,128)(2,1)}, bf16[4,72,1024]{2,1,0:T(8,128)(2,1)}) custom-call(bf16[4,72,1024]{2,1,0:T(8,128)(2,1)} %bitcast.268, bf16[4,72,1024]{2,1,0:T(8,128)(2,1)} %bitcast.266, bf16[4,72,1024]{2,1,0:T(8,128)(2,1)} %bitcast.264, bf16[4,72,1024]{2,1,0:T(8,128)(2,1)} %get-tuple-element.94.out_ref, ...), custom_call_target="tpu_custom_call" | custom-call | flops 16106127360 | bytes 8388608 | tf_op jit(solution)/shard_map/attend_back/pallas_call | solution.py:242
  304.0 11.9 %collective-permute-start.36 = (bf16[128,1152]{1,0:T(8,128)(2,1)}, bf16[128,1152]{1,0:T(8,128)(2,1)}, u32[]{:S(2)}, u32[]{:S(2)}) collective-permute-start(bf16[128,1152]{1,0:T(8,128)(2,1)} %get-tuple-element.125), channel_id=1, source_target_pairs={{1,0},{17,1},{9,2},{25,3},{0,4},{16,5},{8,6},{24,7},{5,8},{21,9},{... | collective-permute-start | bytes 884744 | tf_op jit(solution)/shard_map/ppermute | solution.py:638
  325.0 4.2 all-to-all-start
  329.3 7.9 %all-to-all-done = f32[4,4,1728]{2,1,0:T(4,128)S(1)} async-done(((f32[4,4,1728]{2,1,0:T(4,128)}), f32[4,4,1728]{2,1,0:T(4,128)S(1)}, u32[]{:S(2)}, u32[]{:S(2)}) %all-to-all-start) | async-done | bytes 110624 | tf_op jit(solution)/shard_map/all_to_all | solution.py:670
  345.2 10.1 %collective-permute-done.41 = f32[1,4,4032]{2,1,0:T(4,128)S(1)} collective-permute-done((f32[1,4,4032]{2,1,0:T(4,128)S(1)}, f32[1,4,4032]{2,1,0:T(4,128)S(1)}, u32[]{:S(2)}, u32[]{:S(2)}) %collective-permute-start.41) | collective-permute-done | bytes 64544 | tf_op jit(solution)/shard_map/ppermute | solution.py:84
  364.3 11.8 %collective-permute-start.43 = (f32[4,4,4032]{2,1,0:T(4,128)S(1)}, f32[4,4,4032]{2,1,0:T(4,128)S(1)}, u32[]{:S(2)}, u32[]{:S(2)}) collective-permute-start(f32[4,4,4032]{2,1,0:T(4,128)S(1)} %pad_maximum_fusion.21), channel_id=1, source_target_pairs={{0,1},{1,0},{2,3},{3,2},{4,5},{5,4},{6,7},{7,6},{8,9},{9,8},{10,11... | collective-permute-start | bytes 774152 | tf_op jit(solution)/shard_map/ppermute | solution.py:84
  376.1 5.8 %collective-permute-done.38 = bf16[128,1152]{1,0:T(8,128)(2,1)S(1)} collective-permute-done((bf16[128,1152]{1,0:T(8,128)(2,1)S(1)}, bf16[128,1152]{1,0:T(8,128)(2,1)S(1)}, u32[]{:S(2)}, u32[]{:S(2)}) %collective-permute-start.38) | collective-permute-done | bytes 294944 | tf_op jit(solution)/shard_map/ppermute | solution.py:694
  393.4 5.3 %collective-permute-start.56 = (bf16[2,288,576]{2,1,0:T(8,128)(2,1)S(1)}, bf16[2,288,576]{2,1,0:T(8,128)(2,1)}, u32[]{:S(2)}, u32[]{:S(2)}) collective-permute-start(bf16[2,288,576]{2,1,0:T(8,128)(2,1)S(1)} %add_convert_fusion.5), channel_id=1, source_target_pairs={{0,0},{1,1},{2,18},{3,19},{4,12},{5,13},{6,30},{7,31},{8,16},{9,17... | collective-permute-start | bytes 1990664 | tf_op jit(solution)/shard_map/ppermute | solution.py:730
  405.3 5.2 %collective-permute-done.55 = bf16[1,1,1,144,288]{4,3,2,1,0:T(8,128)(2,1)S(1)} collective-permute-done((bf16[1,1,1,144,288]{4,3,2,1,0:T(8,128)(2,1)S(1)}, bf16[1,1,1,144,288]{4,3,2,1,0:T(8,128)(2,1)S(1)}, u32[]{:S(2)}, u32[]{:S(2)}) %collective-permute-start.55) | collective-permute-done | bytes 82976 | tf_op jit(solution)/shard_map/ppermute | solution.py:542
  411.2 3.5 collective-permute-done.49
  418.6 4.3 fusion.30
  422.9 4.3 collective-permute-start.57
  428.6 12.6 %collective-permute-done.50 = bf16[3,1,144,288]{3,2,1,0:T(8,128)(2,1)} collective-permute-done((bf16[3,1,144,288]{3,2,1,0:T(8,128)(2,1)}, bf16[3,1,144,288]{3,2,1,0:T(8,128)(2,1)}, u32[]{:S(2)}, u32[]{:S(2)}) %collective-permute-start.50) | collective-permute-done | bytes 248864 | tf_op jit(solution)/shard_map/ppermute | solution.py:542
  449.6 3.7 collective-permute-start.51
  456.7 4.8 %collective-permute-done.51 = bf16[144,288]{0,1:T(8,128)(2,1)} collective-permute-done((bf16[144,288]{0,1:T(8,128)(2,1)}, bf16[144,288]{0,1:T(8,128)(2,1)}, u32[]{:S(2)}, u32[]{:S(2)}) %collective-permute-start.51) | collective-permute-done | bytes 82976 | tf_op jit(solution)/shard_map/ppermute | solution.py:776
  (499 shorter events, 229.0 us)
Async XLA Ops:
  1.6 26.4 %collective-permute-start.4 = (s32[8]{0:T(128)S(1)}, s32[8]{0:T(128)S(1)}, u32[]{:S(2)}, u32[]{:S(2)}) collective-permute-start(s32[8]{0:T(128)S(1)} %fusion.69), channel_id=1, source_target_pairs={{0,0},{1,16},{2,8},{3,24},{4,1},{5,17},{6,9},{7,25},{8,4},{9,20},{... | collective-permute-start | bytes 104 | tf_op jit(solution)/shard_map/ppermute | solution.py:368
  9.3 38.1 %collective-permute-start = (bf16[128,1152]{1,0:T(8,128)(2,1)}, bf16[128,1152]{1,0:T(8,128)(2,1)}, u32[]{:S(2)}, u32[]{:S(2)}) collective-permute-start(bf16[128,1152]{1,0:T(8,128)(2,1)} %get-tuple-element.259), channel_id=1, source_target_pairs={{0,0},{1,16},{2,8},{3,24},{4,1},{5,17},{6,9},{7,25},{8,4},{9,20},{... | collective-permute-start | bytes 884744 | tf_op jit(solution)/shard_map/ppermute | solution.py:371
  12.4 34.9 %collective-permute-start.1 = (bf16[128,1152]{1,0:T(8,128)(2,1)}, bf16[128,1152]{1,0:T(8,128)(2,1)}, u32[]{:S(2)}, u32[]{:S(2)}) collective-permute-start(bf16[128,1152]{1,0:T(8,128)(2,1)} %get-tuple-element.260), channel_id=1, source_target_pairs={{0,1},{1,17},{2,9},{3,25},{4,0},{5,16},{6,8},{7,24},{8,5},{9,21},{... | collective-permute-start | bytes 884744 | tf_op jit(solution)/shard_map/ppermute | solution.py:371
  17.2 27.2 %collective-permute-start.2 = (bf16[288,1152]{1,0:T(8,128)(2,1)}, bf16[288,1152]{1,0:T(8,128)(2,1)}, u32[]{:S(2)}, u32[]{:S(2)}) collective-permute-start(bf16[288,1152]{1,0:T(8,128)(2,1)} %broadcast_select_fusion.10), channel_id=1, source_target_pairs={{0,16},{8,24},{16,0},{24,8},{1,17},{9,25},{17,1},{25,9},{2,18},{10... | collective-permute-start | bytes 1990664 | tf_op jit(solution)/shard_map/ppermute | solution.py:382
  49.9 27.0 %collective-permute-start.7 = (bf16[1,2,128,1152]{3,2,1,0:T(8,128)(2,1)S(1)}, bf16[1,2,128,1152]{3,2,1,0:T(8,128)(2,1)}, u32[]{:S(2)}, u32[]{:S(2)}) collective-permute-start(bf16[1,2,128,1152]{3,2,1,0:T(8,128)(2,1)S(1)} %bitcast.230), channel_id=1, source_target_pairs={{0,16},{8,24},{16,0},{24,8},{1,17},{9,25},{17,1},{25,9},{2,18},{10... | collective-permute-start | bytes 1769480 | tf_op jit(solution)/shard_map/ppermute | solution.py:74
  55.7 24.6 %collective-permute-start.10 = (bf16[128,1152]{1,0:T(8,128)(2,1)}, bf16[128,1152]{1,0:T(8,128)(2,1)S(1)}, u32[]{:S(2)}, u32[]{:S(2)}) collective-permute-start(bf16[128,1152]{1,0:T(8,128)(2,1)} %get-tuple-element.257), channel_id=1, source_target_pairs={{0,0},{1,16},{2,8},{3,24},{4,1},{5,17},{6,9},{7,25},{8,4},{9,20},{... | collective-permute-start | bytes 884744 | tf_op jit(solution)/shard_map/ppermute | solution.py:347
  57.7 22.7 %collective-permute-start.11 = (bf16[128,1152]{1,0:T(8,128)(2,1)}, bf16[128,1152]{1,0:T(8,128)(2,1)S(1)}, u32[]{:S(2)}, u32[]{:S(2)}) collective-permute-start(bf16[128,1152]{1,0:T(8,128)(2,1)} %get-tuple-element.258), channel_id=1, source_target_pairs={{0,1},{1,17},{2,9},{3,25},{4,0},{5,16},{6,8},{7,24},{8,5},{9,21},{... | collective-permute-start | bytes 884744 | tf_op jit(solution)/shard_map/ppermute | solution.py:347
  57.8 38.1 %collective-permute-start.9 = (bf16[288,1440]{1,0:T(8,128)(2,1)}, bf16[288,1440]{1,0:T(8,128)(2,1)S(1)}, u32[]{:S(2)}, u32[]{:S(2)}) collective-permute-start(bf16[288,1440]{1,0:T(8,128)(2,1)} %dynamic-slice_bitcast_fusion.3), channel_id=1, source_target_pairs={{0,16},{8,24},{16,0},{24,8},{1,17},{9,25},{17,1},{25,9},{2,18},{10... | collective-permute-start | bytes 2488328 | tf_op jit(solution)/shard_map/ppermute | solution.py:456
  62.9 52.0 %collective-permute-start.13 = (bf16[288,1440]{1,0:T(8,128)(2,1)}, bf16[288,1440]{1,0:T(8,128)(2,1)}, u32[]{:S(2)}, u32[]{:S(2)}) collective-permute-start(bf16[288,1440]{1,0:T(8,128)(2,1)} %get-tuple-element.199), channel_id=1, source_target_pairs={{0,24},{8,16},{16,8},{24,0},{1,25},{9,17},{17,9},{25,1},{2,26},{10... | collective-permute-start | bytes 2488328 | tf_op jit(solution)/shard_map/ppermute | solution.py:478
  80.3 34.5 %collective-permute-start.12 = (bf16[288,1440]{1,0:T(8,128)(2,1)}, bf16[288,1440]{1,0:T(8,128)(2,1)}, u32[]{:S(2)}, u32[]{:S(2)}) collective-permute-start(bf16[288,1440]{1,0:T(8,128)(2,1)} %get-tuple-element.200), channel_id=1, source_target_pairs={{0,8},{8,0},{16,24},{24,16},{1,9},{9,1},{17,25},{25,17},{2,10},{10... | collective-permute-start | bytes 2488328 | tf_op jit(solution)/shard_map/ppermute | solution.py:478
  123.0 15.5 %collective-permute-start.15 = (bf16[1,2,128,1152]{3,2,1,0:T(8,128)(2,1)S(1)}, bf16[1,2,128,1152]{3,2,1,0:T(8,128)(2,1)S(1)}, u32[]{:S(2)}, u32[]{:S(2)}) collective-permute-start(bf16[1,2,128,1152]{3,2,1,0:T(8,128)(2,1)S(1)} %slice.621), channel_id=1, source_target_pairs={{0,16},{8,24},{16,0},{24,8},{1,17},{9,25},{17,1},{25,9},{2,18},{10... | collective-permute-start | bytes 1769480 | tf_op jit(solution)/shard_map/ppermute | solution.py:107
  163.7 14.8 %collective-permute-start.40 = (s32[2,2,8]{2,1,0:T(2,128)S(1)}, s32[2,2,8]{2,1,0:T(2,128)S(1)}, u32[]{:S(2)}, u32[]{:S(2)}) collective-permute-start(s32[2,2,8]{2,1,0:T(2,128)S(1)} %pad_add_fusion.2), channel_id=1, source_target_pairs={{0,8},{8,0},{16,24},{24,16},{1,9},{9,1},{17,25},{25,17},{2,10},{10... | collective-permute-start | bytes 392 | tf_op jit(solution)/shard_map/ppermute | solution.py:84
  166.1 15.4 %collective-permute-start.18 = (bf16[1,2,128,1152]{3,2,1,0:T(8,128)(2,1)}, bf16[1,2,128,1152]{3,2,1,0:T(8,128)(2,1)}, u32[]{:S(2)}, u32[]{:S(2)}) collective-permute-start(bf16[1,2,128,1152]{3,2,1,0:T(8,128)(2,1)} %bitcast.54), channel_id=1, source_target_pairs={{0,16},{8,24},{16,0},{24,8},{1,17},{9,25},{17,1},{25,9},{2,18},{10... | collective-permute-start | bytes 1769480 | tf_op jit(solution)/shard_map/ppermute | solution.py:74
  190.2 15.0 %collective-permute-start.21 = (bf16[1,2,128,1152]{3,2,1,0:T(8,128)(2,1)S(1)}, bf16[1,2,128,1152]{3,2,1,0:T(8,128)(2,1)S(1)}, u32[]{:S(2)}, u32[]{:S(2)}) collective-permute-start(bf16[1,2,128,1152]{3,2,1,0:T(8,128)(2,1)S(1)} %slice.620), channel_id=1, source_target_pairs={{0,16},{8,24},{16,0},{24,8},{1,17},{9,25},{17,1},{25,9},{2,18},{10... | collective-permute-start | bytes 1769480 | tf_op jit(solution)/shard_map/ppermute | solution.py:107
  215.5 15.4 %collective-permute-start.25 = (bf16[288,1152]{1,0:T(8,128)(2,1)S(1)}, bf16[288,1152]{1,0:T(8,128)(2,1)S(1)}, u32[]{:S(2)}, u32[]{:S(2)}) collective-permute-start(bf16[288,1152]{1,0:T(8,128)(2,1)S(1)} %get-tuple-element.228), channel_id=1, source_target_pairs={{0,2},{1,3},{2,0},{3,1},{4,6},{5,7},{6,4},{7,5},{8,10},{9,11},{10,... | collective-permute-start | bytes 1990664 | tf_op jit(solution)/shard_map/ppermute | solution.py:542
  216.3 16.9 %collective-permute-start.24 = (bf16[576,576]{1,0:T(8,128)(2,1)S(1)}, bf16[576,576]{1,0:T(8,128)(2,1)S(1)}, u32[]{:S(2)}, u32[]{:S(2)}) collective-permute-start(bf16[576,576]{1,0:T(8,128)(2,1)S(1)} %get-tuple-element.224), channel_id=1, source_target_pairs={{0,1},{1,0},{2,3},{3,2},{4,5},{5,4},{6,7},{7,6},{8,9},{9,8},{10,11... | collective-permute-start | bytes 1990664 | tf_op jit(solution)/shard_map/ppermute | solution.py:542
  239.0 15.1 %collective-permute-start.27 = (bf16[576,576]{1,0:T(8,128)(2,1)S(1)}, bf16[576,576]{1,0:T(8,128)(2,1)S(1)}, u32[]{:S(2)}, u32[]{:S(2)}) collective-permute-start(bf16[576,576]{1,0:T(8,128)(2,1)S(1)} %get-tuple-element.110), channel_id=1, source_target_pairs={{0,1},{1,0},{2,3},{3,2},{4,5},{5,4},{6,7},{7,6},{8,9},{9,8},{10,11... | collective-permute-start | bytes 1990664 | tf_op jit(solution)/shard_map/ppermute | solution.py:542
  260.1 28.7 %collective-permute-start.31 = (bf16[576,576]{1,0:T(8,128)(2,1)}, bf16[576,576]{1,0:T(8,128)(2,1)}, u32[]{:S(2)}, u32[]{:S(2)}) collective-permute-start(bf16[576,576]{1,0:T(8,128)(2,1)} %get-tuple-element.226), channel_id=1, source_target_pairs={{0,1},{1,0},{2,3},{3,2},{4,5},{5,4},{6,7},{7,6},{8,9},{9,8},{10,11... | collective-permute-start | bytes 1990664 | tf_op jit(solution)/shard_map/ppermute | solution.py:542
  262.9 26.0 %collective-permute-start.30 = (bf16[576,576]{1,0:T(8,128)(2,1)}, bf16[576,576]{1,0:T(8,128)(2,1)}, u32[]{:S(2)}, u32[]{:S(2)}) collective-permute-start(bf16[576,576]{1,0:T(8,128)(2,1)} %get-tuple-element.222), channel_id=1, source_target_pairs={{0,2},{1,3},{2,0},{3,1},{4,6},{5,7},{6,4},{7,5},{8,10},{9,11},{10,... | collective-permute-start | bytes 1990664 | tf_op jit(solution)/shard_map/ppermute | solution.py:542
  267.7 21.1 %collective-permute-start.33 = (bf16[128,1152]{1,0:T(8,128)(2,1)S(1)}, bf16[128,1152]{1,0:T(8,128)(2,1)S(1)}, u32[]{:S(2)}, u32[]{:S(2)}) collective-permute-start(bf16[128,1152]{1,0:T(8,128)(2,1)S(1)} %get-tuple-element.120), channel_id=1, source_target_pairs={{0,0},{16,1},{8,2},{24,3},{1,4},{17,5},{9,6},{25,7},{4,8},{20,9},{... | collective-permute-start | bytes 884744 | tf_op jit(solution)/shard_map/ppermute | solution.py:612
  271.2 17.7 %collective-permute-start.32 = (bf16[2,2,1,144,288]{4,3,2,1,0:T(8,128)(2,1)S(1)}, bf16[2,2,1,144,288]{4,3,2,1,0:T(8,128)(2,1)S(1)}, u32[]{:S(2)}, u32[]{:S(2)}) collective-permute-start(bf16[2,2,1,144,288]{4,3,2,1,0:T(8,128)(2,1)S(1)} %broadcast_select_fusion.12), channel_id=1, source_target_pairs={{0,1},{1,0},{2,3},{3,2},{4,5},{5,4},{6,7},{7,6},{8,9},{9,8},{10,11... | collective-permute-start | bytes 995336 | tf_op jit(solution)/shard_map/ppermute | solution.py:542
  304.0 40.2 %collective-permute-start.36 = (bf16[128,1152]{1,0:T(8,128)(2,1)}, bf16[128,1152]{1,0:T(8,128)(2,1)}, u32[]{:S(2)}, u32[]{:S(2)}) collective-permute-start(bf16[128,1152]{1,0:T(8,128)(2,1)} %get-tuple-element.125), channel_id=1, source_target_pairs={{1,0},{17,1},{9,2},{25,3},{0,4},{16,5},{8,6},{24,7},{5,8},{21,9},{... | collective-permute-start | bytes 884744 | tf_op jit(solution)/shard_map/ppermute | solution.py:638
  315.9 24.3 %collective-permute-start.35 = (bf16[1,2,128,1152]{3,2,1,0:T(8,128)(2,1)}, bf16[1,2,128,1152]{3,2,1,0:T(8,128)(2,1)}, u32[]{:S(2)}, u32[]{:S(2)}) collective-permute-start(bf16[1,2,128,1152]{3,2,1,0:T(8,128)(2,1)} %slice.618), channel_id=1, source_target_pairs={{0,16},{8,24},{16,0},{24,8},{1,17},{9,25},{17,1},{25,9},{2,18},{10... | collective-permute-start | bytes 1769480 | tf_op jit(solution)/shard_map/ppermute | solution.py:107
  320.3 65.2 %collective-permute-start.45 = (bf16[2,288,576]{2,1,0:T(8,128)(2,1)}, bf16[2,288,576]{2,1,0:T(8,128)(2,1)}, u32[]{:S(2)}, u32[]{:S(2)}) collective-permute-start(bf16[2,288,576]{2,1,0:T(8,128)(2,1)} %broadcast_select_fusion.3), channel_id=1, source_target_pairs={{0,4},{1,5},{2,6},{3,7},{4,0},{5,1},{6,2},{7,3},{8,12},{9,13},{10,... | collective-permute-start | bytes 1990664 | tf_op jit(solution)/shard_map/ppermute | solution.py:542
  321.5 64.1 %collective-permute-start.44 = (bf16[3,1,144,1152]{3,2,1,0:T(8,128)(2,1)}, bf16[3,1,144,1152]{3,2,1,0:T(8,128)(2,1)}, u32[]{:S(2)}, u32[]{:S(2)}) collective-permute-start(bf16[3,1,144,1152]{3,2,1,0:T(8,128)(2,1)} %broadcast_select_fusion.2), channel_id=1, source_target_pairs={{0,1},{1,0},{2,3},{3,2},{4,5},{5,4},{6,7},{7,6},{8,9},{9,8},{10,11... | collective-permute-start | bytes 2985992 | tf_op jit(solution)/shard_map/ppermute | solution.py:542
  358.1 23.9 %collective-permute-start.38 = (bf16[128,1152]{1,0:T(8,128)(2,1)S(1)}, bf16[128,1152]{1,0:T(8,128)(2,1)S(1)}, u32[]{:S(2)}, u32[]{:S(2)}) collective-permute-start(bf16[128,1152]{1,0:T(8,128)(2,1)S(1)} %get-tuple-element.250), channel_id=1, source_target_pairs={{1,0},{17,1},{9,2},{25,3},{0,4},{16,5},{8,6},{24,7},{5,8},{21,9},{... | collective-permute-start | bytes 884744 | tf_op jit(solution)/shard_map/ppermute | solution.py:694
  360.4 21.5 %collective-permute-start.37 = (bf16[128,1152]{1,0:T(8,128)(2,1)S(1)}, bf16[128,1152]{1,0:T(8,128)(2,1)S(1)}, u32[]{:S(2)}, u32[]{:S(2)}) collective-permute-start(bf16[128,1152]{1,0:T(8,128)(2,1)S(1)} %get-tuple-element.251), channel_id=1, source_target_pairs={{0,0},{16,1},{8,2},{24,3},{1,4},{17,5},{9,6},{25,7},{4,8},{20,9},{... | collective-permute-start | bytes 884744 | tf_op jit(solution)/shard_map/ppermute | solution.py:694
  364.3 20.9 %collective-permute-start.43 = (f32[4,4,4032]{2,1,0:T(4,128)S(1)}, f32[4,4,4032]{2,1,0:T(4,128)S(1)}, u32[]{:S(2)}, u32[]{:S(2)}) collective-permute-start(f32[4,4,4032]{2,1,0:T(4,128)S(1)} %pad_maximum_fusion.21), channel_id=1, source_target_pairs={{0,1},{1,0},{2,3},{3,2},{4,5},{5,4},{6,7},{7,6},{8,9},{9,8},{10,11... | collective-permute-start | bytes 774152 | tf_op jit(solution)/shard_map/ppermute | solution.py:84
  393.3 21.4 %collective-permute-start.49 = (bf16[3,1,144,576]{3,2,1,0:T(8,128)(2,1)S(1)}, bf16[3,1,144,576]{3,2,1,0:T(8,128)(2,1)S(1)}, u32[]{:S(2)}, u32[]{:S(2)}) collective-permute-start(bf16[3,1,144,576]{3,2,1,0:T(8,128)(2,1)S(1)} %broadcast_select_fusion.11), channel_id=1, source_target_pairs={{0,2},{1,3},{2,0},{3,1},{4,6},{5,7},{6,4},{7,5},{8,10},{9,11},{10,... | collective-permute-start | bytes 1493000 | tf_op jit(solution)/shard_map/ppermute | solution.py:542
  393.4 29.5 %collective-permute-start.56 = (bf16[2,288,576]{2,1,0:T(8,128)(2,1)S(1)}, bf16[2,288,576]{2,1,0:T(8,128)(2,1)}, u32[]{:S(2)}, u32[]{:S(2)}) collective-permute-start(bf16[2,288,576]{2,1,0:T(8,128)(2,1)S(1)} %add_convert_fusion.5), channel_id=1, source_target_pairs={{0,0},{1,1},{2,18},{3,19},{4,12},{5,13},{6,30},{7,31},{8,16},{9,17... | collective-permute-start | bytes 1990664 | tf_op jit(solution)/shard_map/ppermute | solution.py:730
  416.0 25.2 %collective-permute-start.50 = (bf16[3,1,144,288]{3,2,1,0:T(8,128)(2,1)}, bf16[3,1,144,288]{3,2,1,0:T(8,128)(2,1)}, u32[]{:S(2)}, u32[]{:S(2)}) collective-permute-start(bf16[3,1,144,288]{3,2,1,0:T(8,128)(2,1)} %broadcast_select_fusion.13), channel_id=1, source_target_pairs={{0,4},{1,5},{2,6},{3,7},{4,0},{5,1},{6,2},{7,3},{8,12},{9,13},{10,... | collective-permute-start | bytes 746504 | tf_op jit(solution)/shard_map/ppermute | solution.py:542
  422.9 40.6 %collective-permute-start.57 = (bf16[2,288,576]{2,1,0:T(8,128)(2,1)}, bf16[2,288,576]{2,1,0:T(8,128)(2,1)}, u32[]{:S(2)}, u32[]{:S(2)}) collective-permute-start(bf16[2,288,576]{2,1,0:T(8,128)(2,1)} %collective-permute-done.56), channel_id=1, source_target_pairs={{0,0},{1,1},{2,2},{3,3},{4,4},{5,5},{6,6},{7,7},{8,12},{9,13},{10,... | collective-permute-start | bytes 1990664 | tf_op jit(solution)/shard_map/ppermute | solution.py:731
  (120 other events, 991.1 us)

commit v4 on v3

--- a/solution.py
+++ b/solution.py
@@ -64,30 +64,20 @@
     return lax.optimization_barrier(arrays)
 
 
-def after(array, *others):
-    return lax.optimization_barrier((array, *others))[0]
-
-
-def gather_parts(part, axis, count, *waits):
+def gather_parts(part, axis, count):
     held = part[None]
     for bit in reversed(bits_up(count)):
-        came = lax.ppermute(held, axis, xor_perm(count, bit))
-        if waits and held.shape[0] == 1:
-            came = after(came, *waits)
-        held = jnp.concatenate([held, came])
+        held = jnp.concatenate([held, lax.ppermute(held, axis, xor_perm(count, bit))])
     return held
 
 
-def gather_stack(part, axis, count, bits=None):
-    held, order = part[None], [0]
-    for bit in bits or reversed(bits_up(count)):
-        held = jnp.concatenate([held, lax.ppermute(held, axis, xor_perm(count, bit))])
-        order = order + [mask ^ bit for mask in order]
-    return jnp.stack([held[order.index(mask)] for mask in range(count)])
-
-
-def gather_all(part, axis, count, bits=None):
-    return xor_shuffle(gather_stack(part, axis, count, bits), lax.axis_index(axis))
+def gather_stack(part, axis, count):
+    held = gather_parts(part, axis, count)
+    return jnp.stack([held[reverse_bits(mask, count)] for mask in range(count)])
+
+
+def gather_all(part, axis, count):
+    return xor_shuffle(gather_stack(part, axis, count), lax.axis_index(axis))
 
 
 def mask_order(count):
@@ -98,42 +88,23 @@
 
 
 def scatter_first(near, far, axis, count):
-    return near.astype(F32) + lax.ppermute(far, axis, xor_perm(count, 1)).astype(F32)
-
-
-def scatter_rest(held, axis, count, *waits):
+    came = lax.ppermute(far, axis, xor_perm(count, 1))
+    half = near.shape[0] // 2
+    sent = (near[half:].astype(F32) + came[half:].astype(F32)).astype(BF16)
+    sent, near, came = together(sent, near, came)
+    return sent, near[:half].astype(F32) + came[:half].astype(F32)
+
+
+def scatter_rest(sent, held, axis, count):
     for bit in bits_up(count)[1:]:
+        held = held + lax.ppermute(sent, axis, xor_perm(count, bit)).astype(F32)
         half = held.shape[0] // 2
-        came = lax.ppermute(held[half:].astype(BF16), axis, xor_perm(count, bit))
-        if waits and half == 1:
-            came = after(came, *waits)
-        held = held[:half] + came.astype(F32)
+        sent, held = held[half:].astype(BF16), held[: max(half, 1)]
     return held[0]
 
 
-def scatter_sum(near, far, axis, count, *waits):
-    return scatter_rest(scatter_first(near, far, axis, count), axis, count, *waits)
-
-
-def exchange(parts, axis, count):
-    held = xor_shuffle(parts, lax.axis_index(axis))[None]
-    for bit in reversed(bits_up(count)):
-        half = held.shape[1] // 2
-        came = lax.ppermute(held[:, half:], axis, xor_perm(count, bit))
-        held = jnp.concatenate([held[:, :half], came])
-    return held[:, 0]
-
-
-def scatter_blocks(parts, axis, count):
-    me = lax.axis_index(axis)
-    held = parts
-    for at, bit in enumerate(bits_up(count)):
-        held = held.reshape((-1, 2) + parts.shape[1:])
-        mine = (me >> at) & 1
-        held = pick(held, mine, 1) + lax.ppermute(
-            pick(held, mine ^ 1, 1), axis, xor_perm(count, bit)
-        )
-    return held[0]
+def scatter_sum(near, far, axis, count):
+    return scatter_rest(*scatter_first(near, far, axis, count), axis, count)
 
 
 def attend_kernel(piece, facts_ref, q_ref, k_ref, v_ref, out_ref, prob_ref):
@@ -172,7 +143,7 @@
 def attend(queries, keys, values, facts, piece):
     heads, depth, count = queries.shape
     keys_len = keys.shape[2]
-    lanes = min(512, count)
+    lanes = min(count, (1 << 20) // keys_len)
     chunk = lambda head, step, facts: (head, 0, step)
     whole = lambda head, step, facts: (head, 0, 0)
     return pl.pallas_call(
@@ -236,7 +207,7 @@
 def attend_back(queries, keys, values, attended, grad, prob):
     heads, depth, count = queries.shape
     keys_len = keys.shape[2]
-    lanes = min(512, count)
+    lanes = min(count, (1 << 20) // keys_len)
     chunk = lambda head, step: (head, 0, step)
     whole = lambda head, step: (head, 0, 0)
     return pl.pallas_call(
@@ -367,11 +338,11 @@
     facts = jnp.concatenate([lengths, cond_index], axis=1)
     facts_own = lax.ppermute(pick(facts, my_slot), both, outward[0])
     tokens_sent = [pick(tokens, my_slot ^ turn) for turn in range(rows_dev)]
+    slot_to = [[(3 * d + slot) % dp for d in range(dp)] for slot in range(3)]
+    w_qkv, tokens_sent = together(w_qkv, tokens_sent)
     tokens_own = jnp.stack(
         [lax.ppermute(part, both, outward[turn]) for turn, part in enumerate(tokens_sent)]
     )
-    slot_to = [[(3 * d + slot) % dp for d in range(dp)] for slot in range(3)]
-    w_qkv = after(w_qkv, tokens_sent)
     w_slots = [w_qkv.T[slot * head_width : (slot + 1) * head_width] for slot in range(3)]
     stay = [[d == to for d, to in enumerate(target)] for target in slot_to]
     if all(first != last for first, last in zip(stay[0], stay[2], strict=True)):
@@ -394,20 +365,22 @@
         w_slots = [
             lax.ppermute(w_slots[slot], "dp", list(enumerate(slot_to[slot]))) for slot in range(3)
         ]
+    image_ends, index_own = jnp.cumsum(facts_own[:images]), facts_own[images:]
+    classes = jnp.arange(cond_table.shape[0], dtype=jnp.int32)
+
+    def conditions(index):
+        return dot((index[:, None] == classes[None]).astype(BF16), cond_table)
+
+    silu_own = jax.nn.silu(conditions(index_own)).astype(BF16)
+    mod_part = dot(silu_own, w_mod) + cut(b_mod, me * mod_width, mod_width)
+    w_out, w_down, mod_part = together(w_out, w_down, mod_part)
+    modulation = gather_stack(mod_part, "dp", dp)
     row_blocks = jnp.concatenate(
         [jnp.stack(jnp.split(member.T, dp, axis=1)) for member in (w_down, w_out)], axis=2
     )
-
-    image_ends = jnp.cumsum(facts_own[:images])
-    classes = jnp.arange(cond_table.shape[0], dtype=jnp.int32)
-
-    def conditions(index):
-        return dot((index[:, None] == classes[None]).astype(BF16), cond_table)
-
-    silu_own = jax.nn.silu(conditions(facts_own[images:])).astype(BF16)
-    mod_part = dot(after(silu_own, slots_sent), w_mod) + cut(b_mod, me * mod_width, mod_width)
-    modulation = gather_stack(mod_part, "dp", dp)
-    tokens_own, w_slots, modulation = together(tokens_own, w_slots, modulation)
+    tokens_own, w_slots, modulation, row_blocks, cotangent = together(
+        tokens_own, w_slots, modulation, row_blocks, cotangent
+    )
     modulation = xor_shuffle(modulation, me)
     seg_all = jnp.sum(
         (image_ends[None, None] <= piece_first[..., None]).astype(jnp.int32), axis=-1
@@ -427,7 +400,10 @@
         return gather_parts(own, "dp", dp, *waits).reshape((-1,) + own.shape[1:])
 
     tokens_all = gather_tokens(tokens_own)
-    cotangent, row_blocks, _ = together(cotangent, row_blocks, tokens_own)
+    row_parts = {
+        mask: lax.ppermute(pick(row_blocks, me ^ mask), "dp", xor_perm(dp, mask))
+        for mask in range(2, dp)
+    }
     slot_of = [lax.rem(me + kind * (dp % 3), 3) for kind in range(3)]
     w_heads = jnp.concatenate(
         [
@@ -452,11 +428,8 @@
     cotangent_own = to_groups(cotangent)
     count = hidden_a_all.shape[0]
     half = count // 2
-    row_parts = {
-        2: lax.ppermute(after(pick(row_blocks, me ^ 2), tokens_all), "dp", xor_perm(dp, 2))
-    }
     projected = (dot(w_heads, hidden_a_all, 1, 1) + bias_heads[:, None]).astype(BF16)
-    projected, row_parts = together(projected, row_parts)
+    projected, row_blocks = together(projected, row_blocks)
     projected = projected.reshape(3, heads, HD, count)
     queries, keys, values = projected[0], projected[1], projected[2]
     seg_row = seg_all
@@ -471,13 +444,8 @@
     one_image = jnp.all(seg_row == seg_row[0]).astype(jnp.int32)
     attend_facts = jnp.concatenate([one_image[None], seg_row, seg_all])
     attended, prob_low = attend(queries, keys, values, attend_facts, piece)
-    row_blocks = after(row_blocks, projected)
     row_parts[0] = pick(row_blocks, me)
-    for mask in range(1, dp):
-        if mask != 2:
-            row_parts[mask] = lax.ppermute(
-                pick(row_blocks, me ^ mask), "dp", xor_perm(dp, mask)
-            )
+    row_parts[1] = lax.ppermute(pick(row_blocks, me ^ 1), "dp", xor_perm(dp, 1))
     attended, cotangent_own, row_parts = together(attended, cotangent_own, row_parts)
     attended = attended.reshape(head_width, count)
     row_parts = jnp.stack([row_parts[mask] for mask in range(dp)])
@@ -492,15 +460,17 @@
     far_half, near_half = products(
         lambda part: dot(part, w_out_rows, 0, 1), lambda low, high: attended[:, low:high]
     )
+    far_half, row_parts = together(far_half, row_parts)
     branch = scatter_sum(near_half, far_half, "dp", dp) + b_out
     middle = tokens_own.astype(F32) + gate_a * branch
     norm_b, spread_b = layer_norm(middle)
     hidden_b = (norm_b * (1.0 + scale_b) + shift_b).astype(BF16)
-    row_parts, _ = together(row_parts, far_half)
     w_down_rows = jnp.concatenate(list(xor_shuffle(row_parts[:, :, :hidden_width], me)))
+    hidden_b, w_down_rows = together(hidden_b, w_down_rows)
     hidden_b_all = gather_tokens(hidden_b).reshape(count, width)
 
-    cotangent_all = gather_tokens(after(cotangent_own, hidden_b_all))
+    cotangent_own, hidden_b_all = together(cotangent_own, hidden_b_all)
+    cotangent_all = gather_tokens(cotangent_own)
     grad_output = cotangent_own.astype(F32)
     b_up_own = cut(b_up, me * hidden_width, hidden_width)
     pre_act = dot(hidden_b_all, w_up) + b_up_own
@@ -509,20 +479,18 @@
     far_mlp, near_mlp = products(
         lambda part: dot(part, w_down_rows, 1, 1), lambda low, high: activated[low:high]
     )
-    mlp_out = scatter_first(near_mlp, far_mlp, "dp", dp)
-    cotangent_all, mlp_out = together(cotangent_all, mlp_out)
+    mlp_sent, mlp_held = scatter_first(near_mlp, far_mlp, "dp", dp)
+    cotangent_all, mlp_sent = together(cotangent_all, mlp_sent)
     grad_mlp_all = (gate_b_all * cotangent_all.astype(F32)).astype(BF16).reshape(count, width)
-    mlp_out = scatter_rest(mlp_out, "dp", dp) + b_down
+    mlp_out = scatter_rest(mlp_sent, mlp_held, "dp", dp) + b_down
     grad_act = dot(grad_mlp_all, w_down_rows)
     grad_pre = (grad_act * slope.astype(F32)).astype(BF16)
     far_half, near_half = products(
         lambda part: dot(part, w_up, 1, 1), lambda low, high: grad_pre[low:high]
     )
-    grad_hidden_b = scatter_first(near_half, far_half, "dp", dp)
-    mlp_out, grad_hidden_b, near_half, grad_pre, activated = together(
-        mlp_out, grad_hidden_b, near_half, grad_pre, activated
-    )
-    grad_hidden_b = scatter_rest(grad_hidden_b, "dp", dp)
+    sent, grad_hidden_b = scatter_first(near_half, far_half, "dp", dp)
+    mlp_out, sent, grad_pre, activated = together(mlp_out, sent, grad_pre, activated)
+    grad_hidden_b = scatter_rest(sent, grad_hidden_b, "dp", dp)
     stages = log2(band)
     near_first = list(range(stages))
 
@@ -568,28 +536,24 @@
     up_far, down_far = halves(up_far, 0), halves(down_far, 0)
     up_came = [send(up_far[0], near_bits[0])]
     down_came = [send(down_far[0], first_far)]
-    grad_hidden_b = after(grad_hidden_b, up_came[0], down_came[0])
-    up_came.append(send(after(up_far[1], grad_hidden_b), near_bits[0]))
-    down_came.append(send(after(down_far[1], grad_hidden_b), first_far))
+    up_came, up_far = together(up_came, up_far[1])
+    down_came, down_far = together(down_came, down_far[1])
+    up_came.append(send(up_far, near_bits[0]))
+    down_came.append(send(down_far, first_far))
 
     grad_middle = grad_output + layer_norm_back(grad_hidden_b * (1.0 + scale_b), norm_b, spread_b)
     grad_branch = (gate_a * grad_middle).astype(BF16)
-    grad_branch_all = gather_tokens(grad_branch, up_came[1], down_came[1]).reshape(count, width)
-    middle, mlp_out, _ = together(middle, mlp_out, grad_branch)
+    middle, mlp_out, grad_branch = together(middle, mlp_out, grad_branch)
+    grad_branch_all = gather_tokens(grad_branch).reshape(count, width)
     output = (middle + gate_b * mlp_out).astype(BF16)
+    output, grad_branch_all = together(output, grad_branch_all)
+    output_came = [
+        lax.ppermute(output[turn], both, inward[turn]) for turn in range(rows_dev)
+    ]
     up_mine, up_far = choose(joined(up_mine, jnp.concatenate(up_came)), 0, first_far)
     down_mine, down_far = choose(joined(down_mine, jnp.concatenate(down_came)), 1, near_bits[0])
     up_came, down_came = send(up_far, first_far), send(down_far, near_bits[0])
     grad_attended = dot(w_out_rows, grad_branch_all, 0, 1).astype(BF16)
-    out_mine, out_far = choose(
-        dot(grad_branch_all, attended, 0, 1)
-        .astype(BF16)
-        .reshape((2,) * stages + (unit, head_width)),
-        stages - 1,
-        0,
-        plain=True,
-    )
-    out_came = send(out_far, 0)
     grad_q, grad_k, grad_v = attend_back(
         queries,
         keys,
@@ -608,37 +572,36 @@
     grad_heads = jnp.concatenate(
         [member.reshape(head_width, count) for member in (grad_q, grad_k, grad_v)]
     )
-    output_came = [
-        lax.ppermute(after(output[turn], grad_branch_all), both, inward[turn])
-        for turn in range(rows_dev - 1)
-    ]
-    grad_heads, up_came, down_came, out_came, output_came = together(
-        grad_heads, up_came, down_came, out_came, output_came
-    )
+    grad_heads, up_came, down_came = together(grad_heads, up_came, down_came)
     far_half, near_half = products(
         lambda part: dot(part, w_heads, 0, 0), lambda low, high: grad_heads[:, low:high]
     )
-    grad_hidden_a = scatter_first(near_half, far_half, "dp", dp)
-    out_came, grad_heads, near_half, far_half, _ = together(
-        out_came, grad_heads, near_half, far_half, grad_hidden_a
-    )
-    grad_hidden_a = scatter_rest(grad_hidden_a, "dp", dp)
-    up_mine, up_came, down_mine, down_came, _ = together(
-        up_mine, up_came, down_mine, down_came, near_half
-    )
+    sent, grad_hidden_a = scatter_first(near_half, far_half, "dp", dp)
+    attended, grad_heads, near_half, far_half, sent, up_came, down_came, output_came = together(
+        attended, grad_heads, near_half, far_half, sent, up_came, down_came, output_came
+    )
+    output = xor_shuffle(jnp.stack(output_came), my_slot)
+    grad_hidden_a = scatter_rest(sent, grad_hidden_a, "dp", dp)
     up_down = jnp.stack([joined(up_mine, up_came), joined(down_mine, down_came)])
     up_down_rest = [2] * (len(near_bits) - 1) + [1] * (len(far_bits) - 1), near_bits[1:] + far_bits[1:]
     up_down_mine, up_down_far = choose(up_down, up_down_rest[0][0], up_down_rest[1][0])
+    up_down_far, grad_heads, attended = together(up_down_far, grad_heads, attended)
     up_down_came = send(up_down_far, up_down_rest[1][0])
     grad_w_heads = dot(grad_heads, hidden_a_all).astype(BF16).reshape(3, across, unit, width)
     qkv_axes = [1] * log2(across) + [3] * log2(dp)
     qkv_mine, qkv_far = choose(grad_w_heads, qkv_axes[0], near_first[0])
+    near_half, far_half, qkv_far, attended = together(near_half, far_half, qkv_far, attended)
     qkv_came = send(qkv_far, near_first[0])
-    output_came = output_came + [
-        lax.ppermute(after(output[-1], grad_heads), both, inward[rows_dev - 1])
-    ]
-    out_half = joined(out_mine, out_came)
-    near_half, far_half, _ = together(near_half, far_half, (qkv_far, up_down_far))
+    out_bits = [far_bits[0]] + near_bits + far_bits[1:]
+    out_mine, out_far = choose(
+        dot(grad_branch_all, attended, 0, 1)
+        .astype(BF16)
+        .reshape((2,) * stages + (unit, head_width)),
+        stages - 1 - out_bits[0],
+        out_bits[0],
+        plain=True,
+    )
+    out_came = send(out_far, out_bits[0])
 
     hot_tokens = jnp.broadcast_to(
         hot_all.T.astype(BF16)[:, :, None], (images, hot_all.shape[0], piece)
@@ -667,7 +630,9 @@
         axis=1,
     )
     grad_mod = jnp.transpose(grad_mod.reshape(images, dp, mod_width), (1, 0, 2))
-    grad_mod_own = jnp.sum(lax.all_to_all(grad_mod, "dp", 0, 0, tiled=True), axis=0)
+    grad_mod_came = lax.all_to_all(grad_mod, "dp", 0, 0, tiled=True)
+    grad_mod_came, qkv_came = together(grad_mod_came, qkv_came)
+    grad_mod_own = jnp.sum(grad_mod_came, axis=0)
     high = grad_mod_own.astype(BF16)
     low = (grad_mod_own - high.astype(F32)).astype(BF16)
     grad_silu = dot(jnp.concatenate([high, low], axis=0), w_mod, 1, 1)
@@ -681,28 +646,37 @@
     ]
     assert images >= len(bias_rows)
     bias_rows = [
-        jnp.pad(member, (0, width - member.shape[0])) for member in bias_rows
-    ] + [jnp.zeros((width,), F32)] * (images - len(bias_rows))
-    packed = jnp.concatenate([grad_mod_own, grad_silu, jnp.stack(bias_rows)], axis=1)
-    grad_hidden_a, output_came, packed = together(grad_hidden_a, output_came, packed)
-    output = xor_shuffle(jnp.stack(output_came), my_slot)
+        jnp.pad(member, (0, width + 128 - member.shape[0])) for member in bias_rows
+    ] + [jnp.zeros((width + 128,), F32)] * (images - len(bias_rows))
+    bias_rows = jnp.stack(bias_rows) + jnp.pad(
+        index_own.astype(F32)[:, None], ((0, 0), (width, 127))
+    )
+    packed = jnp.concatenate([grad_mod_own, grad_silu, bias_rows], axis=1)
+    grad_hidden_a, packed = together(grad_hidden_a, packed)
+    qkv_mine, qkv_far = choose(joined(qkv_mine, qkv_came), qkv_axes[1], near_first[1])
     inputs = tokens_own.astype(F32)
     norm_a, spread_a = layer_norm(inputs)
     grad_tokens = grad_middle + layer_norm_back(grad_hidden_a * (1.0 + scale_a), norm_a, spread_a)
     grad_tokens = grad_tokens.astype(BF16)
+    packed, grad_tokens = together(packed, grad_tokens)
+    held, masks = packed[None], [0]
+    for bit in far_bits + near_bits:
+        if bit == near_bits[0]:
+            held, grad_tokens, qkv_far, out_came = together(held, grad_tokens, qkv_far, out_came)
+        held = jnp.concatenate([held, lax.ppermute(held, "band", xor_perm(band, 1 << bit))])
+        masks = masks + [mask ^ (1 << bit) for mask in masks]
+    packed = xor_shuffle(jnp.stack([held[masks.index(mask)] for mask in range(band)]), group)
     grad_tokens_came = [
         lax.ppermute(grad_tokens[turn], both, inward[turn]) for turn in range(rows_dev)
     ]
-    packed, _ = together(packed, grad_tokens)
-    packed = gather_all(packed, "band", band, [1 << bit for bit in far_bits + near_bits])
-    packed, qkv_came, up_down_came, out_half = together(
-        packed, qkv_came, up_down_came, out_half
-    )
-    qkv_half = joined(qkv_mine, qkv_came)
-    qkv_mine, qkv_far = choose(qkv_half, qkv_axes[1], near_first[1])
     qkv_came = send(qkv_far, near_first[1])
-    out_mine, out_far = choose(out_half, stages - 2, near_first[1], plain=True)
-    out_came = send(out_far, near_first[1])
+    out_mine, out_far = choose(
+        joined(out_mine, out_came), stages - 1 - out_bits[1], out_bits[1], plain=True
+    )
+    out_came = send(out_far, out_bits[1])
+    packed, qkv_came, up_down_came, out_came, grad_tokens_came = together(
+        packed, qkv_came, up_down_came, out_came, grad_tokens_came
+    )
     up_down = sum_groups(
         joined(up_down_mine, up_down_came), up_down_rest[0][1:], up_down_rest[1][1:]
     )
@@ -716,20 +690,24 @@
     final_pack = jnp.concatenate(
         [
             grad_silu_groups.reshape(rows * images, width),
-            jnp.sum(packed[:, :, mod_width + width :], axis=0),
+            jnp.sum(packed[:, :, mod_width + width : mod_width + 2 * width], axis=0),
             mod_sum,
         ]
     )
     qkv_sum = sum_groups(joined(qkv_mine, qkv_came), qkv_axes[2:], near_first[2:])
     qkv_sum = qkv_sum.reshape(3, unit, head_width)
     out_sum = sum_groups(
-        joined(out_mine, out_came), list(reversed(range(stages - 2))), near_first[2:], plain=True
+        joined(out_mine, out_came),
+        [stages - 1 - bit for bit in out_bits[2:]],
+        out_bits[2:],
+        plain=True,
     )
     final_out = out_sum.reshape(unit, head_width).T.astype(F32)
     final_pack = gather_all(final_pack, "dp", dp)
     up_down = lax.ppermute(up_down, both, owner_pairs(lambda d, b, block, unit: block * band + b))
+    up_down, qkv_sum = together(up_down, qkv_sum)
     up_down = lax.ppermute(
-        after(up_down, qkv_sum),
+        up_down,
         both,
         [
             (d * band + b, d * band + ((b // across) ^ reverse_bits(d, dp)) * across + reverse_bits(b % across, across))
@@ -777,10 +755,8 @@
         )
     final_qkv = jnp.concatenate(final_qkv).T.astype(F32)
 
-    facts_all = gather_stack(after(facts, hidden_a_all), "dp", dp)
-    facts_all = jnp.stack([facts_all[mask] for mask in order])
-    index_all = xor_shuffle(facts_all, me_turned).reshape(rows, 2 * images)[:, images:].reshape(-1)
-    condition = conditions(after(index_all, grad_branch))
+    index_all = packed[::spans, :, mod_width + 2 * width].reshape(-1).astype(jnp.int32)
+    condition = conditions(index_all)
     silu_all = jax.nn.silu(condition).astype(BF16)
     silu_rows = rows * images
     grad_silu_rows = jnp.sum(final_pack[:, :silu_rows], axis=0)

time: 475 us -> 457 us (0.962)
  the two profiles are of different devices: /device:TPU:1 before, /device:TPU:24 now
where the time goes in v4:
time: 457 us; the launch traced here: 450 us
  waiting for transfers between devices  157 us (34%)
  starting transfers between devices  89.9 us (20%)
  other arithmetic  83.8 us (18%)
  matrix products  52.7 us (12%)
  local copies, waits for them, and re-layouts  38.8 us (8%)
  Pallas kernels  24.5 us (5%)
    ppermute x12, waiting for transfers between devices, gather_parts(): lax.ppermute(held, axis, xor_perm(count, bit))  52.6 us
    dot_general x25, matrix products, dot(): lax.dot_general(left, right, (((left_dim,), (right_dim,)), ((), ())), pre...  46.4 us
    ppermute x13, waiting for transfers between devices, send(): return lax.ppermute(part, 'band', xor_perm(band, 1 << bit))  33.7 us
    ppermute x4, waiting for transfers between devices, scatter_rest(): held = held + lax.ppermute(sent, axis, xor_perm(count, bit)).astype(F32)  25.4 us
    ppermute x12, starting transfers between devices, gather_parts(): lax.ppermute(held, axis, xor_perm(count, bit))  15.3 us
    ppermute x3, waiting for transfers between devices, shards(): lax.ppermute(held, 'band', xor_perm(band, 1 << bit))  13.2 us
    ppermute x3, waiting for transfers between devices, shards(): lax.ppermute(pick(qkv_sum, kind), both, owner_pairs(owner))  12.8 us
    pallas_call x1, Pallas kernels, attend(): pl.pallas_call(functools.partial(attend_kernel, piece), grid_spec=pltpu.P...  12.4 us
  transfers between devices with their start and end apart: 57, of which 28 were waited for; matrix products, arithmetic and copies ran while one was open for 30% of the time, Pallas kernels for 5%

profile of v4, /device:TPU:24, one launch (start us, length us, event | category | flops | bytes accessed | tf_op | source)
XLA Modules:
  0.0 450.5 jit_solution(2416484699874795378)
XLA Ops:
  5.9 5.7 %collective-permute-start.1 = (bf16[128,1152]{1,0:T(8,128)(2,1)}, bf16[128,1152]{1,0:T(8,128)(2,1)}, u32[]{:S(2)}, u32[]{:S(2)}) collective-permute-start(bf16[128,1152]{1,0:T(8,128)(2,1)} %get-tuple-element.112), channel_id=1, source_target_pairs={{0,0},{1,16},{2,8},{3,24},{4,1},{5,17},{6,9},{7,25},{8,4},{9,20},{... | collective-permute-start | bytes 884744 | tf_op jit(solution)/shard_map/ppermute | solution.py:344
  17.1 4.3 convolution_add_fusion.3
  31.7 5.5 %collective-permute-done.5 = f32[1,4,1728]{2,1,0:T(4,128)S(1)} collective-permute-done((f32[1,4,1728]{2,1,0:T(4,128)S(1)}, f32[1,4,1728]{2,1,0:T(4,128)S(1)}, u32[]{:S(2)}, u32[]{:S(2)}) %collective-permute-start.5) | collective-permute-done | bytes 27680 | tf_op jit(solution)/shard_map/ppermute | solution.py:70
  55.4 18.5 %collective-permute-done.7 = bf16[1,2,128,1152]{3,2,1,0:T(8,128)(2,1)S(1)} collective-permute-done((bf16[1,2,128,1152]{3,2,1,0:T(8,128)(2,1)S(1)}, bf16[1,2,128,1152]{3,2,1,0:T(8,128)(2,1)S(1)}, u32[]{:S(2)}, u32[]{:S(2)}) %collective-permute-start.7) | collective-permute-done | bytes 589856 | tf_op jit(solution)/shard_map/ppermute | solution.py:70
  75.9 5.9 %collective-permute-start.8 = (bf16[2,2,128,1152]{3,2,1,0:T(8,128)(2,1)}, bf16[2,2,128,1152]{3,2,1,0:T(8,128)(2,1)}, u32[]{:S(2)}, u32[]{:S(2)}) collective-permute-start(bf16[2,2,128,1152]{3,2,1,0:T(8,128)(2,1)} %pad_maximum_fusion.7), channel_id=1, source_target_pairs={{0,8},{8,0},{16,24},{24,16},{1,9},{9,1},{17,25},{25,17},{2,10},{10... | collective-permute-start | bytes 3538952 | tf_op jit(solution)/shard_map/ppermute | solution.py:70
  99.1 12.4 %attend.1 = (bf16[4,72,1024]{2,1,0:T(8,128)(2,1)}, bf16[4,1024,1024]{2,1,0:T(8,128)(2,1)}) custom-call(s32[17]{0:T(128)} %pad_add_fusion.1.facts_ref, bf16[4,72,1024]{2,1,0:T(8,128)(2,1)} %bitcast.296, bf16[4,72,1024]{2,1,0:T(8,128)(2,1)} %bitcast.294, bf16[4,72,1024]{2,1,0:T(8,128)(2,1)} %bitcast.292), custom_call_target="tpu_custom_call" | custom-call | flops 16106127360 | bytes 8388608 | tf_op jit(solution)/shard_map/attend/pallas_call | solution.py:149
  121.2 6.1 %pad_maximum_fusion.1 = bf16[1152,1152]{1,0:T(8,128)(2,1)} fusion(bf16[288,1152]{1,0:T(8,128)(2,1)S(1)} %get-tuple-element.265, bf16[288,1152]{1,0:T(8,128)(2,1)S(1)} %get-tuple-element.266, bf16[288,1152]{1,0:T(8,128)(2,1)S(1)} %get-tuple-element.267, bf16[288,1152]{1,0:T(8,128)(2,1)S(1)} %get-tuple-element.264), kind=kLoop, calls=%fused_computation.31 | loop fusion | flops 10616832 | bytes 5308416 | tf_op jit(solution)/shard_map/concatenate | solution.py:468
  127.3 9.5 %collective-permute-done.15 = bf16[1,2,128,1152]{3,2,1,0:T(8,128)(2,1)S(1)} collective-permute-done((bf16[1,2,128,1152]{3,2,1,0:T(8,128)(2,1)S(1)}, bf16[1,2,128,1152]{3,2,1,0:T(8,128)(2,1)S(1)}, u32[]{:S(2)}, u32[]{:S(2)}) %collective-permute-start.15) | collective-permute-done | bytes 589856 | tf_op jit(solution)/shard_map/ppermute | solution.py:100
  144.0 11.4 %collective-permute-done.16 = bf16[1,2,128,1152]{3,2,1,0:T(8,128)(2,1)} collective-permute-done((bf16[1,2,128,1152]{3,2,1,0:T(8,128)(2,1)}, bf16[1,2,128,1152]{3,2,1,0:T(8,128)(2,1)}, u32[]{:S(2)}, u32[]{:S(2)}) %collective-permute-start.16) | collective-permute-done | bytes 589856 | tf_op jit(solution)/shard_map/ppermute | solution.py:70
  162.6 5.1 %add_convert_fusion = (bf16[1024,1152]{1,0:T(8,128)(2,1)S(1)}, bf16[1024,1152]{1,0:T(8,128)(2,1)S(1)}) fusion(f32[1152]{0:T(1024)S(1)} %copy-done.74, bf16[1024,1152]{1,0:T(8,128)(2,1)S(1)} %bitcast.284, bf16[1152,1152]{1,0:T(8,128)(2,1)S(1)} %copy-done), kind=kOutput, calls=%fused_computation.12 | convolution fusion | flops 2741501952 | bytes 9736704 | tf_op jit(solution)/shard_map/dot_general | solution.py:26
  169.9 8.0 %collective-permute-done.19 = bf16[1,2,128,1152]{3,2,1,0:T(8,128)(2,1)S(1)} collective-permute-done((bf16[1,2,128,1152]{3,2,1,0:T(8,128)(2,1)S(1)}, bf16[1,2,128,1152]{3,2,1,0:T(8,128)(2,1)S(1)}, u32[]{:S(2)}, u32[]{:S(2)}) %collective-permute-start.19) | collective-permute-done | bytes 589856 | tf_op jit(solution)/shard_map/ppermute | solution.py:70
  183.2 3.9 fusion.4
  192.5 5.4 %collective-permute-done.21 = bf16[1,2,128,1152]{3,2,1,0:T(8,128)(2,1)S(1)} collective-permute-done((bf16[1,2,128,1152]{3,2,1,0:T(8,128)(2,1)S(1)}, bf16[1,2,128,1152]{3,2,1,0:T(8,128)(2,1)S(1)}, u32[]{:S(2)}, u32[]{:S(2)}) %collective-permute-start.21) | collective-permute-done | bytes 589856 | tf_op jit(solution)/shard_map/ppermute | solution.py:100
  209.3 10.6 %collective-permute-done.23 = bf16[1,2,128,1152]{3,2,1,0:T(8,128)(2,1)S(1)} collective-permute-done((bf16[1,2,128,1152]{3,2,1,0:T(8,128)(2,1)S(1)}, bf16[1,2,128,1152]{3,2,1,0:T(8,128)(2,1)S(1)}, u32[]{:S(2)}, u32[]{:S(2)}) %collective-permute-start.23) | collective-permute-done | bytes 589856 | tf_op jit(solution)/shard_map/ppermute | solution.py:100
  227.2 9.1 %collective-permute-done.24 = bf16[1,2,128,1152]{3,2,1,0:T(8,128)(2,1)S(1)} collective-permute-done((bf16[1,2,128,1152]{3,2,1,0:T(8,128)(2,1)S(1)}, bf16[1,2,128,1152]{3,2,1,0:T(8,128)(2,1)S(1)}, u32[]{:S(2)}, u32[]{:S(2)}) %collective-permute-start.24) | collective-permute-done | bytes 589856 | tf_op jit(solution)/shard_map/ppermute | solution.py:70
  242.4 3.3 collective-permute-done.27
  251.1 12.0 %attend_back.1 = (bf16[4,72,1024]{2,1,0:T(8,128)(2,1)}, bf16[4,72,1024]{2,1,0:T(8,128)(2,1)}, bf16[4,72,1024]{2,1,0:T(8,128)(2,1)}) custom-call(bf16[4,72,1024]{2,1,0:T(8,128)(2,1)} %bitcast.297, bf16[4,72,1024]{2,1,0:T(8,128)(2,1)} %bitcast.295, bf16[4,72,1024]{2,1,0:T(8,128)(2,1)} %bitcast.293, bf16[4,72,1024]{2,1,0:T(8,128)(2,1)} %get-tuple-element.128.out_ref, ...), custom_call_target="tpu_custom_call" | custom-call | flops 16106127360 | bytes 8388608 | tf_op jit(solution)/shard_map/attend_back/pallas_call | solution.py:213
  268.9 5.3 %collective-permute-start.33 = (bf16[128,1152]{1,0:T(8,128)(2,1)S(1)}, bf16[128,1152]{1,0:T(8,128)(2,1)S(1)}, u32[]{:S(2)}, u32[]{:S(2)}) collective-permute-start(bf16[128,1152]{1,0:T(8,128)(2,1)S(1)} %get-tuple-element.311), channel_id=1, source_target_pairs={{0,0},{16,1},{8,2},{24,3},{1,4},{17,5},{9,6},{25,7},{4,8},{20,9},{... | collective-permute-start | bytes 884744 | tf_op jit(solution)/shard_map/ppermute | solution.py:551
  278.8 5.9 %collective-permute-done.33 = bf16[128,1152]{1,0:T(8,128)(2,1)S(1)} collective-permute-done((bf16[128,1152]{1,0:T(8,128)(2,1)S(1)}, bf16[128,1152]{1,0:T(8,128)(2,1)S(1)}, u32[]{:S(2)}, u32[]{:S(2)}) %collective-permute-start.33) | collective-permute-done | bytes 294944 | tf_op jit(solution)/shard_map/ppermute | solution.py:551
  288.1 4.1 collective-permute-start.35
  303.8 3.3 all-to-all-start
  318.1 18.4 %collective-permute-done.36 = bf16[3,1,144,1152]{3,2,1,0:T(8,128)(2,1)} collective-permute-done((bf16[3,1,144,1152]{3,2,1,0:T(8,128)(2,1)}, bf16[3,1,144,1152]{3,2,1,0:T(8,128)(2,1)}, u32[]{:S(2)}, u32[]{:S(2)}) %collective-permute-start.36) | collective-permute-done | bytes 995360 | tf_op jit(solution)/shard_map/ppermute | solution.py:510
  347.5 5.6 %collective-permute-done.38 = f32[2,4,4160]{2,1,0:T(4,128)S(1)} collective-permute-done((f32[2,4,4160]{2,1,0:T(4,128)S(1)}, f32[2,4,4160]{2,1,0:T(4,128)S(1)}, u32[]{:S(2)}, u32[]{:S(2)}) %collective-permute-start.38) | collective-permute-done | bytes 133152 | tf_op jit(solution)/shard_map/ppermute | solution.py:666
  356.7 6.0 %collective-permute-done.40 = f32[4,4,4160]{2,1,0:T(4,128)S(1)} collective-permute-done((f32[4,4,4160]{2,1,0:T(4,128)S(1)}, f32[4,4,4160]{2,1,0:T(4,128)S(1)}, u32[]{:S(2)}, u32[]{:S(2)}) %collective-permute-start.40) | collective-permute-done | bytes 266272 | tf_op jit(solution)/shard_map/ppermute | solution.py:666
  367.8 5.7 %collective-permute-done.45 = bf16[128,1152]{1,0:T(8,128)(2,1)S(1)} collective-permute-done((bf16[128,1152]{1,0:T(8,128)(2,1)S(1)}, bf16[128,1152]{1,0:T(8,128)(2,1)S(1)}, u32[]{:S(2)}, u32[]{:S(2)}) %collective-permute-start.45) | collective-permute-done | bytes 294944 | tf_op jit(solution)/shard_map/ppermute | solution.py:670
  373.5 4.3 collective-permute-done.44
  385.4 8.7 %collective-permute-start.48 = (f32[32,864]{1,0:T(8,128)S(1)}, f32[32,864]{1,0:T(8,128)S(1)}, u32[]{:S(2)}, u32[]{:S(2)}) collective-permute-start(f32[32,864]{1,0:T(8,128)S(1)} %constant_dynamic-slice_fusion.3), channel_id=1, source_target_pairs={{0,0},{1,1},{2,16},{3,17},{4,8},{5,9},{6,24},{7,25},{8,18},{9,19},... | collective-permute-start | bytes 331784 | tf_op jit(solution)/shard_map/ppermute | solution.py:777
  403.8 5.8 %collective-permute-done.50 = bf16[3,1,144,288]{3,2,1,0:T(8,128)(2,1)S(1)} collective-permute-done((bf16[3,1,144,288]{3,2,1,0:T(8,128)(2,1)S(1)}, bf16[3,1,144,288]{3,2,1,0:T(8,128)(2,1)S(1)}, u32[]{:S(2)}, u32[]{:S(2)}) %collective-permute-start.50) | collective-permute-done | bytes 248864 | tf_op jit(solution)/shard_map/ppermute | solution.py:510
  410.3 7.3 %collective-permute-start.55 = (bf16[2,288,576]{2,1,0:T(8,128)(2,1)}, bf16[2,288,576]{2,1,0:T(8,128)(2,1)}, u32[]{:S(2)}, u32[]{:S(2)}) collective-permute-start(bf16[2,288,576]{2,1,0:T(8,128)(2,1)} %collective-permute-done.49), channel_id=1, source_target_pairs={{0,0},{1,1},{2,2},{3,3},{4,4},{5,5},{6,6},{7,7},{8,12},{9,13},{10,... | collective-permute-start | bytes 1990664 | tf_op jit(solution)/shard_map/ppermute | solution.py:709
  417.6 4.3 fusion.33
  433.1 5.3 %collective-permute-done.52 = bf16[144,288]{0,1:T(8,128)(2,1)} collective-permute-done((bf16[144,288]{0,1:T(8,128)(2,1)}, bf16[144,288]{0,1:T(8,128)(2,1)}, u32[]{:S(2)}, u32[]{:S(2)}) %collective-permute-start.52) | collective-permute-done | bytes 82976 | tf_op jit(solution)/shard_map/ppermute | solution.py:754
  438.3 7.6 %collective-permute-done.53 = bf16[144,288]{0,1:T(8,128)(2,1)} collective-permute-done((bf16[144,288]{0,1:T(8,128)(2,1)}, bf16[144,288]{0,1:T(8,128)(2,1)}, u32[]{:S(2)}, u32[]{:S(2)}) %collective-permute-start.53) | collective-permute-done | bytes 82976 | tf_op jit(solution)/shard_map/ppermute | solution.py:754
  (473 shorter events, 213.1 us)
Async XLA Ops:
  5.9 36.3 %collective-permute-start.1 = (bf16[128,1152]{1,0:T(8,128)(2,1)}, bf16[128,1152]{1,0:T(8,128)(2,1)}, u32[]{:S(2)}, u32[]{:S(2)}) collective-permute-start(bf16[128,1152]{1,0:T(8,128)(2,1)} %get-tuple-element.112), channel_id=1, source_target_pairs={{0,0},{1,16},{2,8},{3,24},{4,1},{5,17},{6,9},{7,25},{8,4},{9,20},{... | collective-permute-start | bytes 884744 | tf_op jit(solution)/shard_map/ppermute | solution.py:344
  11.6 30.6 %collective-permute-start.2 = (bf16[128,1152]{1,0:T(8,128)(2,1)S(1)}, bf16[128,1152]{1,0:T(8,128)(2,1)}, u32[]{:S(2)}, u32[]{:S(2)}) collective-permute-start(bf16[128,1152]{1,0:T(8,128)(2,1)S(1)} %get-tuple-element.113), channel_id=1, source_target_pairs={{0,1},{1,17},{2,9},{3,25},{4,0},{5,16},{6,8},{7,24},{8,5},{9,21},{... | collective-permute-start | bytes 884744 | tf_op jit(solution)/shard_map/ppermute | solution.py:344
  13.9 26.1 %collective-permute-start.3 = (bf16[288,1152]{1,0:T(8,128)(2,1)}, bf16[288,1152]{1,0:T(8,128)(2,1)}, u32[]{:S(2)}, u32[]{:S(2)}) collective-permute-start(bf16[288,1152]{1,0:T(8,128)(2,1)} %broadcast_select_fusion.8), channel_id=1, source_target_pairs={{0,16},{8,24},{16,0},{24,8},{1,17},{9,25},{17,1},{25,9},{2,18},{10... | collective-permute-start | bytes 1990664 | tf_op jit(solution)/shard_map/ppermute | solution.py:353
  21.4 15.8 %collective-permute-start.5 = (f32[1,4,1728]{2,1,0:T(4,128)S(1)}, f32[1,4,1728]{2,1,0:T(4,128)S(1)}, u32[]{:S(2)}, u32[]{:S(2)}) collective-permute-start(f32[1,4,1728]{2,1,0:T(4,128)S(1)} %bitcast.305), channel_id=1, source_target_pairs={{0,16},{8,24},{16,0},{24,8},{1,17},{9,25},{17,1},{25,9},{2,18},{10... | collective-permute-start | bytes 82952 | tf_op jit(solution)/shard_map/ppermute | solution.py:70
  45.1 37.4 %collective-permute-start.9 = (bf16[128,1152]{1,0:T(8,128)(2,1)}, bf16[128,1152]{1,0:T(8,128)(2,1)}, u32[]{:S(2)}, u32[]{:S(2)}) collective-permute-start(bf16[128,1152]{1,0:T(8,128)(2,1)} %get-tuple-element.312), channel_id=1, source_target_pairs={{0,0},{1,16},{2,8},{3,24},{4,1},{5,17},{6,9},{7,25},{8,4},{9,20},{... | collective-permute-start | bytes 884744 | tf_op jit(solution)/shard_map/ppermute | solution.py:318
  47.2 35.3 %collective-permute-start.10 = (bf16[128,1152]{1,0:T(8,128)(2,1)}, bf16[128,1152]{1,0:T(8,128)(2,1)}, u32[]{:S(2)}, u32[]{:S(2)}) collective-permute-start(bf16[128,1152]{1,0:T(8,128)(2,1)} %get-tuple-element.313), channel_id=1, source_target_pairs={{0,1},{1,17},{2,9},{3,25},{4,0},{5,16},{6,8},{7,24},{8,5},{9,21},{... | collective-permute-start | bytes 884744 | tf_op jit(solution)/shard_map/ppermute | solution.py:318
  50.1 23.8 %collective-permute-start.7 = (bf16[1,2,128,1152]{3,2,1,0:T(8,128)(2,1)S(1)}, bf16[1,2,128,1152]{3,2,1,0:T(8,128)(2,1)S(1)}, u32[]{:S(2)}, u32[]{:S(2)}) collective-permute-start(bf16[1,2,128,1152]{3,2,1,0:T(8,128)(2,1)S(1)} %bitcast.247), channel_id=1, source_target_pairs={{0,16},{8,24},{16,0},{24,8},{1,17},{9,25},{17,1},{25,9},{2,18},{10... | collective-permute-start | bytes 1769480 | tf_op jit(solution)/shard_map/ppermute | solution.py:70
  52.4 59.1 %collective-permute-start.13 = (bf16[288,1440]{1,0:T(8,128)(2,1)}, bf16[288,1440]{1,0:T(8,128)(2,1)}, u32[]{:S(2)}, u32[]{:S(2)}) collective-permute-start(bf16[288,1440]{1,0:T(8,128)(2,1)} %get-tuple-element.260), channel_id=1, source_target_pairs={{0,24},{8,16},{16,8},{24,0},{1,25},{9,17},{17,9},{25,1},{2,26},{10... | collective-permute-start | bytes 2488328 | tf_op jit(solution)/shard_map/ppermute | solution.py:404
  52.4 59.5 %collective-permute-start.12 = (bf16[288,1440]{1,0:T(8,128)(2,1)}, bf16[288,1440]{1,0:T(8,128)(2,1)}, u32[]{:S(2)}, u32[]{:S(2)}) collective-permute-start(bf16[288,1440]{1,0:T(8,128)(2,1)} %get-tuple-element.261), channel_id=1, source_target_pairs={{0,16},{8,24},{16,0},{24,8},{1,17},{9,25},{17,1},{25,9},{2,18},{10... | collective-permute-start | bytes 2488328 | tf_op jit(solution)/shard_map/ppermute | solution.py:404
  121.1 15.7 %collective-permute-start.15 = (bf16[1,2,128,1152]{3,2,1,0:T(8,128)(2,1)S(1)}, bf16[1,2,128,1152]{3,2,1,0:T(8,128)(2,1)S(1)}, u32[]{:S(2)}, u32[]{:S(2)}) collective-permute-start(bf16[1,2,128,1152]{3,2,1,0:T(8,128)(2,1)S(1)} %fusion.23), channel_id=1, source_target_pairs={{0,16},{8,24},{16,0},{24,8},{1,17},{9,25},{17,1},{25,9},{2,18},{10... | collective-permute-start | bytes 1769480 | tf_op jit(solution)/shard_map/ppermute | solution.py:100
  140.2 15.1 %collective-permute-start.16 = (bf16[1,2,128,1152]{3,2,1,0:T(8,128)(2,1)}, bf16[1,2,128,1152]{3,2,1,0:T(8,128)(2,1)}, u32[]{:S(2)}, u32[]{:S(2)}) collective-permute-start(bf16[1,2,128,1152]{3,2,1,0:T(8,128)(2,1)} %bitcast.56), channel_id=1, source_target_pairs={{0,16},{8,24},{16,0},{24,8},{1,17},{9,25},{17,1},{25,9},{2,18},{10... | collective-permute-start | bytes 1769480 | tf_op jit(solution)/shard_map/ppermute | solution.py:70
  162.0 15.8 %collective-permute-start.19 = (bf16[1,2,128,1152]{3,2,1,0:T(8,128)(2,1)S(1)}, bf16[1,2,128,1152]{3,2,1,0:T(8,128)(2,1)S(1)}, u32[]{:S(2)}, u32[]{:S(2)}) collective-permute-start(bf16[1,2,128,1152]{3,2,1,0:T(8,128)(2,1)S(1)} %bitcast.252), channel_id=1, source_target_pairs={{0,16},{8,24},{16,0},{24,8},{1,17},{9,25},{17,1},{25,9},{2,18},{10... | collective-permute-start | bytes 1769480 | tf_op jit(solution)/shard_map/ppermute | solution.py:70
  182.1 15.8 %collective-permute-start.21 = (bf16[1,2,128,1152]{3,2,1,0:T(8,128)(2,1)S(1)}, bf16[1,2,128,1152]{3,2,1,0:T(8,128)(2,1)S(1)}, u32[]{:S(2)}, u32[]{:S(2)}) collective-permute-start(bf16[1,2,128,1152]{3,2,1,0:T(8,128)(2,1)S(1)} %fusion.22), channel_id=1, source_target_pairs={{0,16},{8,24},{16,0},{24,8},{1,17},{9,25},{17,1},{25,9},{2,18},{10... | collective-permute-start | bytes 1769480 | tf_op jit(solution)/shard_map/ppermute | solution.py:100
  205.7 17.5 %collective-permute-start.29 = (bf16[288,1152]{1,0:T(8,128)(2,1)S(1)}, bf16[288,1152]{1,0:T(8,128)(2,1)S(1)}, u32[]{:S(2)}, u32[]{:S(2)}) collective-permute-start(bf16[288,1152]{1,0:T(8,128)(2,1)S(1)} %get-tuple-element.286), channel_id=1, source_target_pairs={{0,2},{1,3},{2,0},{3,1},{4,6},{5,7},{6,4},{7,5},{8,10},{9,11},{10,... | collective-permute-start | bytes 1990664 | tf_op jit(solution)/shard_map/ppermute | solution.py:510
  209.2 18.0 %collective-permute-start.26 = (bf16[576,576]{1,0:T(8,128)(2,1)S(1)}, bf16[576,576]{1,0:T(8,128)(2,1)S(1)}, u32[]{:S(2)}, u32[]{:S(2)}) collective-permute-start(bf16[576,576]{1,0:T(8,128)(2,1)S(1)} %get-tuple-element.284), channel_id=1, source_target_pairs={{0,1},{1,0},{2,3},{3,2},{4,5},{5,4},{6,7},{7,6},{8,9},{9,8},{10,11... | collective-permute-start | bytes 1990664 | tf_op jit(solution)/shard_map/ppermute | solution.py:510
  223.2 16.3 %collective-permute-start.30 = (bf16[288,1152]{1,0:T(8,128)(2,1)S(1)}, bf16[288,1152]{1,0:T(8,128)(2,1)S(1)}, u32[]{:S(2)}, u32[]{:S(2)}) collective-permute-start(bf16[288,1152]{1,0:T(8,128)(2,1)S(1)} %get-tuple-element.168), channel_id=1, source_target_pairs={{0,2},{1,3},{2,0},{3,1},{4,6},{5,7},{6,4},{7,5},{8,10},{9,11},{10,... | collective-permute-start | bytes 1990664 | tf_op jit(solution)/shard_map/ppermute | solution.py:510
  227.1 18.5 %collective-permute-start.27 = (bf16[576,576]{1,0:T(8,128)(2,1)S(1)}, bf16[576,576]{1,0:T(8,128)(2,1)S(1)}, u32[]{:S(2)}, u32[]{:S(2)}) collective-permute-start(bf16[576,576]{1,0:T(8,128)(2,1)S(1)} %get-tuple-element.165), channel_id=1, source_target_pairs={{0,1},{1,0},{2,3},{3,2},{4,5},{5,4},{6,7},{7,6},{8,9},{9,8},{10,11... | collective-permute-start | bytes 1990664 | tf_op jit(solution)/shard_map/ppermute | solution.py:510
  241.2 23.7 %collective-permute-start.31 = (bf16[576,576]{1,0:T(8,128)(2,1)}, bf16[576,576]{1,0:T(8,128)(2,1)}, u32[]{:S(2)}, u32[]{:S(2)}) collective-permute-start(bf16[576,576]{1,0:T(8,128)(2,1)} %broadcast_select_fusion.4), channel_id=1, source_target_pairs={{0,1},{1,0},{2,3},{3,2},{4,5},{5,4},{6,7},{7,6},{8,9},{9,8},{10,11... | collective-permute-start | bytes 1990664 | tf_op jit(solution)/shard_map/ppermute | solution.py:510
  247.8 17.0 %collective-permute-start.28 = (bf16[576,576]{1,0:T(8,128)(2,1)}, bf16[576,576]{1,0:T(8,128)(2,1)}, u32[]{:S(2)}, u32[]{:S(2)}) collective-permute-start(bf16[576,576]{1,0:T(8,128)(2,1)} %broadcast_select_fusion.5), channel_id=1, source_target_pairs={{0,2},{1,3},{2,0},{3,1},{4,6},{5,7},{6,4},{7,5},{8,10},{9,11},{10,... | collective-permute-start | bytes 1990664 | tf_op jit(solution)/shard_map/ppermute | solution.py:510
  268.9 15.8 %collective-permute-start.33 = (bf16[128,1152]{1,0:T(8,128)(2,1)S(1)}, bf16[128,1152]{1,0:T(8,128)(2,1)S(1)}, u32[]{:S(2)}, u32[]{:S(2)}) collective-permute-start(bf16[128,1152]{1,0:T(8,128)(2,1)S(1)} %get-tuple-element.311), channel_id=1, source_target_pairs={{0,0},{16,1},{8,2},{24,3},{1,4},{17,5},{9,6},{25,7},{4,8},{20,9},{... | collective-permute-start | bytes 884744 | tf_op jit(solution)/shard_map/ppermute | solution.py:551
  288.1 27.6 %collective-permute-start.35 = (bf16[1,2,128,1152]{3,2,1,0:T(8,128)(2,1)}, bf16[1,2,128,1152]{3,2,1,0:T(8,128)(2,1)}, u32[]{:S(2)}, u32[]{:S(2)}) collective-permute-start(bf16[1,2,128,1152]{3,2,1,0:T(8,128)(2,1)} %fusion.20), channel_id=1, source_target_pairs={{0,16},{8,24},{16,0},{24,8},{1,17},{9,25},{17,1},{25,9},{2,18},{10... | collective-permute-start | bytes 1769480 | tf_op jit(solution)/shard_map/ppermute | solution.py:100
  295.8 69.3 %collective-permute-start.42 = (bf16[2,288,576]{2,1,0:T(8,128)(2,1)}, bf16[2,288,576]{2,1,0:T(8,128)(2,1)}, u32[]{:S(2)}, u32[]{:S(2)}) collective-permute-start(bf16[2,288,576]{2,1,0:T(8,128)(2,1)} %broadcast_select_fusion.3), channel_id=1, source_target_pairs={{0,4},{1,5},{2,6},{3,7},{4,0},{5,1},{6,2},{7,3},{8,12},{9,13},{10,... | collective-permute-start | bytes 1990664 | tf_op jit(solution)/shard_map/ppermute | solution.py:510
  309.4 43.7 %collective-permute-start.39 = (bf16[2,1,2,144,288]{4,3,2,1,0:T(8,128)(2,1)}, bf16[2,1,2,144,288]{4,3,2,1,0:T(8,128)(2,1)}, u32[]{:S(2)}, u32[]{:S(2)}) collective-permute-start(bf16[2,1,2,144,288]{4,3,2,1,0:T(8,128)(2,1)} %broadcast_select_fusion.10), channel_id=1, source_target_pairs={{0,2},{1,3},{2,0},{3,1},{4,6},{5,7},{6,4},{7,5},{8,10},{9,11},{10,... | collective-permute-start | bytes 995336 | tf_op jit(solution)/shard_map/ppermute | solution.py:510
  312.0 24.4 %collective-permute-start.36 = (bf16[3,1,144,1152]{3,2,1,0:T(8,128)(2,1)}, bf16[3,1,144,1152]{3,2,1,0:T(8,128)(2,1)}, u32[]{:S(2)}, u32[]{:S(2)}) collective-permute-start(bf16[3,1,144,1152]{3,2,1,0:T(8,128)(2,1)} %broadcast_select_fusion.2), channel_id=1, source_target_pairs={{0,1},{1,0},{2,3},{3,2},{4,5},{5,4},{6,7},{7,6},{8,9},{9,8},{10,11... | collective-permute-start | bytes 2985992 | tf_op jit(solution)/shard_map/ppermute | solution.py:510
  356.6 21.8 %collective-permute-start.41 = (bf16[3,1,144,576]{3,2,1,0:T(8,128)(2,1)S(1)}, bf16[3,1,144,576]{3,2,1,0:T(8,128)(2,1)S(1)}, u32[]{:S(2)}, u32[]{:S(2)}) collective-permute-start(bf16[3,1,144,576]{3,2,1,0:T(8,128)(2,1)S(1)} %broadcast_select_fusion.9), channel_id=1, source_target_pairs={{0,2},{1,3},{2,0},{3,1},{4,6},{5,7},{6,4},{7,5},{8,10},{9,11},{10,... | collective-permute-start | bytes 1493000 | tf_op jit(solution)/shard_map/ppermute | solution.py:510
  356.6 16.9 %collective-permute-start.45 = (bf16[128,1152]{1,0:T(8,128)(2,1)S(1)}, bf16[128,1152]{1,0:T(8,128)(2,1)S(1)}, u32[]{:S(2)}, u32[]{:S(2)}) collective-permute-start(bf16[128,1152]{1,0:T(8,128)(2,1)S(1)} %get-tuple-element.305), channel_id=1, source_target_pairs={{1,0},{17,1},{9,2},{25,3},{0,4},{16,5},{8,6},{24,7},{5,8},{21,9},{... | collective-permute-start | bytes 884744 | tf_op jit(solution)/shard_map/ppermute | solution.py:670
  362.7 15.1 %collective-permute-start.44 = (bf16[128,1152]{1,0:T(8,128)(2,1)S(1)}, bf16[128,1152]{1,0:T(8,128)(2,1)S(1)}, u32[]{:S(2)}, u32[]{:S(2)}) collective-permute-start(bf16[128,1152]{1,0:T(8,128)(2,1)S(1)} %get-tuple-element.306), channel_id=1, source_target_pairs={{0,0},{16,1},{8,2},{24,3},{1,4},{17,5},{9,6},{25,7},{4,8},{20,9},{... | collective-permute-start | bytes 884744 | tf_op jit(solution)/shard_map/ppermute | solution.py:670
  383.5 16.9 %collective-permute-start.54 = (bf16[1,1,1,144,288]{4,3,2,1,0:T(8,128)(2,1)}, bf16[1,1,1,144,288]{4,3,2,1,0:T(8,128)(2,1)}, u32[]{:S(2)}, u32[]{:S(2)}) collective-permute-start(bf16[1,1,1,144,288]{4,3,2,1,0:T(8,128)(2,1)} %broadcast_select_fusion.13), channel_id=1, source_target_pairs={{0,4},{1,5},{2,6},{3,7},{4,0},{5,1},{6,2},{7,3},{8,12},{9,13},{10,... | collective-permute-start | bytes 248840 | tf_op jit(solution)/shard_map/ppermute | solution.py:510
  385.4 16.8 %collective-permute-start.48 = (f32[32,864]{1,0:T(8,128)S(1)}, f32[32,864]{1,0:T(8,128)S(1)}, u32[]{:S(2)}, u32[]{:S(2)}) collective-permute-start(f32[32,864]{1,0:T(8,128)S(1)} %constant_dynamic-slice_fusion.3), channel_id=1, source_target_pairs={{0,0},{1,1},{2,16},{3,17},{4,8},{5,9},{6,24},{7,25},{8,18},{9,19},... | collective-permute-start | bytes 331784 | tf_op jit(solution)/shard_map/ppermute | solution.py:777
  410.3 37.6 %collective-permute-start.55 = (bf16[2,288,576]{2,1,0:T(8,128)(2,1)}, bf16[2,288,576]{2,1,0:T(8,128)(2,1)}, u32[]{:S(2)}, u32[]{:S(2)}) collective-permute-start(bf16[2,288,576]{2,1,0:T(8,128)(2,1)} %collective-permute-done.49), channel_id=1, source_target_pairs={{0,0},{1,1},{2,2},{3,3},{4,4},{5,5},{6,6},{7,7},{8,12},{9,13},{10,... | collective-permute-start | bytes 1990664 | tf_op jit(solution)/shard_map/ppermute | solution.py:709
  424.3 21.6 %collective-permute-start.53 = (bf16[144,288]{0,1:T(8,128)(2,1)}, bf16[144,288]{0,1:T(8,128)(2,1)}, u32[]{:S(2)}, u32[]{:S(2)}) collective-permute-start(bf16[144,288]{0,1:T(8,128)(2,1)} %bitcast.105), channel_id=1, source_target_pairs={{0,2},{1,5},{2,18},{3,21},{4,10},{5,13},{6,26},{7,29},{8,16},{9,19... | collective-permute-start | bytes 248840 | tf_op jit(solution)/shard_map/ppermute | solution.py:754
  426.2 19.7 %collective-permute-start.51 = (bf16[144,288]{0,1:T(8,128)(2,1)}, bf16[144,288]{0,1:T(8,128)(2,1)}, u32[]{:S(2)}, u32[]{:S(2)}) collective-permute-start(bf16[144,288]{0,1:T(8,128)(2,1)} %bitcast.103), channel_id=1, source_target_pairs={{0,0},{1,3},{2,16},{3,19},{4,8},{5,11},{6,24},{7,27},{8,22},{9,17}... | collective-permute-start | bytes 248840 | tf_op jit(solution)/shard_map/ppermute | solution.py:754
  (105 other events, 916.0 us)
